TPU v7x, 32 devices: a whole 2x2x4 slice. The times are simulated.
32 devices in a mesh: groups: 2 (over y), tensor: 4 (over z), dp: 2 (over x), seq: 2 (over core).
Axes of the slice: x: 2, y: 2, z: 4, core: 2. Of those that a mesh axis runs over, the one named last changes fastest.
Arguments:
- tokens: bfloat16 [8, 512, 4096], P(('groups', 'dp', 'seq'), 'tensor'), parts along dimension 0, may hold values from -6 to 6
- grad_out: bfloat16 [8, 512, 4096], P(('groups', 'dp', 'seq'), 'tensor'), parts along dimension 0, may hold values from -6 to 6
- up_blocks: bfloat16 [4, 2, 256, 256], P('tensor'), may hold values from -0.375 to 0.375
- down_blocks: bfloat16 [4, 2, 256, 256], P('tensor'), may hold values from -0.375 to 0.375
- pairs: int32 [4, 2, 2], replicated, may hold values from 0 to 15, as said below
- live: int32 [4], replicated, may hold values from 1 to 2, as said below
- left_factor: bfloat16 [4096, 16], replicated, may hold values from -0.09375 to 0.09375
- right_factor: bfloat16 [16, 4096], P(None, 'tensor'), may hold values from -1.5 to 1.5
Outputs:
- grad_tokens: bfloat16 [8, 512, 4096], P(('groups', 'dp', 'seq'), 'tensor'), parts along dimension 0
- grad_up: float32 [8, 2, 256, 256], P(('groups', 'tensor'), None, ('dp', 'seq')), parts along dimension 0
- grad_down: float32 [8, 2, 256, 256], P(('groups', 'tensor'), None, ('dp', 'seq')), parts along dimension 0
- grad_left: float32 [8192, 16], P(('groups', 'tensor'), ('dp', 'seq')), parts along dimension 0
- grad_right: float32 [32, 4096], P(('groups', 'dp', 'seq'), 'tensor'), parts along dimension 0
There are 2 independent parts, one for each index of `groups`. A program takes and returns all parts, laid end to end along the dimension named above; an argument that names none is the same for every part. Nothing has to cross between parts.
Inputs may be any that keep to these rules, and one draw needn't show every extreme that they name: pairs[p, s, 0] is a feature row block in 0 .. 15 and pairs[p, s, 1] a column block within the panel in 0 .. 3. Each panel has 1 or 2 live slots; some panel has all 2 live.
All inputs are finite; a program needn't handle non-finite values.
Results may differ from a plain program's by a relative error of at most 0.006.
Values may be sent and summed in bfloat16 or wider, within the bound.
No kernel may reach another device: no remote copies, remote signals or barrier semaphores. Data moves between devices by JAX's collectives and lax.ppermute only.
A program may use at most 128 MiB of HBM per device.

v0:
```python
import jax
import jax.numpy as jnp
from jax import lax
from jax.sharding import PartitionSpec as P


def swish(value):
    return value * jax.nn.sigmoid(value)


def swish_slope(value):
    sig = jax.nn.sigmoid(value)
    return sig * (1.0 + value * (1.0 - sig))


def pick_columns(local, rows_flat, panels, blk):
    tok_rows, width = local.shape
    blocks = local.reshape(tok_rows, width // blk, blk)
    taken = jnp.take(blocks, rows_flat, axis=1)
    return taken.reshape(tok_rows, panels, rows_flat.shape[0] // panels * blk)


def contract(left, right, left_dim, right_dim):
    return lax.dot_general(
        left, right, (((left_dim,), (right_dim,)), ((), ())), preferred_element_type=jnp.float32
    )


def combine_slots(base, terms, same):
    slots = terms.shape[1]
    outputs = []
    for target in range(slots):
        total = base[:, target] if base is not None else jnp.zeros(terms[:, 0].shape, jnp.float32)
        for source in range(slots):
            total = total + jnp.where(same[target, source], terms[:, source], 0.0)
        outputs.append(total)
    return jnp.stack(outputs, axis=1)


def per_device(tokens, grad_out, up_blocks, down_blocks, pairs, live, left_factor, right_factor):
    panels = lax.axis_size("tensor")
    here = lax.axis_index("tensor")
    x_local = tokens[0]
    dy_local = grad_out[0]
    tok_dev, width = x_local.shape
    slots = up_blocks.shape[1]
    blk = up_blocks.shape[2]
    panel_width = right_factor.shape[1]
    rank_size = right_factor.shape[0]
    ncols = panel_width // blk
    up_here = up_blocks[0]
    down_here = down_blocks[0]
    rows_flat = pairs[:, :, 0].reshape(-1)
    my_pairs = lax.dynamic_index_in_dim(pairs, here, 0, keepdims=False)
    my_live = lax.dynamic_index_in_dim(live, here, 0, keepdims=False)
    toks = tok_dev * panels
    my_cols = my_pairs[:, 1]
    slot_ids = jnp.arange(slots, dtype=jnp.int32)
    alive = slot_ids < my_live
    same = (my_cols[:, None] == my_cols[None, :]) & alive[None, :]
    earlier = slot_ids[None, :] < slot_ids[:, None]
    single = alive & jnp.logical_not(jnp.any(same & earlier, axis=1))
    right_taken = jnp.take(right_factor.reshape(rank_size, ncols, blk), my_cols, axis=1)
    right_single = jnp.where(single[None, :, None], right_taken, jnp.zeros_like(right_taken))
    sent_x = pick_columns(x_local, rows_flat, panels, blk)
    sent_dy = pick_columns(dy_local, rows_flat, panels, blk)
    got_x, got_dy = (
        lax.all_to_all(sent_x, "tensor", split_axis=1, concat_axis=0, tiled=True),
        lax.all_to_all(sent_dy, "tensor", split_axis=1, concat_axis=0, tiled=True),
    )
    cols_x = got_x.reshape(toks, slots, blk)
    factor_local = jnp.dot(x_local, left_factor, preferred_element_type=jnp.float32).astype(
        jnp.bfloat16
    )
    factor = lax.all_gather(factor_local, "tensor", axis=0, tiled=True)
    low = jnp.einsum("tr,rsh->tsh", factor, right_taken, preferred_element_type=jnp.float32)
    block_up = jnp.einsum("tsf,sfh->tsh", cols_x, up_here, preferred_element_type=jnp.float32)
    pre = combine_slots(low, block_up, same)
    act = pre.astype(jnp.bfloat16)
    cols_dy = got_dy.reshape(toks, slots, blk)
    block_down = jnp.einsum("tsf,shf->tsh", cols_dy, down_here, preferred_element_type=jnp.float32)
    dh = combine_slots(None, block_down, same)
    act_wide = act.astype(jnp.float32)
    dact = (dh * swish_slope(act_wide)).astype(jnp.bfloat16)
    hid = swish(act_wide).astype(jnp.bfloat16)
    dact_single = jnp.where(single[None, :, None], dact, jnp.zeros_like(dact))
    right_slots = jnp.einsum("tr,tsh->srh", factor, dact_single, preferred_element_type=jnp.float32)
    column_ids = jnp.arange(ncols, dtype=jnp.int32)
    right_blocks = jnp.zeros((rank_size, ncols, blk), jnp.float32)
    for slot in range(slots):
        placed = (my_cols[slot] == column_ids)[None, :, None]
        right_blocks = right_blocks + jnp.where(placed, right_slots[slot][:, None, :], 0.0)
    right_local = right_blocks.reshape(rank_size, panel_width)
    right_sum = lax.psum_scatter(right_local, ("dp", "seq"), scatter_dimension=0, tiled=True)
    g_local = lax.psum_scatter(
        jnp.einsum("tsh,rsh->tr", dact_single, right_single, preferred_element_type=jnp.float32),
        "tensor",
        scatter_dimension=0,
        tiled=True,
    )
    gfac = g_local.astype(jnp.bfloat16)
    gw_up = jnp.einsum("tsf,tsh->sfh", cols_x, dact, preferred_element_type=jnp.float32)
    gw_down = jnp.einsum("tsh,tsf->shf", hid, cols_dy, preferred_element_type=jnp.float32)
    gw_up = jnp.where(alive[:, None, None], gw_up, 0.0)
    gw_down = jnp.where(alive[:, None, None], gw_down, 0.0)
    parts = jnp.einsum("tsh,sfh->tsf", dact, up_here, preferred_element_type=jnp.float32).astype(
        jnp.bfloat16
    )
    parts = jnp.where(alive[None, :, None], parts, jnp.zeros_like(parts))
    up_sum = lax.psum_scatter(gw_up, ("dp", "seq"), scatter_dimension=1, tiled=True)
    down_sum = lax.psum_scatter(gw_down, ("dp", "seq"), scatter_dimension=1, tiled=True)
    back = lax.all_to_all(parts, "tensor", split_axis=0, concat_axis=1, tiled=True)
    onehot = (rows_flat[:, None] == jnp.arange(width // blk, dtype=jnp.int32)[None, :]).astype(
        jnp.bfloat16
    )
    summed = jnp.einsum("tqc,qr->trc", back, onehot, preferred_element_type=jnp.float32)
    dx = (summed.reshape(tok_dev, width) + contract(gfac, left_factor, 1, 1)).astype(jnp.bfloat16)
    left_local = contract(x_local, gfac, 0, 0)
    left_part = lax.psum_scatter(left_local, "tensor", scatter_dimension=0, tiled=True)
    left_sum = lax.psum_scatter(left_part, ("dp", "seq"), scatter_dimension=1, tiled=True)
    return (dx[None], up_sum[None], down_sum[None], left_sum, right_sum)


def solution(mesh):
    return jax.shard_map(
        per_device,
        mesh=mesh,
        in_specs=(
            P(("groups", "dp", "seq"), "tensor", None),
            P(("groups", "dp", "seq"), "tensor", None),
            P("tensor", None, None, None),
            P("tensor", None, None, None),
            P(),
            P(),
            P(),
            P(None, "tensor"),
        ),
        out_specs=(
            P(("groups", "dp", "seq"), "tensor", None),
            P(("groups", "tensor"), None, ("dp", "seq"), None),
            P(("groups", "tensor"), None, ("dp", "seq"), None),
            P(("groups", "tensor"), ("dp", "seq")),
            P(("groups", "dp", "seq"), "tensor"),
        ),
        check_vma=False,
    )
```

profile of v0, /device:TPU:0, one launch (start us, length us, event | category | flops | bytes accessed | tf_op | source)
XLA Modules:
  0.0 197.5 jit_solution(7725351991863837988)
XLA Ops:
  8.1 1.7 copy.58
  11.1 1.3 copy.65
  13.0 1.8 gather_fusion.2
  16.0 6.3 %all-to-all-start.1 = ((bf16[128,4,512]{0,2,1:T(8,128)(2,1)}), bf16[128,4,512]{0,2,1:T(8,128)(2,1)S(1)}, u32[]{:S(2)}, u32[]{:S(2)}) async-start(bf16[128,4,512]{0,2,1:T(8,128)(2,1)} %bitcast.18), calls=%async_computation.1 | async-start | bytes 1048576 | tf_op jit(solution)/shard_map/all_to_all | solution.py:68
  27.2 14.9 %all_gather.3 = bf16[512,16]{0,1:T(8,128)(2,1)S(1)} all-gather(bf16[128,16]{0,1:T(8,128)(2,1)S(1)} %convolution_convert_fusion.1), channel_id=1, replica_groups=mesh['groups'=2,'tensor'=4,'dp'=2,'seq'=2] {'tensor'}, dimensions={0}, use_global_device_ids=true | all-gather | bytes 20480 | tf_op jit(solution)/shard_map/all_gather | solution.py:75
  43.0 4.2 %all-to-all-start = ((bf16[128,4,512]{0,2,1:T(8,128)(2,1)}), bf16[128,4,512]{0,2,1:T(8,128)(2,1)}, u32[]{:S(2)}, u32[]{:S(2)}) async-start(bf16[128,4,512]{0,2,1:T(8,128)(2,1)} %bitcast.5), calls=%async_computation | async-start | bytes 1048576 | tf_op jit(solution)/shard_map/all_to_all | solution.py:69
  50.3 9.0 %all-to-all-done = bf16[128,4,512]{0,2,1:T(8,128)(2,1)} async-done(((bf16[128,4,512]{0,2,1:T(8,128)(2,1)}), bf16[128,4,512]{0,2,1:T(8,128)(2,1)}, u32[]{:S(2)}, u32[]{:S(2)}) %all-to-all-start) | async-done | bytes 524320 | tf_op jit(solution)/shard_map/all_to_all | solution.py:69
  59.2 2.0 %copy.61 = bf16[4,128,1,512]{3,1,0,2:T(8,128)(2,1)} copy(bf16[4,128,1,512]{1,3,0,2:T(8,128)(2,1)} %bitcast.7) | data formatting | bytes 1048576 | tf_op jit(solution)/shard_map/all_to_all | solution.py:69
  64.1 2.6 %select_add_fusion.1 = (f32[512,1,256]{2,0,1:T(8,128)S(1)}, f32[512,1,256]{2,0,1:T(8,128)S(1)}) fusion(f32[512,2,256]{2,0,1:T(8,128)S(1)} %convolution_bitcast_fusion.2, pred[]{:T(512)} %bitcast.10, pred[]{:T(512)} %bitcast.2, pred[]{:T(512)} %bitcast.12, pred[]{:T(512)} %bitcast.11), kind=kLoop, calls=%fused_computation.42 | loop fusion | flops 786432 | bytes 2097156 | tf_op jit(solution)/shard_map/add | solution.py:35
  66.7 2.6 %fusion.18 = (bf16[512,1,256]{2,0,1:T(8,128)(2,1)S(1)}, bf16[512,1,256]{2,0,1:T(8,128)(2,1)S(1)}) fusion(f32[512,2,256]{2,0,1:T(8,128)S(1)} %fusion.25, f32[512,2,256]{2,0,1:T(8,128)S(1)} %convolution_bitcast_fusion.1, pred[]{:T(512)} %bitcast.10, pred[]{:T(512)} %bitcast.2, pred[]{:T(512)} %bitcast.12, pred[]{:T(512)} %bitcast.11), kind=kLoop, calls=%fused_computation.35 | loop fusion | flops 1310720 | bytes 2621444 | tf_op jit(solution)/shard_map/convert
  73.7 15.6 %reduce-scatter.5.cloned.1.call-done = f32[128,16]{0,1:T(8,128)} async-done(((f32[512,16]{0,1:T(8,128)}), f32[128,16]{0,1:T(8,128)}) %reduce-scatter.5.cloned.1.call-update) | async-done | bytes 8208 | tf_op jit(solution)/shard_map/reduce_scatter | solution.py:95
  89.2 1.7 convolution_bitcast_fusion
  92.0 1.3 select_add_fusion.2
  93.3 16.0 %reduce-scatter.11.cloned.1.call-done = f32[1024,16]{0,1:T(8,128)} async-done(((f32[4096,16]{0,1:T(8,128)}), f32[1024,16]{0,1:T(8,128)}) %reduce-scatter.11.cloned.1.call-update) | async-done | bytes 65552 | tf_op jit(solution)/shard_map/reduce_scatter | solution.py:119
  109.5 2.0 %convolution_select_fusion = f32[2,256,256]{2,1,0:T(8,128)} fusion(bf16[512,2,256]{2,1,0:T(2,128)(2,1)S(1)} %reshape.79, bf16[512,1,256]{2,0,1:T(8,128)(2,1)S(1)} %copy-done.5, bf16[512,1,256]{2,0,1:T(8,128)(2,1)S(1)} %copy-done.3, pred[2]{0:T(512)(128)(4,1)} %copy-done.12), kind=kOutput, calls=%fused_computation.13 | convolution fusion | flops 136183808 | bytes 1572866 | tf_op jit(solution)/shard_map/tsh,tsf->shf/dot_general | solution.py:103
  111.8 1.3 copy.69
  113.2 3.5 %all-to-all-start.2 = ((bf16[512,2,256]{2,1,0:T(2,128)(2,1)}), bf16[512,2,256]{2,1,0:T(2,128)(2,1)S(1)}, u32[]{:S(2)}, u32[]{:S(2)}) async-start(bf16[512,2,256]{2,1,0:T(2,128)(2,1)} %copy.69), calls=%async_computation.2 | async-start | bytes 1048576 | tf_op jit(solution)/shard_map/all_to_all | solution.py:112
  119.1 22.6 %all-reduce.5.cloned.1.call-done = (f32[1024,16]{0,1:T(8,128)}, f32[16,1024]{1,0:T(8,128)}) async-done(((f32[1024,16]{0,1:T(8,128)}, f32[16,1024]{1,0:T(8,128)}), (f32[1024,16]{0,1:T(8,128)}, f32[16,1024]{1,0:T(8,128)})) %all-reduce.5.cloned.1.call-update) | async-done | bytes 131088
  141.6 1.4 constant_dynamic-slice_fusion
  143.0 1.4 constant_dynamic-slice_fusion.1
  145.5 1.6 copy.78
  147.2 1.4 fusion.1
  148.6 17.8 %reduce-scatter.9.cloned.1.call-done = f32[2,64,256]{2,1,0:T(8,128)} async-done(((f32[2,256,256]{2,1,0:T(8,128)}), f32[2,64,256]{2,1,0:T(8,128)}) %reduce-scatter.9.cloned.1.call-update) | async-done | bytes 131088 | tf_op jit(solution)/shard_map/reduce_scatter | solution.py:111
  166.4 24.6 %reduce-scatter.7.cloned.1.call-done = f32[2,64,256]{2,1,0:T(8,128)} async-done(((f32[2,256,256]{2,1,0:T(8,128)}), f32[2,64,256]{2,1,0:T(8,128)}) %reduce-scatter.7.cloned.1.call-update) | async-done | bytes 131088 | tf_op jit(solution)/shard_map/reduce_scatter | solution.py:110
  (105 shorter events, 24.1 us)
Async XLA Ops:
  7.2 55.3 %copy-start = (bf16[1,2,256,256]{3,2,1,0:T(8,128)(2,1)S(1)}, bf16[1,2,256,256]{3,2,1,0:T(8,128)(2,1)}, u32[]{:S(2)}) copy-start(bf16[1,2,256,256]{3,2,1,0:T(8,128)(2,1)} %param.12) | copy-start | bytes 786436
  8.1 2.3 %copy-start.14 = (s32[8]{0:T(128)}, s32[8]{0:T(128)S(1)}, u32[]{:S(2)}) copy-start(s32[8]{0:T(128)S(1)} %eq.50) | copy-start | bytes 100
  14.8 7.6 %copy-start.11 = (s32[4,2,2]{0,2,1:T(2,128)S(1)}, s32[4,2,2]{0,2,1:T(2,128)}, u32[]{:S(2)}) copy-start(s32[4,2,2]{0,2,1:T(2,128)} %param.14) | copy-start | bytes 196
  14.8 7.8 %copy-start.18 = (s32[4]{0:T(128)S(1)}, s32[4]{0:T(128)}, u32[]{:S(2)}) copy-start(s32[4]{0:T(128)} %param.15) | copy-start | bytes 52
  15.0 8.2 %copy-start.10 = (bf16[16,1024]{1,0:T(8,128)(2,1)S(1)}, bf16[16,1024]{1,0:T(8,128)(2,1)}, u32[]{:S(2)}) copy-start(bf16[16,1024]{1,0:T(8,128)(2,1)} %param.17) | copy-start | bytes 98308
  15.0 11.8 %copy-start.6 = (bf16[4096,16]{0,1:T(8,128)(2,1)S(1)}, bf16[4096,16]{0,1:T(8,128)(2,1)}, u32[]{:S(2)}) copy-start(bf16[4096,16]{0,1:T(8,128)(2,1)} %param.16) | copy-start | bytes 393220
  16.0 27.0 %all-to-all-start.1 = ((bf16[128,4,512]{0,2,1:T(8,128)(2,1)}), bf16[128,4,512]{0,2,1:T(8,128)(2,1)S(1)}, u32[]{:S(2)}, u32[]{:S(2)}) async-start(bf16[128,4,512]{0,2,1:T(8,128)(2,1)} %bitcast.18), calls=%async_computation.1 | async-start | bytes 1048576 | tf_op jit(solution)/shard_map/all_to_all | solution.py:68
  26.8 22.8 %copy-start.7 = (bf16[2,16,256]{2,1,0:T(8,128)(2,1)}, bf16[2,16,256]{2,1,0:T(8,128)(2,1)S(1)}, u32[]{:S(2)}) copy-start(bf16[2,16,256]{2,1,0:T(8,128)(2,1)S(1)} %gather_fusion) | copy-start | bytes 49156
  42.8 5.3 %copy-start.12 = (pred[2]{0:T(512)(128)(4,1)}, pred[2]{0:T(512)(128)(4,1)S(1)}, u32[]{:S(2)}) copy-start(pred[2]{0:T(512)(128)(4,1)S(1)} %iota_compare_fusion.3) | copy-start | bytes 10
  43.0 6.6 %copy-start.16 = (pred[2]{0:T(512)(128)(4,1)}, pred[2]{0:T(512)(128)(4,1)S(1)}, u32[]{:S(2)}) copy-start(pred[2]{0:T(512)(128)(4,1)S(1)} %and_reduce_fusion.1) | copy-start | bytes 10
  43.0 16.2 %all-to-all-start = ((bf16[128,4,512]{0,2,1:T(8,128)(2,1)}), bf16[128,4,512]{0,2,1:T(8,128)(2,1)}, u32[]{:S(2)}, u32[]{:S(2)}) async-start(bf16[128,4,512]{0,2,1:T(8,128)(2,1)} %bitcast.5), calls=%async_computation | async-start | bytes 1048576 | tf_op jit(solution)/shard_map/all_to_all | solution.py:69
  47.2 42.1 %reduce-scatter.5.cloned.1.call-start = ((), (), s32[]{:S(2)}) async-start(), calls=%async_computation.7 | async-start | bytes 40960 | tf_op jit(solution)/shard_map/reduce_scatter | solution.py:95
  66.7 3.4 %copy-start.8 = (bf16[2,16,256]{2,1,0:T(8,128)(2,1)S(1)}, bf16[2,16,256]{2,1,0:T(8,128)(2,1)}, u32[]{:S(2)}) copy-start(bf16[2,16,256]{2,1,0:T(8,128)(2,1)} %copy-done.7) | copy-start | bytes 49156
  66.7 3.4 %copy-start.17 = (pred[2]{0:T(512)(128)(4,1)S(1)}, pred[2]{0:T(512)(128)(4,1)}, u32[]{:S(2)}) copy-start(pred[2]{0:T(512)(128)(4,1)} %copy-done.16) | copy-start | bytes 10
  66.7 3.4 %copy-start.20 = (pred[2]{0:T(512)(128)(4,1)S(1)}, pred[2]{0:T(512)(128)(4,1)}, u32[]{:S(2)}) copy-start(pred[2]{0:T(512)(128)(4,1)} %not_and_fusion) | copy-start | bytes 10
  71.1 38.4 %copy-start.3 = (bf16[512,1,256]{2,0,1:T(8,128)(2,1)S(1)}, bf16[512,1,256]{2,0,1:T(8,128)(2,1)}, u32[]{:S(2)}) copy-start(bf16[512,1,256]{2,0,1:T(8,128)(2,1)} %copy-done.2) | copy-start | bytes 786436
  71.1 38.4 %copy-start.5 = (bf16[512,1,256]{2,0,1:T(8,128)(2,1)S(1)}, bf16[512,1,256]{2,0,1:T(8,128)(2,1)}, u32[]{:S(2)}) copy-start(bf16[512,1,256]{2,0,1:T(8,128)(2,1)} %copy-done.4) | copy-start | bytes 786436
  71.1 38.3 %reduce-scatter.11.cloned.1.call-start = ((), (), s32[]{:S(2)}) async-start(), calls=%async_computation.10 | async-start | bytes 327680 | tf_op jit(solution)/shard_map/reduce_scatter | solution.py:119
  90.9 50.7 %all-reduce.5.cloned.1.call-start = ((), (), s32[]{:S(2)}) async-start(), calls=%async_computation.11 | async-start | bytes 262144
  109.4 57.0 %reduce-scatter.9.cloned.1.call-start = ((), (), s32[]{:S(2)}) async-start(), calls=%async_computation.9 | async-start | bytes 655360 | tf_op jit(solution)/shard_map/reduce_scatter | solution.py:111
  111.8 6.0 %copy-start.19 = (u32[32]{0:T(128)S(1)}, u32[32]{0:T(128)}, u32[]{:S(2)}) copy-start(u32[32]{0:T(128)} %constant.54) | copy-start | bytes 388
  113.2 31.2 %all-to-all-start.2 = ((bf16[512,2,256]{2,1,0:T(2,128)(2,1)}), bf16[512,2,256]{2,1,0:T(2,128)(2,1)S(1)}, u32[]{:S(2)}, u32[]{:S(2)}) async-start(bf16[512,2,256]{2,1,0:T(2,128)(2,1)} %copy.69), calls=%async_computation.2 | async-start | bytes 1048576 | tf_op jit(solution)/shard_map/all_to_all | solution.py:112
  116.7 28.3 %copy-start.15 = (s32[8]{0:T(128)S(1)}, s32[8]{0:T(128)}, u32[]{:S(2)}) copy-start(s32[8]{0:T(128)} %copy-done.14) | copy-start | bytes 100
  116.7 74.4 %reduce-scatter.7.cloned.1.call-start = ((), (), s32[]{:S(2)}) async-start(), calls=%async_computation.8 | async-start | bytes 655360 | tf_op jit(solution)/shard_map/reduce_scatter | solution.py:110
  (5 other events, 7.5 us)
Sparse Core Ops, SparseCore 0:
  71.2 17.9 reduce-scatter.4
  91.6 17.7 reduce-scatter.10
  111.8 29.8 all-reduce.4
  144.7 21.6 reduce-scatter.8
  169.3 21.6 reduce-scatter.6
where the time goes:
time: 198 us
  waiting for transfers between devices  106 us (54%)
  local copies, waits for them, and re-layouts  25.9 us (13%)
  blocking collectives  14.9 us (8%)
  between operations  14.9 us (8%)
  starting transfers between devices  14.1 us (7%)
  matrix products  11.2 us (6%)
  other arithmetic  10.9 us (6%)
    reduce_scatter x1, waiting for transfers between devices, per_device(): lax.psum_scatter(gw_up, ('dp', 'seq'), scatter_dimension=1, tiled=True)  24.6 us
    unnamed x6, waiting for transfers between devices  22.6 us
    reduce_scatter x1, waiting for transfers between devices, per_device(): lax.psum_scatter(gw_down, ('dp', 'seq'), scatter_dimension=1, tiled=True)  17.8 us
    reduce_scatter x1, waiting for transfers between devices, per_device(): lax.psum_scatter(left_local, 'tensor', scatter_dimension=0, tiled=True)  16 us
    reduce_scatter x1, waiting for transfers between devices, per_device(): lax.psum_scatter(jnp.einsum('tsh,rsh->tr', dact_single, right_single, pre...  15.6 us
    all_gather x1, blocking collectives, per_device(): factor = lax.all_gather(factor_local, 'tensor', axis=0, tiled=True)  14.9 us
    all_to_all x1, waiting for transfers between devices, per_device(): lax.all_to_all(sent_dy, 'tensor', split_axis=1, concat_axis=0, tiled=True)  8.96 us
    unnamed x50, local copies, waits for them, and re-layouts  7.81 us
  transfers between devices with their start and end apart: 8, of which 6 were waited for; matrix products, arithmetic and copies ran while one was open for 13% of the time, Pallas kernels for 0%

commit v1 on v0

v1 whole, which is shorter than its diff:
```python
import functools

import jax
import jax.numpy as jnp
from jax import lax
from jax.experimental import pallas as pl
from jax.experimental.pallas import tpu as pltpu
from jax.sharding import PartitionSpec as P

BF = jnp.bfloat16
F32 = jnp.float32
VM = pltpu.VMEM


def dot(a, b, ca, cb):
    return lax.dot_general(a, b, (((ca,), (cb,)), ((), ())), preferred_element_type=F32)


def split_seq(value, ndp, nseq, here):
    rows = value.shape[0] // (ndp * nseq)
    v = [[value[(d * nseq + s) * rows : (d * nseq + s + 1) * rows] for d in range(ndp)] for s in range(nseq)]
    first, second = jnp.stack(v[0]), jnp.stack(v[1])
    return jnp.where(here == 0, first, second), jnp.where(here == 0, second, first)


def panel_math(ndp, nseq, shift, pairs, live, xcol, dycol, factor, up, down, right, keep, give, parts, gacc, rgrad):
    npan = lax.axis_size("tensor")
    here = lax.axis_index("seq")
    panel = lax.rem(lax.axis_index("tensor") + shift, npan)
    slots = parts.shape[0]
    blk = parts.shape[2]
    cols = [pairs[panel, s, 1] for s in range(slots)]
    alive = [s < live[panel] for s in range(slots)]
    fac = factor[...]
    block_up, block_down, rights = [], [], []
    for s in range(slots):
        block_up.append(dot(xcol[s], up(s), 1, 0))
        block_down.append(dot(dycol[s], down(s), 1, 1))
        rights.append(right(cols[s]))
    rgrad[...] = jnp.zeros(rgrad.shape, F32)
    gsum = None
    for s in range(slots):
        pre = dot(fac, rights[s], 1, 0)
        dh = jnp.zeros(pre.shape, F32)
        single = alive[s]
        for t in range(slots):
            same = jnp.logical_and(cols[t] == cols[s], alive[t])
            pre = pre + jnp.where(same, block_up[t], 0.0)
            dh = dh + jnp.where(same, block_down[t], 0.0)
            if t < s:
                single = jnp.logical_and(single, jnp.logical_not(same))
        act = pre.astype(BF).astype(F32)
        sig = jax.nn.sigmoid(act)
        hid = (act * sig).astype(BF)
        dpre = (dh * (sig * (1.0 + act * (1.0 - sig)))).astype(BF)
        once = jnp.where(single, dpre, jnp.zeros_like(dpre))
        term = dot(once, rights[s], 1, 1)
        gsum = term if gsum is None else gsum + term
        where = pl.ds(pl.multiple_of(cols[s] * blk, blk), blk)
        rgrad[:, where] = rgrad[:, where] + dot(fac, once, 0, 0)
        part = dot(dpre, up(s), 1, 1)
        parts[s] = jnp.where(alive[s], part, 0.0).astype(BF)
        gup = jnp.where(alive[s], dot(xcol[s], dpre, 0, 0), 0.0)
        gdown = jnp.where(alive[s], dot(hid, dycol[s], 0, 0), 0.0)
        for a, grad in ((0, gup), (1, gdown)):
            mine, other = split_seq(grad, ndp, nseq, here)
            keep[:, a, s] = mine.astype(keep.dtype)
            give[:, a, s] = other.astype(give.dtype)
    gacc[...] = gsum


def own_kernel(ndp, nseq, pairs, live, x, dy, left, up, down, right, xg, dyg, factor, keep, give, parts, gacc, rgrad):
    npan, slots, _, blk = xg.shape
    me = lax.axis_index("tensor")
    for k in range(npan):
        panel = lax.rem(me + k, npan)
        for s in range(slots):
            where = pl.ds(pl.multiple_of(pairs[panel, s, 0] * blk, blk), blk)
            xg[k, s] = x[:, where]
            dyg[k, s] = dy[:, where]
    factor[...] = dot(x[...], left[...], 1, 0).astype(BF)

    def right_block(c):
        return right[:, pl.ds(pl.multiple_of(c * blk, blk), blk)]

    panel_math(ndp, nseq, 0, pairs, live, xg.at[0], dyg.at[0], factor, lambda s: up[0, s], lambda s: down[0, s],
               right_block, keep, give, parts, gacc, rgrad)


def far_kernel(ndp, nseq, shift, pairs, live, xg, dyg, factor, near, far, keep, give, parts, gacc, rgrad, mats, rblk):
    blk = mats.shape[2]
    rank = rblk.shape[1]
    here, grp = lax.axis_index("seq"), lax.axis_index("groups")
    nseq_ = mats.shape[1]
    for src, c in ((near, here), (far, 1 - here)):
        for i, g in ((0, grp), (1, 1 - grp)):
            mats[g, c] = src[i, :blk]
            rblk[g * nseq_ + c] = src[i, blk : blk + rank]
    panel_math(ndp, nseq, shift, pairs, live, xg, dyg, factor, lambda s: mats[0, s], lambda s: mats[1, s],
               lambda c: rblk[c], keep, give, parts, gacc, rgrad)


def left_kernel(ndp, nseq, x, gacc, rgrad, gfac, keep, give):
    npan = gacc.shape[0]
    chunk = x.shape[1] // npan
    me, here = lax.axis_index("tensor"), lax.axis_index("seq")
    total = gacc[0]
    for k in range(1, npan):
        total = total + gacc[k]
    gf = total.astype(BF)
    gfac[...] = gf
    for k in range(npan):
        panel = lax.rem(me + k, npan)
        lg = dot(gf, x[:, pl.ds(pl.multiple_of(panel * chunk, chunk), chunk)], 0, 0)
        for value, lo in ((lg, 0), (rgrad[k], chunk)):
            mine, other = split_seq(value, ndp, nseq, here)
            width = value.shape[1]
            rows = mine.shape[1]
            for d in range(ndp):
                keep[k, d * rows : (d + 1) * rows, lo : lo + width] = mine[d]
                give[k, d * rows : (d + 1) * rows, lo : lo + width] = other[d]


def dx_kernel(pairs, live, left, gfac, parts, dx, acc):
    npan, slots, _, blk = parts.shape
    me = lax.axis_index("tensor")
    acc[...] = dot(gfac[...], left[...], 1, 1)
    for k in range(npan):
        panel = lax.rem(me + k, npan)
        for s in range(slots):

            @pl.when(s < live[panel])
            def _():
                where = pl.ds(pl.multiple_of(pairs[panel, s, 0] * blk, blk), blk)
                acc[:, where] = acc[:, where] + parts[k, s].astype(F32)

    dx[...] = acc[...].astype(BF)


def specs(smem, vmem):
    return [pl.BlockSpec(memory_space=pltpu.SMEM)] * smem + [pl.BlockSpec(memory_space=VM)] * vmem


def call(kernel, smem, outs, scratch, args, mib, flops):
    return pl.pallas_call(
        kernel,
        out_shape=[jax.ShapeDtypeStruct(s, d) for s, d in outs],
        in_specs=specs(smem, len(args) - smem),
        out_specs=specs(0, len(outs)),
        scratch_shapes=[pltpu.VMEM(s, d) for s, d in scratch],
        compiler_params=pltpu.CompilerParams(vmem_limit_bytes=mib << 20),
        cost_estimate=pl.CostEstimate(flops=flops, bytes_accessed=mib << 18, transcendentals=0),
    )(*args)


def shift_over(axis, value, k):
    n = lax.axis_size(axis)
    return lax.ppermute(value, axis, [(i, (i + k) % n) for i in range(n)])


def pick(value, index, axis):
    return lax.dynamic_index_in_dim(value, index, axis, keepdims=False)


def over_cores_and_dp(keep, give):
    summed = keep.astype(F32) + shift_over("seq", give, 1).astype(F32)
    ndp = lax.axis_size("dp")
    d = lax.axis_index("dp")
    total = pick(summed, d, 0)
    for j in range(1, ndp):
        away = pick(summed, lax.rem(d + j, ndp), 0).astype(BF)
        total = total + shift_over("dp", away, j).astype(F32)
    return total


def per_device(tokens, grad_out, up_blocks, down_blocks, pairs, live, left_factor, right_factor):
    npan, ndp, nseq = lax.axis_size("tensor"), lax.axis_size("dp"), lax.axis_size("seq")
    core, grp = lax.axis_index("seq"), lax.axis_index("groups")
    x, dy = tokens[0], grad_out[0]
    toks, width = x.shape
    slots, blk = up_blocks.shape[1], up_blocks.shape[2]
    rank, pwidth = right_factor.shape
    ncols = pwidth // blk
    assert nseq == 2 and slots == 2 and lax.axis_size("groups") == 2 and ncols == 4
    rows = blk // (ndp * nseq)
    rk = rank // (ndp * nseq)

    quarter = jnp.concatenate(
        [
            jnp.where(grp == 0, pick(up_blocks[0], core, 0), pick(down_blocks[0], core, 0)),
            lax.dynamic_slice_in_dim(right_factor, (grp * 2 + core) * blk, blk, 1),
        ],
        axis=0,
    )
    order = [npan // 2] + [k for k in range(1, npan) if k != npan // 2]
    got = {}
    for k in order:
        got[k] = shift_over("tensor", quarter, npan - k)

    grad_shape = (ndp, 2, slots, rows, blk)
    term_outs = [
        (grad_shape, BF),
        (grad_shape, BF),
        ((slots, toks, blk), BF),
        ((toks, rank), F32),
        ((rank, pwidth), F32),
    ]
    flops = 10 * slots * toks * blk * blk
    xg, dyg, factor, keep0, give0, parts0, gacc0, rgrad0 = call(
        functools.partial(own_kernel, ndp, nseq), 2,
        [((npan, slots, toks, blk), BF), ((npan, slots, toks, blk), BF), ((toks, rank), BF)] + term_outs,
        [], (pairs, live, x, dy, left_factor, up_blocks, down_blocks, right_factor), 24, flops,
    )
    parts, gacc, rgrad = {0: parts0}, {0: gacc0}, {0: rgrad0}
    sums = {0: over_cores_and_dp(keep0, give0)}
    for k in order:
        near = jnp.stack([got[k], shift_over("groups", got[k], 1)])
        far = shift_over("seq", near, 1)
        keep, give, parts[k], gacc[k], rgrad[k] = call(
            functools.partial(far_kernel, ndp, nseq, k), 2, term_outs,
            [((2, nseq, blk, blk), BF), ((ncols, rank, blk), BF)],
            (pairs, live, xg[k], dyg[k], factor, near, far), 12, flops,
        )
        sums[k] = over_cores_and_dp(keep, give)

    gfac, lkeep, lgive = call(
        functools.partial(left_kernel, ndp, nseq), 0,
        [((toks, rank), BF)] + [((npan, ndp * rk, width // npan + pwidth), F32)] * 2, [],
        (x, jnp.stack([gacc[k] for k in range(npan)]), jnp.stack([rgrad[k] for k in range(npan)])), 24, 2 * rank * toks * width,
    )
    shape = (npan, ndp, rk, width // npan + pwidth)
    low = over_cores_and_dp(lkeep.reshape(shape).swapaxes(0, 1), lgive.reshape(shape).swapaxes(0, 1))
    (dx,) = call(
        dx_kernel, 2, [((toks, width), BF)], [((toks, width), F32)],
        (pairs, live, left_factor, gfac, jnp.stack([parts[k] for k in range(npan)])), 24, 2 * rank * toks * width,
    )
    total, low_total = sums[0], low[0]
    for k in order:
        total = total + shift_over("tensor", sums[k].astype(BF), k).astype(F32)
        low_total = low_total + shift_over("tensor", low[k].astype(BF), k).astype(F32)
    left = low_total[:, : width // npan].T
    return dx[None], total[0][None], total[1][None], left, low_total[:, width // npan :]


def solution(mesh):
    return jax.shard_map(
        per_device,
        mesh=mesh,
        in_specs=(
            P(("groups", "dp", "seq"), "tensor", None),
            P(("groups", "dp", "seq"), "tensor", None),
            P("tensor", None, None, None),
            P("tensor", None, None, None),
            P(),
            P(),
            P(),
            P(None, "tensor"),
        ),
        out_specs=(
            P(("groups", "dp", "seq"), "tensor", None),
            P(("groups", "tensor"), None, ("dp", "seq"), None),
            P(("groups", "tensor"), None, ("dp", "seq"), None),
            P(("groups", "tensor"), ("dp", "seq")),
            P(("groups", "dp", "seq"), "tensor"),
        ),
        check_vma=False,
    )
```

time: 198 us -> 78.9 us (0.40)
  waiting for transfers between devices: 106 us -> 23.8 us
  blocking collectives: 14.9 us -> 0 us
  between operations: 14.9 us -> 1.07 us
  local copies, waits for them, and re-layouts: 25.9 us -> 12.3 us
  matrix products: 11.2 us -> 0 us
  starting transfers between devices: 14.1 us -> 24 us
  Pallas kernels: 0 us -> 9.19 us
  other arithmetic: 10.9 us -> 8.19 us
    reduce_scatter x4 -> x0, waiting for transfers between devices: 74 us -> none  [the longest x1 24.6 us: per_device(): lax.psum_scatter(gw_up, ('dp', 'seq'), scatter_dimension=1, tiled=True)]
    ppermute x0 -> x25, starting transfers between devices: none -> 24 us  [shift_over(): return lax.ppermute(value, axis, [(i, (i + k) % n) for i in range(n)])]
    ppermute x0 -> x25, waiting for transfers between devices: none -> 23.8 us  [shift_over(): return lax.ppermute(value, axis, [(i, (i + k) % n) for i in range(n)])]
    unnamed x6 -> x0, waiting for transfers between devices: 22.6 us -> none
    all_gather x1 -> x0, blocking collectives: 14.9 us -> none  [per_device(): factor = lax.all_gather(factor_local, 'tensor', axis=0, tiled=True)]
    all_to_all x3 -> x0, starting transfers between devices: 13.9 us -> none  [the longest x1 6.32 us: per_device(): lax.all_to_all(sent_x, 'tensor', split_axis=1, concat_axis=0, tiled=True)]
    dot_general x12 -> x0, matrix products: 11.2 us -> none  [the longest x2 3.08 us: contract(): lax.dot_general(left, right, (((left_dim,), (right_dim,)), ((), ())), pre...]
    pallas_call x0 -> x6, Pallas kernels: none -> 9.19 us  [call(): pl.pallas_call(kernel, out_shape=[jax.ShapeDtypeStruct(s, d) for s, d in...]
  transfers between devices with their start and end apart: 8 -> 25, of which waited for: 6 -> 10; matrix products, arithmetic and copies ran while one was open for 13% -> 13% of each run, Pallas kernels for 0% -> 12%
where the time goes in v1:
time: 78.9 us; the launch traced here: 78.6 us
  starting transfers between devices  24 us (30%)
  waiting for transfers between devices  23.8 us (30%)
  local copies, waits for them, and re-layouts  12.3 us (16%)
  Pallas kernels  9.19 us (12%)
  other arithmetic  8.19 us (10%)
  between operations  1.07 us (1%)
    ppermute x25, starting transfers between devices, shift_over(): return lax.ppermute(value, axis, [(i, (i + k) % n) for i in range(n)])  24 us
    ppermute x25, waiting for transfers between devices, shift_over(): return lax.ppermute(value, axis, [(i, (i + k) % n) for i in range(n)])  23.8 us
    pallas_call x6, Pallas kernels, call(): pl.pallas_call(kernel, out_shape=[jax.ShapeDtypeStruct(s, d) for s, d in...  9.19 us
    unnamed x58, local copies, waits for them, and re-layouts  8.48 us
    another operation x3, other arithmetic, per_device(): near = jnp.stack([got[k], shift_over('groups', got[k], 1)])  3 us
    add x5, other arithmetic, over_cores_and_dp(): summed = keep.astype(F32) + shift_over('seq', give, 1).astype(F32)  2.3 us
  transfers between devices with their start and end apart: 25, of which 10 were waited for; matrix products, arithmetic and copies ran while one was open for 13% of the time, Pallas kernels for 12%

profile of v1, /device:TPU:0, one launch (start us, length us, event | category | flops | bytes accessed | tf_op | source)
XLA Modules:
  0.0 78.6 jit_solution(9615652295180322636)
XLA Ops:
  3.1 5.0 %collective-permute-start = (bf16[272,256]{1,0:T(8,128)(2,1)}, bf16[272,256]{1,0:T(8,128)(2,1)}, u32[]{:S(2)}, u32[]{:S(2)}) collective-permute-start(bf16[272,256]{1,0:T(8,128)(2,1)} %pad_maximum_fusion.6), channel_id=1, source_target_pairs={{0,12},{4,0},{8,4},{12,8},{1,13},{5,1},{9,5},{13,9},{2,14},{6,2},{... | collective-permute-start | bytes 417800 | tf_op jit(solution)/shard_map/ppermute | solution.py:158
  9.1 3.4 %collective-permute-done = bf16[272,256]{1,0:T(8,128)(2,1)} collective-permute-done((bf16[272,256]{1,0:T(8,128)(2,1)}, bf16[272,256]{1,0:T(8,128)(2,1)}, u32[]{:S(2)}, u32[]{:S(2)}) %collective-permute-start) | collective-permute-done | bytes 139296 | tf_op jit(solution)/shard_map/ppermute | solution.py:158
  12.5 1.5 %collective-permute-start.1 = (bf16[272,256]{1,0:T(8,128)(2,1)}, bf16[272,256]{1,0:T(8,128)(2,1)}, u32[]{:S(2)}, u32[]{:S(2)}) collective-permute-start(bf16[272,256]{1,0:T(8,128)(2,1)} %collective-permute-done), channel_id=1, source_target_pairs={{0,16},{16,0},{1,17},{17,1},{2,18},{18,2},{3,19},{19,3},{4,20},{20... | collective-permute-start | bytes 417800 | tf_op jit(solution)/shard_map/ppermute | solution.py:158
  14.1 6.2 %collective-permute-done.3 = bf16[272,256]{1,0:T(8,128)(2,1)} collective-permute-done((bf16[272,256]{1,0:T(8,128)(2,1)}, bf16[272,256]{1,0:T(8,128)(2,1)}, u32[]{:S(2)}, u32[]{:S(2)}) %collective-permute-start.3) | collective-permute-done | bytes 139296 | tf_op jit(solution)/shard_map/ppermute | solution.py:158
  20.3 1.5 %collective-permute-start.4 = (bf16[272,256]{1,0:T(8,128)(2,1)}, bf16[272,256]{1,0:T(8,128)(2,1)}, u32[]{:S(2)}, u32[]{:S(2)}) collective-permute-start(bf16[272,256]{1,0:T(8,128)(2,1)} %collective-permute-done.3), channel_id=1, source_target_pairs={{0,16},{16,0},{1,17},{17,1},{2,18},{18,2},{3,19},{19,3},{4,20},{20... | collective-permute-start | bytes 417800 | tf_op jit(solution)/shard_map/ppermute | solution.py:158
  22.6 1.4 %copy.42.left = bf16[4096,16]{1,0:T(8,128)(2,1)S(1)} copy(bf16[4096,16]{0,1:T(8,128)(2,1)} %param.14) | data formatting | bytes 262144 | tf_op args[6]
  24.7 1.2 %copy-done.1 = bf16[1,128,4096]{2,1,0:T(8,128)(2,1)S(1)} copy-done((bf16[1,128,4096]{2,1,0:T(8,128)(2,1)S(1)}, bf16[1,128,4096]{2,1,0:T(8,128)(2,1)}, u32[]{:S(2)}) %copy-start.1) | copy-done | bytes 1048600
  25.9 2.5 %shard_map.119 = (bf16[4,2,128,256]{3,2,1,0:T(8,128)(2,1)S(1)}, bf16[4,2,128,256]{3,2,1,0:T(8,128)(2,1)S(1)}, bf16[128,16]{1,0:T(8,128)(2,1)S(1)}, bf16[2,2,2,64...) custom-call(s32[4,2,2]{2,1,0:T(2,128)S(1)} %copy.41.pairs, ...), custom_call_target="tpu_custom_call" | custom-call | flops 167772160 | bytes 6291456 | tf_op jit(solution)/shard_map/pallas_call | solution.py:145
  33.7 3.1 %collective-permute-done.7 = bf16[272,256]{1,0:T(8,128)(2,1)S(1)} collective-permute-done((bf16[272,256]{1,0:T(8,128)(2,1)}, bf16[272,256]{1,0:T(8,128)(2,1)S(1)}, u32[]{:S(2)}, u32[]{:S(2)}) %collective-permute-start.7) | collective-permute-done | bytes 139296 | tf_op jit(solution)/shard_map/ppermute | solution.py:158
  37.8 1.4 %shard_map.120 = (bf16[2,2,2,64,256]{4,3,2,1,0:T(8,128)(2,1)S(1)}, bf16[2,2,2,64,256]{4,3,2,1,0:T(8,128)(2,1)S(1)}, bf16[2,128,256]{2,1,0:T(8,128)(2,1)S(1)}, f32[128,16]{1,0:T(8,128)S(1)}, f32[16,1024]{1,0:T(8,128)S(1)}) custom-call(s32[4,2,2]{2,1,0:T(2,128)S(1)} %copy.41.pairs, s32[4]{0:T(128)S(1)} %copy-done.19, ...), custom_call_target="tpu_custom_call" | custom-call | flops 167772160 | bytes 3145728 | tf_op jit(solution)/shard_map/pallas_call | solution.py:145
  39.9 1.4 %shard_map.121 = (bf16[2,2,2,64,256]{4,3,2,1,0:T(8,128)(2,1)S(1)}, bf16[2,2,2,64,256]{4,3,2,1,0:T(8,128)(2,1)S(1)}, bf16[2,128,256]{2,1,0:T(8,128)(2,1)S(1)}, f32[128,16]{1,0:T(8,128)S(1)}, f32[16,1024]{1,0:T(8,128)S(1)}) custom-call(s32[4,2,2]{2,1,0:T(2,128)S(1)} %copy.41.pairs, s32[4]{0:T(128)S(1)} %copy-done.19, ...), custom_call_target="tpu_custom_call" | custom-call | flops 167772160 | bytes 3145728 | tf_op jit(solution)/shard_map/pallas_call | solution.py:145
  42.0 1.4 %shard_map.122 = (bf16[2,2,2,64,256]{4,3,2,1,0:T(8,128)(2,1)S(1)}, bf16[2,2,2,64,256]{4,3,2,1,0:T(8,128)(2,1)S(1)}, bf16[2,128,256]{2,1,0:T(8,128)(2,1)S(1)}, f32[128,16]{1,0:T(8,128)S(1)}, f32[16,1024]{1,0:T(8,128)S(1)}) custom-call(s32[4,2,2]{2,1,0:T(2,128)S(1)} %copy.41.pairs, s32[4]{0:T(128)S(1)} %copy-done.19, ...), custom_call_target="tpu_custom_call" | custom-call | flops 167772160 | bytes 3145728 | tf_op jit(solution)/shard_map/pallas_call | solution.py:145
  47.5 1.5 %collective-permute-start.10 = (bf16[2,2,64,256]{3,2,1,0:T(8,128)(2,1)}, bf16[2,2,64,256]{3,2,1,0:T(8,128)(2,1)}, u32[]{:S(2)}, u32[]{:S(2)}) collective-permute-start(bf16[2,2,64,256]{3,2,1,0:T(8,128)(2,1)} %fusion.6), channel_id=1, source_target_pairs={{0,2},{2,0},{1,3},{3,1},{4,6},{6,4},{5,7},{7,5},{8,10},{10,8},{9,1... | collective-permute-start | bytes 393224 | tf_op jit(solution)/shard_map/ppermute | solution.py:158
  50.2 2.2 %shard_map.124 = bf16[128,4096]{1,0:T(8,128)(2,1)} custom-call(s32[4,2,2]{2,1,0:T(2,128)S(1)} %copy.41.pairs, s32[4]{0:T(128)S(1)} %copy-done.19, bf16[4096,16]{1,0:T(8,128)(2,1)S(1)} %copy.42.left, bf16[128,16]{1,0:T(8,128)(2,1)S(1)} %get-tuple-element.42.gfac, bf16[4,2,128,256]{3,2,1,0:T(8,128)(2,1)S(1)} %pad_maximum_fusion.parts), custom_call_target="tpu_custom_call" | custom-call | flops 16777216 | bytes 6291456 | tf_op jit(solution)/shard_map/pallas_call | solution.py:145
  52.5 1.1 %bitcast_add_fusion = f32[2,4,4,2048]{3,2,1,0:T(4,128)S(1)} fusion(f32[2,4,4,2048]{3,2,1,0:T(4,128)} %collective-permute-done.20, f32[4,2,4,2048]{3,2,1,0:T(4,128)S(1)} %reshape.30), kind=kLoop, calls=%fused_computation.10 | loop fusion | flops 65536 | bytes 786432 | tf_op jit(solution)/shard_map/add | solution.py:166
  54.3 1.6 %collective-permute-start.12 = (bf16[2,2,64,256]{3,2,1,0:T(8,128)(2,1)S(1)}, bf16[2,2,64,256]{3,2,1,0:T(8,128)(2,1)S(1)}, u32[]{:S(2)}, u32[]{:S(2)}) collective-permute-start(bf16[2,2,64,256]{3,2,1,0:T(8,128)(2,1)S(1)} %fusion.7), channel_id=1, source_target_pairs={{0,2},{2,0},{1,3},{3,1},{4,6},{6,4},{5,7},{7,5},{8,10},{10,8},{9,1... | collective-permute-start | bytes 393224 | tf_op jit(solution)/shard_map/ppermute | solution.py:158
  56.0 2.6 %collective-permute-done.21 = bf16[4,4,2048]{2,1,0:T(4,128)(2,1)S(1)} collective-permute-done((bf16[4,4,2048]{2,1,0:T(4,128)(2,1)S(1)}, bf16[4,4,2048]{2,1,0:T(4,128)(2,1)S(1)}, u32[]{:S(2)}, u32[]{:S(2)}) %collective-permute-start.21) | collective-permute-done | bytes 65568 | tf_op jit(solution)/shard_map/ppermute | solution.py:158
  58.7 2.1 %collective-permute-start.23 = (bf16[4,2048]{1,0:T(4,128)(2,1)S(1)}, bf16[4,2048]{1,0:T(4,128)(2,1)S(1)}, u32[]{:S(2)}, u32[]{:S(2)}) collective-permute-start(bf16[4,2048]{1,0:T(4,128)(2,1)S(1)} %get-tuple-element.69), channel_id=1, source_target_pairs={{0,4},{4,8},{8,12},{12,0},{1,5},{5,9},{9,13},{13,1},{2,6},{6,10},{... | collective-permute-start | bytes 49160 | tf_op jit(solution)/shard_map/ppermute | solution.py:158
  60.8 1.8 %collective-permute-start.24 = (bf16[4,2048]{1,0:T(4,128)(2,1)S(1)}, bf16[4,2048]{1,0:T(4,128)(2,1)S(1)}, u32[]{:S(2)}, u32[]{:S(2)}) collective-permute-start(bf16[4,2048]{1,0:T(4,128)(2,1)S(1)} %get-tuple-element.68), channel_id=1, source_target_pairs={{0,12},{4,0},{8,4},{12,8},{1,13},{5,1},{9,5},{13,9},{2,14},{6,2},{... | collective-permute-start | bytes 49160 | tf_op jit(solution)/shard_map/ppermute | solution.py:158
  64.3 1.1 %collective-permute-start.18 = (bf16[2,2,64,256]{3,2,1,0:T(8,128)(2,1)S(1)}, bf16[2,2,64,256]{3,2,1,0:T(8,128)(2,1)S(1)}, u32[]{:S(2)}, u32[]{:S(2)}) collective-permute-start(bf16[2,2,64,256]{3,2,1,0:T(8,128)(2,1)S(1)} %fusion.9), channel_id=1, source_target_pairs={{0,2},{2,0},{1,3},{3,1},{4,6},{6,4},{5,7},{7,5},{8,10},{10,8},{9,1... | collective-permute-start | bytes 393224 | tf_op jit(solution)/shard_map/ppermute | solution.py:158
  65.9 2.4 %collective-permute-done.15 = bf16[2,2,64,256]{3,2,1,0:T(8,128)(2,1)S(1)} collective-permute-done((bf16[2,2,64,256]{3,2,1,0:T(8,128)(2,1)S(1)}, bf16[2,2,64,256]{3,2,1,0:T(8,128)(2,1)S(1)}, u32[]{:S(2)}, u32[]{:S(2)}) %collective-permute-start.15) | collective-permute-done | bytes 131104 | tf_op jit(solution)/shard_map/ppermute | solution.py:158
  69.8 2.6 %collective-permute-start.19 = (bf16[2,2,64,256]{3,2,1,0:T(8,128)(2,1)S(1)}, bf16[2,2,64,256]{3,2,1,0:T(8,128)(2,1)S(1)}, u32[]{:S(2)}, u32[]{:S(2)}) collective-permute-start(bf16[2,2,64,256]{3,2,1,0:T(8,128)(2,1)S(1)} %fusion), channel_id=1, source_target_pairs={{0,12},{4,0},{8,4},{12,8},{1,13},{5,1},{9,5},{13,9},{2,14},{6,2},{... | collective-permute-start | bytes 393224 | tf_op jit(solution)/shard_map/ppermute | solution.py:158
  72.9 2.6 %collective-permute-done.13 = bf16[2,2,64,256]{3,2,1,0:T(8,128)(2,1)S(1)} collective-permute-done((bf16[2,2,64,256]{3,2,1,0:T(8,128)(2,1)S(1)}, bf16[2,2,64,256]{3,2,1,0:T(8,128)(2,1)S(1)}, u32[]{:S(2)}, u32[]{:S(2)}) %collective-permute-start.13) | collective-permute-done | bytes 131104 | tf_op jit(solution)/shard_map/ppermute | solution.py:158
  75.5 1.3 %collective-permute-done.19 = bf16[2,2,64,256]{3,2,1,0:T(8,128)(2,1)S(1)} collective-permute-done((bf16[2,2,64,256]{3,2,1,0:T(8,128)(2,1)S(1)}, bf16[2,2,64,256]{3,2,1,0:T(8,128)(2,1)S(1)}, u32[]{:S(2)}, u32[]{:S(2)}) %collective-permute-start.19) | collective-permute-done | bytes 131104 | tf_op jit(solution)/shard_map/ppermute | solution.py:158
  (122 shorter events, 24.7 us)
Async XLA Ops:
  3.1 9.5 %collective-permute-start = (bf16[272,256]{1,0:T(8,128)(2,1)}, bf16[272,256]{1,0:T(8,128)(2,1)}, u32[]{:S(2)}, u32[]{:S(2)}) collective-permute-start(bf16[272,256]{1,0:T(8,128)(2,1)} %pad_maximum_fusion.6), channel_id=1, source_target_pairs={{0,12},{4,0},{8,4},{12,8},{1,13},{5,1},{9,5},{13,9},{2,14},{6,2},{... | collective-permute-start | bytes 417800 | tf_op jit(solution)/shard_map/ppermute | solution.py:158
  8.1 12.1 %collective-permute-start.3 = (bf16[272,256]{1,0:T(8,128)(2,1)}, bf16[272,256]{1,0:T(8,128)(2,1)}, u32[]{:S(2)}, u32[]{:S(2)}) collective-permute-start(bf16[272,256]{1,0:T(8,128)(2,1)} %pad_maximum_fusion.6), channel_id=1, source_target_pairs={{0,8},{4,12},{8,0},{12,4},{1,9},{5,13},{9,1},{13,5},{2,10},{6,14},... | collective-permute-start | bytes 417800 | tf_op jit(solution)/shard_map/ppermute | solution.py:158
  8.1 22.3 %collective-permute-start.6 = (bf16[272,256]{1,0:T(8,128)(2,1)}, bf16[272,256]{1,0:T(8,128)(2,1)}, u32[]{:S(2)}, u32[]{:S(2)}) collective-permute-start(bf16[272,256]{1,0:T(8,128)(2,1)} %pad_maximum_fusion.6), channel_id=1, source_target_pairs={{0,4},{4,8},{8,12},{12,0},{1,5},{5,9},{9,13},{13,1},{2,6},{6,10},{... | collective-permute-start | bytes 417800 | tf_op jit(solution)/shard_map/ppermute | solution.py:158
  12.5 18.4 %collective-permute-start.1 = (bf16[272,256]{1,0:T(8,128)(2,1)}, bf16[272,256]{1,0:T(8,128)(2,1)}, u32[]{:S(2)}, u32[]{:S(2)}) collective-permute-start(bf16[272,256]{1,0:T(8,128)(2,1)} %collective-permute-done), channel_id=1, source_target_pairs={{0,16},{16,0},{1,17},{17,1},{2,18},{18,2},{3,19},{19,3},{4,20},{20... | collective-permute-start | bytes 417800 | tf_op jit(solution)/shard_map/ppermute | solution.py:158
  20.3 12.0 %collective-permute-start.4 = (bf16[272,256]{1,0:T(8,128)(2,1)}, bf16[272,256]{1,0:T(8,128)(2,1)}, u32[]{:S(2)}, u32[]{:S(2)}) collective-permute-start(bf16[272,256]{1,0:T(8,128)(2,1)} %collective-permute-done.3), channel_id=1, source_target_pairs={{0,16},{16,0},{1,17},{17,1},{2,18},{18,2},{3,19},{19,3},{4,20},{20... | collective-permute-start | bytes 417800 | tf_op jit(solution)/shard_map/ppermute | solution.py:158
  30.4 15.3 %collective-permute-start.9 = (bf16[2,2,2,64,256]{4,3,2,1,0:T(8,128)(2,1)}, bf16[2,2,2,64,256]{4,3,2,1,0:T(8,128)(2,1)}, u32[]{:S(2)}, u32[]{:S(2)}) collective-permute-start(bf16[2,2,2,64,256]{4,3,2,1,0:T(8,128)(2,1)} %get-tuple-element.48), channel_id=1, source_target_pairs={{0,1},{1,0},{2,3},{3,2},{4,5},{5,4},{6,7},{7,6},{8,9},{9,8},{10,11... | collective-permute-start | bytes 786440 | tf_op jit(solution)/shard_map/ppermute | solution.py:158
  30.4 6.3 %collective-permute-start.7 = (bf16[272,256]{1,0:T(8,128)(2,1)}, bf16[272,256]{1,0:T(8,128)(2,1)S(1)}, u32[]{:S(2)}, u32[]{:S(2)}) collective-permute-start(bf16[272,256]{1,0:T(8,128)(2,1)} %collective-permute-done.6), channel_id=1, source_target_pairs={{0,16},{16,0},{1,17},{17,1},{2,18},{18,2},{3,19},{19,3},{4,20},{20... | collective-permute-start | bytes 417800 | tf_op jit(solution)/shard_map/ppermute | solution.py:158
  32.0 5.9 %collective-permute-start.2 = (bf16[2,272,256]{2,1,0:T(8,128)(2,1)S(1)}, bf16[2,272,256]{2,1,0:T(8,128)(2,1)S(1)}, u32[]{:S(2)}, u32[]{:S(2)}) collective-permute-start(bf16[2,272,256]{2,1,0:T(8,128)(2,1)S(1)} %pad_maximum_fusion.1.near), channel_id=1, source_target_pairs={{0,1},{1,0},{2,3},{3,2},{4,5},{5,4},{6,7},{7,6},{8,9},{9,8},{10,11... | collective-permute-start | bytes 835592 | tf_op jit(solution)/shard_map/ppermute | solution.py:158
  33.3 6.6 %collective-permute-start.5 = (bf16[2,272,256]{2,1,0:T(8,128)(2,1)S(1)}, bf16[2,272,256]{2,1,0:T(8,128)(2,1)S(1)}, u32[]{:S(2)}, u32[]{:S(2)}) collective-permute-start(bf16[2,272,256]{2,1,0:T(8,128)(2,1)S(1)} %pad_maximum_fusion.2.near), channel_id=1, source_target_pairs={{0,1},{1,0},{2,3},{3,2},{4,5},{5,4},{6,7},{7,6},{8,9},{9,8},{10,11... | collective-permute-start | bytes 835592 | tf_op jit(solution)/shard_map/ppermute | solution.py:158
  45.3 7.2 %collective-permute-start.20 = (f32[2,4,4,2048]{3,2,1,0:T(4,128)}, f32[2,4,4,2048]{3,2,1,0:T(4,128)}, u32[]{:S(2)}, u32[]{:S(2)}) collective-permute-start(f32[2,4,4,2048]{3,2,1,0:T(4,128)} %bitcast.88), channel_id=1, source_target_pairs={{0,1},{1,0},{2,3},{3,2},{4,5},{5,4},{6,7},{7,6},{8,9},{9,8},{10,11... | collective-permute-start | bytes 786440 | tf_op jit(solution)/shard_map/ppermute | solution.py:158
  47.5 25.4 %collective-permute-start.10 = (bf16[2,2,64,256]{3,2,1,0:T(8,128)(2,1)}, bf16[2,2,64,256]{3,2,1,0:T(8,128)(2,1)}, u32[]{:S(2)}, u32[]{:S(2)}) collective-permute-start(bf16[2,2,64,256]{3,2,1,0:T(8,128)(2,1)} %fusion.6), channel_id=1, source_target_pairs={{0,2},{2,0},{1,3},{3,1},{4,6},{6,4},{5,7},{7,5},{8,10},{10,8},{9,1... | collective-permute-start | bytes 393224 | tf_op jit(solution)/shard_map/ppermute | solution.py:158
  49.1 5.0 %collective-permute-start.11 = (bf16[2,2,2,64,256]{4,3,2,1,0:T(8,128)(2,1)S(1)}, bf16[2,2,2,64,256]{4,3,2,1,0:T(8,128)(2,1)S(1)}, u32[]{:S(2)}, u32[]{:S(2)}) collective-permute-start(bf16[2,2,2,64,256]{4,3,2,1,0:T(8,128)(2,1)S(1)} %copy-done.25), channel_id=1, source_target_pairs={{0,1},{1,0},{2,3},{3,2},{4,5},{5,4},{6,7},{7,6},{8,9},{9,8},{10,11... | collective-permute-start | bytes 786440 | tf_op jit(solution)/shard_map/ppermute | solution.py:158
  49.2 6.6 %collective-permute-start.14 = (bf16[2,2,2,64,256]{4,3,2,1,0:T(8,128)(2,1)S(1)}, bf16[2,2,2,64,256]{4,3,2,1,0:T(8,128)(2,1)S(1)}, u32[]{:S(2)}, u32[]{:S(2)}) collective-permute-start(bf16[2,2,2,64,256]{4,3,2,1,0:T(8,128)(2,1)S(1)} %copy-done.21), channel_id=1, source_target_pairs={{0,1},{1,0},{2,3},{3,2},{4,5},{5,4},{6,7},{7,6},{8,9},{9,8},{10,11... | collective-permute-start | bytes 786440 | tf_op jit(solution)/shard_map/ppermute | solution.py:158
  49.7 6.2 %collective-permute-start.17 = (bf16[2,2,2,64,256]{4,3,2,1,0:T(8,128)(2,1)S(1)}, bf16[2,2,2,64,256]{4,3,2,1,0:T(8,128)(2,1)S(1)}, u32[]{:S(2)}, u32[]{:S(2)}) collective-permute-start(bf16[2,2,2,64,256]{4,3,2,1,0:T(8,128)(2,1)S(1)} %copy-done.23), channel_id=1, source_target_pairs={{0,1},{1,0},{2,3},{3,2},{4,5},{5,4},{6,7},{7,6},{8,9},{9,8},{10,11... | collective-permute-start | bytes 786440 | tf_op jit(solution)/shard_map/ppermute | solution.py:158
  53.6 5.0 %collective-permute-start.21 = (bf16[4,4,2048]{2,1,0:T(4,128)(2,1)S(1)}, bf16[4,4,2048]{2,1,0:T(4,128)(2,1)S(1)}, u32[]{:S(2)}, u32[]{:S(2)}) collective-permute-start(bf16[4,4,2048]{2,1,0:T(4,128)(2,1)S(1)} %fusion.10), channel_id=1, source_target_pairs={{0,2},{2,0},{1,3},{3,1},{4,6},{6,4},{5,7},{7,5},{8,10},{10,8},{9,1... | collective-permute-start | bytes 196616 | tf_op jit(solution)/shard_map/ppermute | solution.py:158
  54.3 11.2 %collective-permute-start.12 = (bf16[2,2,64,256]{3,2,1,0:T(8,128)(2,1)S(1)}, bf16[2,2,64,256]{3,2,1,0:T(8,128)(2,1)S(1)}, u32[]{:S(2)}, u32[]{:S(2)}) collective-permute-start(bf16[2,2,64,256]{3,2,1,0:T(8,128)(2,1)S(1)} %fusion.7), channel_id=1, source_target_pairs={{0,2},{2,0},{1,3},{3,1},{4,6},{6,4},{5,7},{7,5},{8,10},{10,8},{9,1... | collective-permute-start | bytes 393224 | tf_op jit(solution)/shard_map/ppermute | solution.py:158
  58.6 4.7 %collective-permute-start.22 = (bf16[4,2048]{1,0:T(4,128)(2,1)S(1)}, bf16[4,2048]{1,0:T(4,128)(2,1)S(1)}, u32[]{:S(2)}, u32[]{:S(2)}) collective-permute-start(bf16[4,2048]{1,0:T(4,128)(2,1)S(1)} %get-tuple-element.67), channel_id=1, source_target_pairs={{0,8},{4,12},{8,0},{12,4},{1,9},{5,13},{9,1},{13,5},{2,10},{6,14},... | collective-permute-start | bytes 49160 | tf_op jit(solution)/shard_map/ppermute | solution.py:158
  58.7 5.6 %collective-permute-start.23 = (bf16[4,2048]{1,0:T(4,128)(2,1)S(1)}, bf16[4,2048]{1,0:T(4,128)(2,1)S(1)}, u32[]{:S(2)}, u32[]{:S(2)}) collective-permute-start(bf16[4,2048]{1,0:T(4,128)(2,1)S(1)} %get-tuple-element.69), channel_id=1, source_target_pairs={{0,4},{4,8},{8,12},{12,0},{1,5},{5,9},{9,13},{13,1},{2,6},{6,10},{... | collective-permute-start | bytes 49160 | tf_op jit(solution)/shard_map/ppermute | solution.py:158
  60.8 4.6 %collective-permute-start.24 = (bf16[4,2048]{1,0:T(4,128)(2,1)S(1)}, bf16[4,2048]{1,0:T(4,128)(2,1)S(1)}, u32[]{:S(2)}, u32[]{:S(2)}) collective-permute-start(bf16[4,2048]{1,0:T(4,128)(2,1)S(1)} %get-tuple-element.68), channel_id=1, source_target_pairs={{0,12},{4,0},{8,4},{12,8},{1,13},{5,1},{9,5},{13,9},{2,14},{6,2},{... | collective-permute-start | bytes 49160 | tf_op jit(solution)/shard_map/ppermute | solution.py:158
  63.4 5.0 %collective-permute-start.15 = (bf16[2,2,64,256]{3,2,1,0:T(8,128)(2,1)S(1)}, bf16[2,2,64,256]{3,2,1,0:T(8,128)(2,1)S(1)}, u32[]{:S(2)}, u32[]{:S(2)}) collective-permute-start(bf16[2,2,64,256]{3,2,1,0:T(8,128)(2,1)S(1)} %fusion.8), channel_id=1, source_target_pairs={{0,2},{2,0},{1,3},{3,1},{4,6},{6,4},{5,7},{7,5},{8,10},{10,8},{9,1... | collective-permute-start | bytes 393224 | tf_op jit(solution)/shard_map/ppermute | solution.py:158
  64.3 5.4 %collective-permute-start.18 = (bf16[2,2,64,256]{3,2,1,0:T(8,128)(2,1)S(1)}, bf16[2,2,64,256]{3,2,1,0:T(8,128)(2,1)S(1)}, u32[]{:S(2)}, u32[]{:S(2)}) collective-permute-start(bf16[2,2,64,256]{3,2,1,0:T(8,128)(2,1)S(1)} %fusion.9), channel_id=1, source_target_pairs={{0,2},{2,0},{1,3},{3,1},{4,6},{6,4},{5,7},{7,5},{8,10},{10,8},{9,1... | collective-permute-start | bytes 393224 | tf_op jit(solution)/shard_map/ppermute | solution.py:158
  65.5 10.0 %collective-permute-start.13 = (bf16[2,2,64,256]{3,2,1,0:T(8,128)(2,1)S(1)}, bf16[2,2,64,256]{3,2,1,0:T(8,128)(2,1)S(1)}, u32[]{:S(2)}, u32[]{:S(2)}) collective-permute-start(bf16[2,2,64,256]{3,2,1,0:T(8,128)(2,1)S(1)} %fusion.2), channel_id=1, source_target_pairs={{0,8},{4,12},{8,0},{12,4},{1,9},{5,13},{9,1},{13,5},{2,10},{6,14},... | collective-permute-start | bytes 393224 | tf_op jit(solution)/shard_map/ppermute | solution.py:158
  68.4 7.2 %collective-permute-start.16 = (bf16[2,2,64,256]{3,2,1,0:T(8,128)(2,1)S(1)}, bf16[2,2,64,256]{3,2,1,0:T(8,128)(2,1)S(1)}, u32[]{:S(2)}, u32[]{:S(2)}) collective-permute-start(bf16[2,2,64,256]{3,2,1,0:T(8,128)(2,1)S(1)} %fusion.1), channel_id=1, source_target_pairs={{0,4},{4,8},{8,12},{12,0},{1,5},{5,9},{9,13},{13,1},{2,6},{6,10},{... | collective-permute-start | bytes 393224 | tf_op jit(solution)/shard_map/ppermute | solution.py:158
  69.8 7.1 %collective-permute-start.19 = (bf16[2,2,64,256]{3,2,1,0:T(8,128)(2,1)S(1)}, bf16[2,2,64,256]{3,2,1,0:T(8,128)(2,1)S(1)}, u32[]{:S(2)}, u32[]{:S(2)}) collective-permute-start(bf16[2,2,64,256]{3,2,1,0:T(8,128)(2,1)S(1)} %fusion), channel_id=1, source_target_pairs={{0,12},{4,0},{8,4},{12,8},{1,13},{5,1},{9,5},{13,9},{2,14},{6,2},{... | collective-permute-start | bytes 393224 | tf_op jit(solution)/shard_map/ppermute | solution.py:158
  (29 other events, 78.9 us)

commit v2 on v0

v2 whole, which is shorter than its diff:
```python
import functools
import itertools

import jax
import jax.numpy as jnp
from jax import lax
from jax.experimental import pallas as pl
from jax.experimental.pallas import tpu as pltpu
from jax.sharding import PartitionSpec as P

BF = jnp.bfloat16
F32 = jnp.float32
VM, SM, HBM = pltpu.VMEM, pltpu.SMEM, pltpu.HBM
PLANE = ("tensor", "dp", "seq")


def dot(a, b, ca, cb):
    return lax.dot_general(a, b, (((ca,), (cb,)), ((), ())), preferred_element_type=F32)


def class_of(d, c, ndp):
    return c * ndp + (d ^ (c * (ndp - 1)))


def plane(ndp, nseq):
    return [(i, j) for i in range(ndp)[::-1] for j in range(nseq)[::-1]]


def block(ref, index, size, axis=1):
    where = pl.ds(pl.multiple_of(index * size, size), size)
    return ref.at[:, where] if axis == 1 else ref.at[where]


def collect_kernel(dims, pairs, x, dy, left, up, down, right, *refs):
    ndp, nseq, turns = dims
    nclass = ndp * nseq
    weights, outs = refs[0], refs[1 : 1 + nclass]
    xbuf, lbuf, sems = refs[1 + nclass :]
    slots, blk = up.shape[:2]
    toks = x.shape[0]
    rank, ncols = right.shape[0], right.shape[1] // blk
    me, d, c = (lax.axis_index(a) for a in PLANE)
    copies = [pltpu.make_async_copy(left, lbuf, sems.at[0])]
    parts = 4
    rows = toks // parts
    for n in range(parts):
        here = pl.ds(n * rows, rows)
        copies.append(pltpu.make_async_copy(x.at[here], xbuf.at[here], sems.at[1 + n]))
    first = len(copies)
    moves = []
    for a, src in enumerate((up, down)):
        for s in range(slots):
            moves.append((src.at[s], weights.at[pl.ds((a * slots + s) * blk, blk)]))
    for j in range(ncols):
        moves.append((right.at[:, pl.ds(j * blk, blk)], weights.at[pl.ds(2 * slots * blk + j * rank, rank)]))
    for (i, j), out in zip(plane(ndp, nseq), outs):
        cls = class_of(d ^ i, c ^ j, ndp)
        for t in range(turns):
            panel = me ^ (cls + t * nclass)
            for a, src in enumerate((x, dy)):
                for s in range(slots):
                    row = ((t * 2 + a) * slots + s) * toks
                    moves.append((block(src, pairs[s, 0, panel], blk), out.at[pl.ds(row, toks)]))
    for n, (src, dst) in enumerate(moves):
        copies.append(pltpu.make_async_copy(src, dst, sems.at[first + n]))
    for copy in copies:
        copy.start()
    for copy in copies[:first]:
        copy.wait()
    factor = dot(lbuf[...], xbuf[...], 1, 1).astype(BF)
    for out in outs:
        tail = pl.ds(out.shape[0] - rank, rank)
        out[tail] = jnp.zeros((rank, blk), BF)
        out[tail, :toks] = factor
    for copy in copies[first:]:
        copy.wait()


def panel_kernel(dims, turn, pairs, live, weights, *refs):
    ndp, nseq, turns = dims
    nclass = ndp * nseq
    tokens, refs = refs[:nclass], refs[nclass:]
    grads, rgrad = refs[:2]
    parts, gfacs, (xcol, dycol, fact) = refs[2 : 2 + nseq], refs[2 + nseq : 2 + 2 * nseq], refs[2 + 2 * nseq :]
    slots, rows, blk = grads.shape[3:]
    rank = rgrad.shape[0]
    toks = fact.shape[1] // nclass
    me, d, c = (lax.axis_index(a) for a in PLANE)
    panel = me ^ (class_of(d, c, ndp) + turn * nclass)
    for n, src in enumerate(tokens):
        here = slice(n * toks, (n + 1) * toks)
        for s in range(slots):
            for a, dst in ((0, xcol), (1, dycol)):
                row = ((turn * 2 + a) * slots + s) * toks
                dst[s, here] = src[row : row + toks]
        fact[:, here] = src[src.shape[0] - rank :, :toks]
    cols = [pairs[s, 1, panel] for s in range(slots)]
    alive = [s < live[panel] for s in range(slots)]
    up = [weights[s * blk : (s + 1) * blk] for s in range(slots)]
    down = [weights[(slots + s) * blk : (slots + s + 1) * blk] for s in range(slots)]
    right = [weights[pl.ds(pl.multiple_of(2 * slots * blk + c_ * rank, rank), rank)] for c_ in cols]
    block_up = [dot(xcol[s], up[s], 1, 0) for s in range(slots)]
    block_down = [dot(dycol[s], down[s], 1, 1) for s in range(slots)]
    rgrad[...] = jnp.zeros(rgrad.shape, F32)
    gsum = None
    for s in range(slots):
        pre = dot(fact[...], right[s], 0, 0)
        dh = jnp.zeros(pre.shape, F32)
        single = alive[s]
        for t in range(slots):
            same = jnp.logical_and(cols[t] == cols[s], alive[t])
            pre = pre + jnp.where(same, block_up[t], 0.0)
            dh = dh + jnp.where(same, block_down[t], 0.0)
            if t < s:
                single = jnp.logical_and(single, jnp.logical_not(same))
        act = pre.astype(BF).astype(F32)
        sig = jax.nn.sigmoid(act)
        hid = (act * sig).astype(BF)
        dpre = (dh * (sig * (1.0 + act * (1.0 - sig)))).astype(BF)
        once = jnp.where(single, dpre, jnp.zeros_like(dpre))
        term = dot(right[s], once, 1, 1)
        gsum = term if gsum is None else gsum + term
        where = pl.ds(pl.multiple_of(cols[s] * blk, blk), blk)
        rgrad[:, where] = rgrad[:, where] + dot(fact[...], once, 1, 0)
        part = jnp.where(alive[s], dot(dpre, up[s], 1, 1), 0.0).astype(BF)
        for n, (i, j) in enumerate(plane(ndp, nseq)):
            parts[j][i, s * toks : (s + 1) * toks] = part[n * toks : (n + 1) * toks]
        gup = jnp.where(alive[s], dot(xcol[s], dpre, 0, 0), 0.0).astype(BF)
        gdown = jnp.where(alive[s], dot(hid, dycol[s], 0, 0), 0.0).astype(BF)
        for a, grad in ((0, gup), (1, gdown)):
            for i, j in itertools.product(range(ndp), range(nseq)):
                lo = (i * nseq + j) * rows
                grads[i, j, a, s] = grad[lo : lo + rows]
    for n, (i, j) in enumerate(plane(ndp, nseq)):
        gfacs[j][i] = gsum[:, n * toks : (n + 1) * toks]


def split_seq(value, ndp, nseq, here):
    rows = value.shape[0] // (ndp * nseq)
    v = [[value[(d * nseq + s) * rows : (d * nseq + s + 1) * rows] for d in range(ndp)] for s in range(nseq)]
    first, second = jnp.stack(v[0]), jnp.stack(v[1])
    return jnp.where(here == 0, first, second), jnp.where(here == 0, second, first)


def left_kernel(dims, x, total, gfac, keep, give):
    ndp, nseq, turns = dims
    npan, chunk = keep.shape[1], keep.shape[3]
    me, here = lax.axis_index("tensor"), lax.axis_index("seq")
    gf = total[...].astype(BF)
    gfac[...] = gf
    for k in range(npan):
        lg = dot(gf, block(x, me ^ k, chunk)[...], 1, 0)
        mine, other = split_seq(lg, ndp, nseq, here)
        for d in range(ndp):
            keep[d, k] = mine[d]
            give[d, k] = other[d]


def dx_kernel(dims, pairs, live, left, gfac, *refs):
    ndp, nseq, turns = dims
    parts, (dx, acc) = refs[:-2], refs[-2:]
    toks = dx.shape[0]
    blk = parts[0].shape[1]
    slots = parts[0].shape[0] // toks
    me, d, c = (lax.axis_index(a) for a in PLANE)
    acc[...] = dot(gfac[...], left[...], 0, 0)
    places = []
    for t in range(turns):
        per = parts[t * (nseq + ndp - 1) : (t + 1) * (nseq + ndp - 1)]
        places += [(t, 0, j, per[j]) for j in range(nseq)]
        places += [(t, i, j, per[nseq + i - 1].at[j]) for i in range(1, ndp) for j in range(nseq)]
    for t, i, j, part in places:
        panel = me ^ (class_of(d ^ i, c ^ j, ndp) + t * ndp * nseq)
        for s in range(slots):

            @pl.when(s < live[panel])
            def _(s=s, part=part, panel=panel):
                where = pl.ds(pl.multiple_of(pairs[s, 0, panel] * blk, blk), blk)
                acc[:, where] = acc[:, where] + part[s * toks : (s + 1) * toks].astype(F32)

    dx[...] = acc[...].astype(BF)


def call(name, kernel, spaces, outs, scratch, args, mib, flops):
    with jax.named_scope(name):
        return pl.pallas_call(
            kernel,
            out_shape=[jax.ShapeDtypeStruct(s, d) for s, d in outs],
            in_specs=[pl.BlockSpec(memory_space=space) for space in spaces],
            out_specs=[pl.BlockSpec(memory_space=VM)] * len(outs),
            scratch_shapes=scratch,
            compiler_params=pltpu.CompilerParams(vmem_limit_bytes=mib << 20),
            cost_estimate=pl.CostEstimate(flops=flops, bytes_accessed=1024, transcendentals=0),
        )(*args)


def permute(name, value, target):
    sizes = [lax.axis_size(a) for a in PLANE]

    def flat(z, d, c):
        return (z * sizes[1] + d) * sizes[2] + c

    spots = itertools.product(*(range(n) for n in sizes))
    with jax.named_scope(name):
        return lax.ppermute(value, PLANE, [(flat(*spot), flat(*target(*spot))) for spot in spots])


def after(value, *others):
    return lax.optimization_barrier((value, others))[0]


def pick(value, index, axis):
    return lax.dynamic_index_in_dim(value, index, axis, keepdims=False)


def per_device(tokens, grad_out, up_blocks, down_blocks, pairs, live, left_factor, right_factor):
    npan, ndp, nseq = (lax.axis_size(a) for a in PLANE)
    me, dpi, core = (lax.axis_index(a) for a in PLANE)
    x, dy = tokens[0], grad_out[0]
    toks, width = x.shape
    up, down = up_blocks[0], down_blocks[0]
    slots, blk = up.shape[:2]
    rank, pwidth = right_factor.shape
    ncols = pwidth // blk
    nclass = ndp * nseq
    turns = npan // nclass
    assert nseq == 2 and npan == turns * nclass and npan & (npan - 1) == 0 and ndp & (ndp - 1) == 0
    dims = (ndp, nseq, turns)
    rows, rk, chunk = blk // nclass, rank // nclass, width // npan
    pairs, left_t = pairs.transpose(1, 2, 0), left_factor.T
    partners = plane(ndp, nseq)

    def handled(d, c, t):
        return class_of(d, c, ndp) + t * nclass

    wrows = 2 * slots * blk + ncols * rank
    trows = turns * 2 * slots * toks + rank
    ncopy = 5 + 2 * slots + ncols + nclass * turns * 2 * slots
    weights, *sent = call(
        "collect", functools.partial(collect_kernel, dims), [SM] + [HBM] * 6,
        [((wrows, blk), BF)] + [((trows, blk), BF)] * nclass,
        [pltpu.VMEM((toks, width), BF), pltpu.VMEM((rank, width), BF), pltpu.SemaphoreType.DMA((ncopy,))],
        (pairs, *(pltpu.with_memory_space_constraint(v, HBM) for v in (x, dy, left_t, up, down, right_factor))), 16, 10**8,
    )
    held = [permute(f"weights{t}", weights, lambda z, d, c, t=t: (z ^ handled(d, c, t), d, c)) for t in range(turns)]
    got = [
        permute(f"tokens{i}{j}", v, lambda z, d, c, i=i, j=j: (z, d ^ i, c ^ j)) if i or j else v
        for (i, j), v in zip(partners, sent)
    ]
    grads, rights, parts, gfacs = [], [], [], []
    for t in range(turns):
        grad, right, *rest = call(
            f"panel{t}", functools.partial(panel_kernel, dims, t), [SM] * 2 + [VM] * (1 + nclass),
            [((ndp, nseq, 2, slots, rows, blk), BF), ((rank, pwidth), F32)]
            + [((ndp, slots * toks, blk), BF)] * nseq + [((ndp, rank, toks), F32)] * nseq,
            [pltpu.VMEM((slots, nclass * toks, blk), BF)] * 2 + [pltpu.VMEM((rank, nclass * toks), BF)],
            (pairs, live, held[t], *got), 16, 10**8,
        )
        grads.append(grad)
        rights.append(right)
        parts.append(rest[:nseq])
        gfacs.append(rest[nseq:])

    swap = lambda z, d, c: (z, d, c ^ 1)

    def across(name, value, i):
        return permute(f"{name}{i}", value, lambda z, d, c: (z, d ^ i, c))

    own = sum(gfacs[t][0] for t in range(turns))
    own = own + permute("gfac_core", sum(gfacs[t][1] for t in range(turns)), swap)
    gsum = own[0]
    for i in range(1, ndp):
        gsum = gsum + across("gfac_dp", own[i], i)
    gfac, keep, give = call(
        "left", functools.partial(left_kernel, dims), [VM] * 2,
        [((rank, toks), BF)] + [((ndp, npan, rk, chunk), F32)] * 2, [], (x, gsum), 12, 10**8,
    )
    low = keep + permute("left_core", give, swap)
    mine = pick(low, dpi, 0)
    away = [pick(low, dpi ^ i, 0).astype(BF) for i in range(1, ndp)]
    for i in range(1, ndp):
        mine = mine + permute(f"left_dp{i}", away[i - 1], lambda z, d, c, i=i: (z, d ^ i, c)).astype(F32)
    part_all = []
    for t in range(turns):
        near = parts[t][0], permute(f"parts_core{t}", parts[t][1], swap)
        part_all += [v[0] for v in near]
        for i in range(1, ndp):
            leave = after(jnp.stack([v[i] for v in near]), away)
            part_all.append(across(f"parts_dp{t}", leave, i))
    lots = []
    for t in range(turns):
        rsplit = rights[t].reshape(ndp, nseq, rk, pwidth)
        for i in range(ndp):
            lots.append(jnp.concatenate(
                [pick(grads[t], dpi ^ i, 0).reshape(nseq, -1, blk), pick(rsplit, dpi ^ i, 0).astype(BF).reshape(nseq, -1, blk)],
                axis=1,
            ))
    lots = after(lots, away)
    came = [
        permute(f"grads{t}{i}", lots[t * ndp + i], lambda z, d, c, t=t, i=i: (z ^ handled(d, c, t), d ^ i, c))
        for t in range(turns) for i in range(ndp)
    ]
    owned = sum(v.astype(F32) for v in came)
    step = npan
    while step > 1:
        step //= 2
        sent = mine[step:].astype(BF)
        mine = mine[:step] + permute(f"left_tensor{step}", sent, lambda z, d, c, k=step: (z ^ k, d, c)).astype(F32)
    left = mine[0]
    (dx,) = call(
        "dx", functools.partial(dx_kernel, dims), [SM] * 2 + [VM] * (2 + len(part_all)),
        [((toks, width), BF)], [pltpu.VMEM((toks, width), F32)],
        (pairs, live, left_t, gfac, *part_all), 12, 10**8,
    )
    owned = after(owned, dx)
    leave = pick(owned, 1 - core, 0).astype(BF)
    total = pick(owned, core, 0) + permute("grads_core", leave, swap).astype(F32)
    nblock = 2 * slots * rows
    blocks = total[:nblock].reshape(2, 1, slots, rows, blk)
    return dx[None], blocks[0], blocks[1], left.T, total[nblock:].reshape(rk, pwidth)


def solution(mesh):
    return jax.shard_map(
        per_device,
        mesh=mesh,
        in_specs=(
            P(("groups", "dp", "seq"), "tensor", None),
            P(("groups", "dp", "seq"), "tensor", None),
            P("tensor", None, None, None),
            P("tensor", None, None, None),
            P(),
            P(),
            P(),
            P(None, "tensor"),
        ),
        out_specs=(
            P(("groups", "dp", "seq"), "tensor", None),
            P(("groups", "tensor"), None, ("dp", "seq"), None),
            P(("groups", "tensor"), None, ("dp", "seq"), None),
            P(("groups", "tensor"), ("dp", "seq")),
            P(("groups", "dp", "seq"), "tensor"),
        ),
        check_vma=False,
    )
```

time: 198 us -> 55.4 us (0.28)
  waiting for transfers between devices: 106 us -> 23.6 us
  local copies, waits for them, and re-layouts: 25.9 us -> 2.24 us
  blocking collectives: 14.9 us -> 0 us
  between operations: 14.9 us -> 0.83 us
  matrix products: 11.2 us -> 0 us
  other arithmetic: 10.9 us -> 0.84 us
  Pallas kernels: 0 us -> 7.42 us
  starting transfers between devices: 14.1 us -> 20.3 us
    reduce_scatter x4 -> x0, waiting for transfers between devices: 74 us -> none  [the longest x1 24.6 us: per_device(): lax.psum_scatter(gw_up, ('dp', 'seq'), scatter_dimension=1, tiled=True)]
    ppermute x0 -> x15, waiting for transfers between devices: none -> 23.6 us  [permute(): lax.ppermute(value, PLANE, [(flat(*spot), flat(*target(*spot))) for spot...]
    unnamed x6 -> x0, waiting for transfers between devices: 22.6 us -> none
    ppermute x0 -> x15, starting transfers between devices: none -> 20.3 us  [permute(): lax.ppermute(value, PLANE, [(flat(*spot), flat(*target(*spot))) for spot...]
    all_gather x1 -> x0, blocking collectives: 14.9 us -> none  [per_device(): factor = lax.all_gather(factor_local, 'tensor', axis=0, tiled=True)]
    all_to_all x3 -> x0, starting transfers between devices: 13.9 us -> none  [the longest x1 6.32 us: per_device(): lax.all_to_all(sent_x, 'tensor', split_axis=1, concat_axis=0, tiled=True)]
    dot_general x12 -> x0, matrix products: 11.2 us -> none  [the longest x2 3.08 us: contract(): lax.dot_general(left, right, (((left_dim,), (right_dim,)), ((), ())), pre...]
    all_to_all x3 -> x0, waiting for transfers between devices: 8.97 us -> none  [the longest x1 8.96 us: per_device(): lax.all_to_all(sent_dy, 'tensor', split_axis=1, concat_axis=0, tiled=True)]
  transfers between devices with their start and end apart: 8 -> 15, of which waited for: 6 -> 10; matrix products, arithmetic and copies ran while one was open for 13% -> 2% of each run, Pallas kernels for 0% -> 4%
where the time goes in v2:
time: 55.4 us; the launch traced here: 55.2 us
  waiting for transfers between devices  23.6 us (43%)
  starting transfers between devices  20.3 us (37%)
  Pallas kernels  7.42 us (13%)
  local copies, waits for them, and re-layouts  2.24 us (4%)
  other arithmetic  0.84 us (2%)
  between operations  0.83 us (1%)
    ppermute x15, waiting for transfers between devices, permute(): lax.ppermute(value, PLANE, [(flat(*spot), flat(*target(*spot))) for spot...  23.6 us
    ppermute x15, starting transfers between devices, permute(): lax.ppermute(value, PLANE, [(flat(*spot), flat(*target(*spot))) for spot...  20.3 us
    pallas_call x4, Pallas kernels, call(): pl.pallas_call(kernel, out_shape=[jax.ShapeDtypeStruct(s, d) for s, d in...  7.42 us
  transfers between devices with their start and end apart: 15, of which 10 were waited for; matrix products, arithmetic and copies ran while one was open for 2% of the time, Pallas kernels for 4%

profile of v2, /device:TPU:0, one launch (start us, length us, event | category | flops | bytes accessed | tf_op | source)
XLA Modules:
  0.0 55.2 jit_solution(13688099472653884104)
XLA Ops:
  0.6 0.7 %copy-done.2 = s32[4,2,2]{0,2,1:T(2,128)S(1)} copy-done((s32[4,2,2]{0,2,1:T(2,128)S(1)}, s32[4,2,2]{0,2,1:T(2,128)}, u32[]{:S(2)}) %copy-start.2) | copy-done | bytes 88
  1.3 2.5 %collect.1 = (bf16[1088,256]{1,0:T(8,128)(2,1)S(1)}, bf16[528,256]{1,0:T(8,128)(2,1)S(1)}, bf16[528,256]{1,0:T(8,128)(2,1)S(1)}, bf16[528,256]{1,0:T(8,128)(2,1)S(1)}, bf16[528,256]{1,0:T(8,128)(2,1)S(1)}) custom-call(s32[2,2,4]{2,1,0:T(2,128)S(1)} %bitcast.37, bf16[128,4096]{1,0:T(8,128)(2,1)} %bitcast.33, bf16[128,4096]{1,0:T(8,128)(2,1)} %bitcast.42, ...), custom_call_target="tpu_custom_call" | custom-call | flops 100000000 | bytes 1024 | tf_op jit(solution)/shard_map/collect/pallas_call | solution.py:186
  3.9 0.7 %collective-permute-start = (bf16[1088,256]{1,0:T(8,128)(2,1)S(1)}, bf16[1088,256]{1,0:T(8,128)(2,1)S(1)}, u32[]{:S(2)}, u32[]{:S(2)}) collective-permute-start(bf16[1088,256]{1,0:T(8,128)(2,1)S(1)} %get-tuple-element.23), channel_id=1, source_target_pairs={{0,0},{1,13},{2,6},{3,11},{4,4},{5,9},{6,2},{7,15},{8,8},{9,5},{10... | collective-permute-start | bytes 1671176 | tf_op jit(solution)/shard_map/weights0/ppermute | solution.py:205
  4.6 6.0 %collective-permute-start.1 = (bf16[528,256]{1,0:T(8,128)(2,1)S(1)}, bf16[528,256]{1,0:T(8,128)(2,1)S(1)}, u32[]{:S(2)}, u32[]{:S(2)}) collective-permute-start(bf16[528,256]{1,0:T(8,128)(2,1)S(1)} %get-tuple-element.24), channel_id=1, source_target_pairs={{0,3},{1,2},{2,1},{3,0},{4,7},{5,6},{6,5},{7,4},{8,11},{9,10},{10,... | collective-permute-start | bytes 811016 | tf_op jit(solution)/shard_map/tokens11/ppermute | solution.py:205
  10.5 1.5 %collective-permute-start.2 = (bf16[528,256]{1,0:T(8,128)(2,1)S(1)}, bf16[528,256]{1,0:T(8,128)(2,1)S(1)}, u32[]{:S(2)}, u32[]{:S(2)}) collective-permute-start(bf16[528,256]{1,0:T(8,128)(2,1)S(1)} %get-tuple-element.25), channel_id=1, source_target_pairs={{0,2},{1,3},{2,0},{3,1},{4,6},{5,7},{6,4},{7,5},{8,10},{9,11},{10,... | collective-permute-start | bytes 811016 | tf_op jit(solution)/shard_map/tokens10/ppermute | solution.py:205
  12.1 5.3 %collective-permute-done.1.refs_0_ = bf16[528,256]{1,0:T(8,128)(2,1)S(1)} collective-permute-done((bf16[528,256]{1,0:T(8,128)(2,1)S(1)}, bf16[528,256]{1,0:T(8,128)(2,1)S(1)}, u32[]{:S(2)}, u32[]{:S(2)}) %collective-permute-start.1) | collective-permute-done | bytes 270368 | tf_op jit(solution)/shard_map/tokens11/ppermute | solution.py:205
  17.4 6.0 %collective-permute-done.2.refs_1_ = bf16[528,256]{1,0:T(8,128)(2,1)S(1)} collective-permute-done((bf16[528,256]{1,0:T(8,128)(2,1)S(1)}, bf16[528,256]{1,0:T(8,128)(2,1)S(1)}, u32[]{:S(2)}, u32[]{:S(2)}) %collective-permute-start.2) | collective-permute-done | bytes 270368 | tf_op jit(solution)/shard_map/tokens10/ppermute | solution.py:205
  23.4 2.4 %panel0.1 = (bf16[2,2,2,2,64,256]{5,4,3,2,1,0:T(8,128)(2,1)S(1)}, f32[16,1024]{1,0:T(8,128)S(1)}, bf16[2,256,256]{2,1,0:T(8,128)(2,1)S(1)}, bf16[2,256,256]{2,1,...) custom-call(s32[2,2,4]{2,1,0:T(2,128)S(1)} %bitcast.38, s32[4]{0:T(128)S(1)} %copy-done.3, ...), custom_call_target="tpu_custom_call" | custom-call | flops 100000000 | bytes 1024 | tf_op jit(solution)/shard_map/panel0/pallas_call | solution.py:186
  26.4 0.7 %collective-permute-done.4 = f32[2,16,128]{2,1,0:T(8,128)S(1)} collective-permute-done((f32[2,16,128]{2,1,0:T(8,128)S(1)}, f32[2,16,128]{2,1,0:T(8,128)S(1)}, u32[]{:S(2)}, u32[]{:S(2)}) %collective-permute-start.4) | collective-permute-done | bytes 16416 | tf_op jit(solution)/shard_map/gfac_core/ppermute | solution.py:205
  27.1 1.6 %collective-permute-start.5 = (f32[16,128]{1,0:T(8,128)S(1)}, f32[16,128]{1,0:T(8,128)S(1)}, u32[]{:S(2)}, u32[]{:S(2)}) collective-permute-start(f32[16,128]{1,0:T(8,128)S(1)} %slice_bitcast_fusion.2), channel_id=1, source_target_pairs={{0,2},{1,3},{2,0},{3,1},{4,6},{5,7},{6,4},{7,5},{8,10},{9,11},{10,... | collective-permute-start | bytes 24584 | tf_op jit(solution)/shard_map/gfac_dp1/ppermute | solution.py:205
  28.7 2.0 %collective-permute-done.5 = f32[16,128]{1,0:T(8,128)S(1)} collective-permute-done((f32[16,128]{1,0:T(8,128)S(1)}, f32[16,128]{1,0:T(8,128)S(1)}, u32[]{:S(2)}, u32[]{:S(2)}) %collective-permute-start.5) | collective-permute-done | bytes 8224 | tf_op jit(solution)/shard_map/gfac_dp1/ppermute | solution.py:205
  31.2 1.2 %collective-permute-done.7 = f32[2,4,4,1024]{3,2,1,0:T(4,128)S(1)} collective-permute-done((f32[2,4,4,1024]{3,2,1,0:T(4,128)S(1)}, f32[2,4,4,1024]{3,2,1,0:T(4,128)S(1)}, u32[]{:S(2)}, u32[]{:S(2)}) %collective-permute-start.7) | collective-permute-done | bytes 131104 | tf_op jit(solution)/shard_map/left_core/ppermute | solution.py:205
  32.4 1.6 %collective-permute-start.12 = (bf16[4,4,1024]{2,1,0:T(4,128)(2,1)S(1)}, bf16[4,4,1024]{2,1,0:T(4,128)(2,1)S(1)}, u32[]{:S(2)}, u32[]{:S(2)}) collective-permute-start(bf16[4,4,1024]{2,1,0:T(4,128)(2,1)S(1)} %fusion.1), channel_id=1, source_target_pairs={{0,2},{1,3},{2,0},{3,1},{4,6},{5,7},{6,4},{7,5},{8,10},{9,11},{10,... | collective-permute-start | bytes 98312 | tf_op jit(solution)/shard_map/left_dp1/ppermute | solution.py:205
  34.6 0.7 %collective-permute-start.9 = (bf16[2,272,256]{2,1,0:T(8,128)(2,1)S(1)}, bf16[2,272,256]{2,1,0:T(8,128)(2,1)S(1)}, u32[]{:S(2)}, u32[]{:S(2)}) collective-permute-start(bf16[2,272,256]{2,1,0:T(8,128)(2,1)S(1)} %get-tuple-element.38), channel_id=1, source_target_pairs={{0,0},{1,13},{2,6},{3,11},{4,4},{5,9},{6,2},{7,15},{8,8},{9,5},{10... | collective-permute-start | bytes 835592 | tf_op jit(solution)/shard_map/grads00/ppermute | solution.py:205
  35.3 1.1 %collective-permute-done.12 = bf16[4,4,1024]{2,1,0:T(4,128)(2,1)S(1)} collective-permute-done((bf16[4,4,1024]{2,1,0:T(4,128)(2,1)S(1)}, bf16[4,4,1024]{2,1,0:T(4,128)(2,1)S(1)}, u32[]{:S(2)}, u32[]{:S(2)}) %collective-permute-start.12) | collective-permute-done | bytes 32800 | tf_op jit(solution)/shard_map/left_dp1/ppermute | solution.py:205
  37.1 4.8 %collective-permute-start.8 = (bf16[2,256,256]{2,1,0:T(8,128)(2,1)S(1)}, bf16[2,256,256]{2,1,0:T(8,128)(2,1)S(1)}, u32[]{:S(2)}, u32[]{:S(2)}) collective-permute-start(bf16[2,256,256]{2,1,0:T(8,128)(2,1)S(1)} %pad_maximum_fusion.2), channel_id=1, source_target_pairs={{0,2},{1,3},{2,0},{3,1},{4,6},{5,7},{6,4},{7,5},{8,10},{9,11},{10,... | collective-permute-start | bytes 786440 | tf_op jit(solution)/shard_map/parts_dp01/ppermute | solution.py:205
  42.0 1.2 %collective-permute-start.14 = (bf16[1,4,1024]{2,1,0:T(4,128)(2,1)S(1)}, bf16[1,4,1024]{2,1,0:T(4,128)(2,1)S(1)}, u32[]{:S(2)}, u32[]{:S(2)}) collective-permute-start(bf16[1,4,1024]{2,1,0:T(4,128)(2,1)S(1)} %slice.83), channel_id=1, source_target_pairs={{0,4},{1,5},{2,6},{3,7},{4,0},{5,1},{6,2},{7,3},{8,12},{9,13},{10,... | collective-permute-start | bytes 24584 | tf_op jit(solution)/shard_map/left_tensor1/ppermute | solution.py:205
  43.2 1.0 %collective-permute-done.10 = bf16[2,272,256]{2,1,0:T(8,128)(2,1)S(1)} collective-permute-done((bf16[2,272,256]{2,1,0:T(8,128)(2,1)S(1)}, bf16[2,272,256]{2,1,0:T(8,128)(2,1)S(1)}, u32[]{:S(2)}, u32[]{:S(2)}) %collective-permute-start.10) | collective-permute-done | bytes 278560 | tf_op jit(solution)/shard_map/grads01/ppermute | solution.py:205
  44.3 5.7 %collective-permute-done.8.refs_2_ = bf16[2,256,256]{2,1,0:T(8,128)(2,1)S(1)} collective-permute-done((bf16[2,256,256]{2,1,0:T(8,128)(2,1)S(1)}, bf16[2,256,256]{2,1,0:T(8,128)(2,1)S(1)}, u32[]{:S(2)}, u32[]{:S(2)}) %collective-permute-start.8) | collective-permute-done | bytes 262176 | tf_op jit(solution)/shard_map/parts_dp01/ppermute | solution.py:205
  50.0 2.2 %dx.1 = bf16[128,4096]{1,0:T(8,128)(2,1)} custom-call(s32[2,2,4]{2,1,0:T(2,128)S(1)} %bitcast.39, s32[4]{0:T(128)S(1)} %copy-done.3, bf16[16,4096]{1,0:T(8,128)(2,1)S(1)} %bitcast.36, bf16[16,128]{1,0:T(8,128)(2,1)S(1)} %get-tuple-element.30.gfac, bf16[256,256]{1,0:T(8,128)(2,1)S(1)} %get-tuple-element.46.refs_0_, ...), custom_call_target="tpu_custom_call" | custom-call | flops 100000000 | bytes 1024 | tf_op jit(solution)/shard_map/dx/pallas_call | solution.py:186
  52.3 0.6 %collective-permute-start.11 = (bf16[272,256]{1,0:T(8,128)(2,1)S(1)}, bf16[272,256]{1,0:T(8,128)(2,1)S(1)}, u32[]{:S(2)}, u32[]{:S(2)}) collective-permute-start(bf16[272,256]{1,0:T(8,128)(2,1)S(1)} %fusion), channel_id=1, source_target_pairs={{0,1},{1,0},{2,3},{3,2},{4,5},{5,4},{6,7},{7,6},{8,9},{9,8},{10,11... | collective-permute-start | bytes 417800 | tf_op jit(solution)/shard_map/grads_core/ppermute | solution.py:205
  52.9 0.6 %fusion.2 = f32[1024,4]{0,1:T(4,128)} fusion(f32[2,4,1024]{2,1,0:T(4,128)S(1)} %slice_add_fusion, bf16[1,4,1024]{2,1,0:T(4,128)(2,1)S(1)} %collective-permute-done.14), kind=kLoop, calls=%fused_computation.18 | loop fusion | flops 8192 | bytes 40960 | tf_op jit(solution)/shard_map/transpose | solution.py:320
  53.9 0.7 %fusion.4 = (f32[128,256]{1,0:T(8,128)}, f32[128,256]{1,0:T(8,128)}) fusion(f32[272,256]{1,0:T(8,128)S(1)} %bitcast_add_fusion), kind=kLoop, calls=%fused_computation.24 | loop fusion | bytes 524288 | tf_op jit(solution)/shard_map/slice | solution.py:320
  54.6 0.6 %reshape.40 = f32[4,1024]{1,0:T(4,128)} reshape(f32[16,256]{1,0:T(8,128)S(1)} %slice.69) | data formatting | bytes 32768 | tf_op jit(solution)/shard_map/reshape | solution.py:320
  (43 shorter events, 2.9 us)
Async XLA Ops:
  0.6 0.7 %copy-start.2 = (s32[4,2,2]{0,2,1:T(2,128)S(1)}, s32[4,2,2]{0,2,1:T(2,128)}, u32[]{:S(2)}) copy-start(s32[4,2,2]{0,2,1:T(2,128)} %param.12) | copy-start | bytes 196
  3.9 19.5 %collective-permute-start = (bf16[1088,256]{1,0:T(8,128)(2,1)S(1)}, bf16[1088,256]{1,0:T(8,128)(2,1)S(1)}, u32[]{:S(2)}, u32[]{:S(2)}) collective-permute-start(bf16[1088,256]{1,0:T(8,128)(2,1)S(1)} %get-tuple-element.23), channel_id=1, source_target_pairs={{0,0},{1,13},{2,6},{3,11},{4,4},{5,9},{6,2},{7,15},{8,8},{9,5},{10... | collective-permute-start | bytes 1671176 | tf_op jit(solution)/shard_map/weights0/ppermute | solution.py:205
  4.6 12.8 %collective-permute-start.1 = (bf16[528,256]{1,0:T(8,128)(2,1)S(1)}, bf16[528,256]{1,0:T(8,128)(2,1)S(1)}, u32[]{:S(2)}, u32[]{:S(2)}) collective-permute-start(bf16[528,256]{1,0:T(8,128)(2,1)S(1)} %get-tuple-element.24), channel_id=1, source_target_pairs={{0,3},{1,2},{2,1},{3,0},{4,7},{5,6},{6,5},{7,4},{8,11},{9,10},{10,... | collective-permute-start | bytes 811016 | tf_op jit(solution)/shard_map/tokens11/ppermute | solution.py:205
  10.5 12.8 %collective-permute-start.2 = (bf16[528,256]{1,0:T(8,128)(2,1)S(1)}, bf16[528,256]{1,0:T(8,128)(2,1)S(1)}, u32[]{:S(2)}, u32[]{:S(2)}) collective-permute-start(bf16[528,256]{1,0:T(8,128)(2,1)S(1)} %get-tuple-element.25), channel_id=1, source_target_pairs={{0,2},{1,3},{2,0},{3,1},{4,6},{5,7},{6,4},{7,5},{8,10},{9,11},{10,... | collective-permute-start | bytes 811016 | tf_op jit(solution)/shard_map/tokens10/ppermute | solution.py:205
  12.1 11.3 %copy-start.3 = (s32[4]{0:T(128)S(1)}, s32[4]{0:T(128)}, u32[]{:S(2)}) copy-start(s32[4]{0:T(128)} %live.3) | copy-start | bytes 52
  12.1 11.3 %collective-permute-start.3 = (bf16[528,256]{1,0:T(8,128)(2,1)S(1)}, bf16[528,256]{1,0:T(8,128)(2,1)S(1)}, u32[]{:S(2)}, u32[]{:S(2)}) collective-permute-start(bf16[528,256]{1,0:T(8,128)(2,1)S(1)} %get-tuple-element.26), channel_id=1, source_target_pairs={{0,1},{1,0},{2,3},{3,2},{4,5},{5,4},{6,7},{7,6},{8,9},{9,8},{10,11... | collective-permute-start | bytes 811016 | tf_op jit(solution)/shard_map/tokens01/ppermute | solution.py:205
  23.4 7.3 %copy-start = (bf16[1,128,4096]{2,1,0:T(8,128)(2,1)S(1)}, bf16[1,128,4096]{2,1,0:T(8,128)(2,1)}, u32[]{:S(2)}) copy-start(bf16[1,128,4096]{2,1,0:T(8,128)(2,1)} %param.8) | copy-start | bytes 3145732
  25.8 1.2 %collective-permute-start.4 = (f32[2,16,128]{2,1,0:T(8,128)S(1)}, f32[2,16,128]{2,1,0:T(8,128)S(1)}, u32[]{:S(2)}, u32[]{:S(2)}) collective-permute-start(f32[2,16,128]{2,1,0:T(8,128)S(1)} %get-tuple-element.29), channel_id=1, source_target_pairs={{0,1},{1,0},{2,3},{3,2},{4,5},{5,4},{6,7},{7,6},{8,9},{9,8},{10,11... | collective-permute-start | bytes 49160 | tf_op jit(solution)/shard_map/gfac_core/ppermute | solution.py:205
  25.9 11.1 %collective-permute-start.6 = (bf16[2,256,256]{2,1,0:T(8,128)(2,1)S(1)}, bf16[2,256,256]{2,1,0:T(8,128)(2,1)S(1)}, u32[]{:S(2)}, u32[]{:S(2)}) collective-permute-start(bf16[2,256,256]{2,1,0:T(8,128)(2,1)S(1)} %get-tuple-element.32), channel_id=1, source_target_pairs={{0,1},{1,0},{2,3},{3,2},{4,5},{5,4},{6,7},{7,6},{8,9},{9,8},{10,11... | collective-permute-start | bytes 786440 | tf_op jit(solution)/shard_map/parts_core0/ppermute | solution.py:205
  27.1 3.7 %collective-permute-start.5 = (f32[16,128]{1,0:T(8,128)S(1)}, f32[16,128]{1,0:T(8,128)S(1)}, u32[]{:S(2)}, u32[]{:S(2)}) collective-permute-start(f32[16,128]{1,0:T(8,128)S(1)} %slice_bitcast_fusion.2), channel_id=1, source_target_pairs={{0,2},{1,3},{2,0},{3,1},{4,6},{5,7},{6,4},{7,5},{8,10},{9,11},{10,... | collective-permute-start | bytes 24584 | tf_op jit(solution)/shard_map/gfac_dp1/ppermute | solution.py:205
  31.0 1.4 %collective-permute-start.7 = (f32[2,4,4,1024]{3,2,1,0:T(4,128)S(1)}, f32[2,4,4,1024]{3,2,1,0:T(4,128)S(1)}, u32[]{:S(2)}, u32[]{:S(2)}) collective-permute-start(f32[2,4,4,1024]{3,2,1,0:T(4,128)S(1)} %get-tuple-element.34), channel_id=1, source_target_pairs={{0,1},{1,0},{2,3},{3,2},{4,5},{5,4},{6,7},{7,6},{8,9},{9,8},{10,11... | collective-permute-start | bytes 393224 | tf_op jit(solution)/shard_map/left_core/ppermute | solution.py:205
  32.4 4.0 %collective-permute-start.12 = (bf16[4,4,1024]{2,1,0:T(4,128)(2,1)S(1)}, bf16[4,4,1024]{2,1,0:T(4,128)(2,1)S(1)}, u32[]{:S(2)}, u32[]{:S(2)}) collective-permute-start(bf16[4,4,1024]{2,1,0:T(4,128)(2,1)S(1)} %fusion.1), channel_id=1, source_target_pairs={{0,2},{1,3},{2,0},{3,1},{4,6},{5,7},{6,4},{7,5},{8,10},{9,11},{10,... | collective-permute-start | bytes 98312 | tf_op jit(solution)/shard_map/left_dp1/ppermute | solution.py:205
  34.1 10.1 %collective-permute-start.10 = (bf16[2,272,256]{2,1,0:T(8,128)(2,1)S(1)}, bf16[2,272,256]{2,1,0:T(8,128)(2,1)S(1)}, u32[]{:S(2)}, u32[]{:S(2)}) collective-permute-start(bf16[2,272,256]{2,1,0:T(8,128)(2,1)S(1)} %get-tuple-element.39), channel_id=1, source_target_pairs={{0,2},{1,15},{2,4},{3,9},{4,6},{5,11},{6,0},{7,13},{8,10},{9,7},{1... | collective-permute-start | bytes 835592 | tf_op jit(solution)/shard_map/grads01/ppermute | solution.py:205
  34.6 9.6 %collective-permute-start.9 = (bf16[2,272,256]{2,1,0:T(8,128)(2,1)S(1)}, bf16[2,272,256]{2,1,0:T(8,128)(2,1)S(1)}, u32[]{:S(2)}, u32[]{:S(2)}) collective-permute-start(bf16[2,272,256]{2,1,0:T(8,128)(2,1)S(1)} %get-tuple-element.38), channel_id=1, source_target_pairs={{0,0},{1,13},{2,6},{3,11},{4,4},{5,9},{6,2},{7,15},{8,8},{9,5},{10... | collective-permute-start | bytes 835592 | tf_op jit(solution)/shard_map/grads00/ppermute | solution.py:205
  36.5 5.5 %collective-permute-start.13 = (bf16[2,4,1024]{2,1,0:T(4,128)(2,1)S(1)}, bf16[2,4,1024]{2,1,0:T(4,128)(2,1)S(1)}, u32[]{:S(2)}, u32[]{:S(2)}) collective-permute-start(bf16[2,4,1024]{2,1,0:T(4,128)(2,1)S(1)} %slice.82), channel_id=1, source_target_pairs={{0,8},{1,9},{2,10},{3,11},{4,12},{5,13},{6,14},{7,15},{8,0},{9,1},... | collective-permute-start | bytes 49160 | tf_op jit(solution)/shard_map/left_tensor2/ppermute | solution.py:205
  37.1 12.9 %collective-permute-start.8 = (bf16[2,256,256]{2,1,0:T(8,128)(2,1)S(1)}, bf16[2,256,256]{2,1,0:T(8,128)(2,1)S(1)}, u32[]{:S(2)}, u32[]{:S(2)}) collective-permute-start(bf16[2,256,256]{2,1,0:T(8,128)(2,1)S(1)} %pad_maximum_fusion.2), channel_id=1, source_target_pairs={{0,2},{1,3},{2,0},{3,1},{4,6},{5,7},{6,4},{7,5},{8,10},{9,11},{10,... | collective-permute-start | bytes 786440 | tf_op jit(solution)/shard_map/parts_dp01/ppermute | solution.py:205
  42.0 8.0 %copy-start.1 = (bf16[4096,16]{0,1:T(8,128)(2,1)S(1)}, bf16[4096,16]{0,1:T(8,128)(2,1)}, u32[]{:S(2)}) copy-start(bf16[4096,16]{0,1:T(8,128)(2,1)} %param.14) | copy-start | bytes 393220
  42.0 10.8 %collective-permute-start.14 = (bf16[1,4,1024]{2,1,0:T(4,128)(2,1)S(1)}, bf16[1,4,1024]{2,1,0:T(4,128)(2,1)S(1)}, u32[]{:S(2)}, u32[]{:S(2)}) collective-permute-start(bf16[1,4,1024]{2,1,0:T(4,128)(2,1)S(1)} %slice.83), channel_id=1, source_target_pairs={{0,4},{1,5},{2,6},{3,7},{4,0},{5,1},{6,2},{7,3},{8,12},{9,13},{10,... | collective-permute-start | bytes 24584 | tf_op jit(solution)/shard_map/left_tensor1/ppermute | solution.py:205
  52.3 1.6 %collective-permute-start.11 = (bf16[272,256]{1,0:T(8,128)(2,1)S(1)}, bf16[272,256]{1,0:T(8,128)(2,1)S(1)}, u32[]{:S(2)}, u32[]{:S(2)}) collective-permute-start(bf16[272,256]{1,0:T(8,128)(2,1)S(1)} %fusion), channel_id=1, source_target_pairs={{0,1},{1,0},{2,3},{3,2},{4,5},{5,4},{6,7},{7,6},{8,9},{9,8},{10,11... | collective-permute-start | bytes 417800 | tf_op jit(solution)/shard_map/grads_core/ppermute | solution.py:205

commit v3 on v2

--- a/solution.py
+++ b/solution.py
@@ -35,7 +35,9 @@
     ndp, nseq, turns = dims
     nclass = ndp * nseq
     weights, outs = refs[0], refs[1 : 1 + nclass]
-    xbuf, lbuf, sems = refs[1 + nclass :]
+    xbuf, lbuf, table, sems = refs[1 + nclass :]
+    look = pltpu.make_async_copy(pairs, table, sems.at[sems.shape[0] - 1])
+    look.start()
     slots, blk = up.shape[:2]
     toks = x.shape[0]
     rank, ncols = right.shape[0], right.shape[1] // blk
@@ -53,18 +55,22 @@
             moves.append((src.at[s], weights.at[pl.ds((a * slots + s) * blk, blk)]))
     for j in range(ncols):
         moves.append((right.at[:, pl.ds(j * blk, blk)], weights.at[pl.ds(2 * slots * blk + j * rank, rank)]))
+    for n, (src, dst) in enumerate(moves):
+        copies.append(pltpu.make_async_copy(src, dst, sems.at[first + n]))
+    for copy in copies:
+        copy.start()
+    look.wait()
     for (i, j), out in zip(plane(ndp, nseq), outs):
         cls = class_of(d ^ i, c ^ j, ndp)
         for t in range(turns):
             panel = me ^ (cls + t * nclass)
-            for a, src in enumerate((x, dy)):
-                for s in range(slots):
-                    row = ((t * 2 + a) * slots + s) * toks
-                    moves.append((block(src, pairs[s, 0, panel], blk), out.at[pl.ds(row, toks)]))
-    for n, (src, dst) in enumerate(moves):
-        copies.append(pltpu.make_async_copy(src, dst, sems.at[first + n]))
-    for copy in copies:
-        copy.start()
+            for s in range(slots):
+                row = table[s, 0, panel]
+                for a, src in enumerate((x, dy)):
+                    lo = ((t * 2 + a) * slots + s) * toks
+                    copy = pltpu.make_async_copy(block(src, row, blk), out.at[pl.ds(lo, toks)], sems.at[len(copies)])
+                    copy.start()
+                    copies.append(copy)
     for copy in copies[:first]:
         copy.wait()
     factor = dot(lbuf[...], xbuf[...], 1, 1).astype(BF)
@@ -181,6 +187,22 @@
     dx[...] = acc[...].astype(BF)
 
 
+def finish_kernel(nblock, mine, other, left, up, down, right, left_out):
+    slots, rows, blk = up.shape
+    total = mine[...] + other[...].astype(F32)
+    for a, out in ((0, up), (1, down)):
+        for s in range(slots):
+            lo = (a * slots + s) * rows
+            out[s] = total[lo : lo + rows]
+    width = right.shape[1]
+    per = width // blk
+    for r in range(right.shape[0]):
+        for j in range(per):
+            lo = nblock + r * per + j
+            right[r : r + 1, j * blk : (j + 1) * blk] = total[lo : lo + 1]
+    left_out[...] = left[...]
+
+
 def call(name, kernel, spaces, outs, scratch, args, mib, flops):
     with jax.named_scope(name):
         return pl.pallas_call(
@@ -237,10 +259,10 @@
     trows = turns * 2 * slots * toks + rank
     ncopy = 5 + 2 * slots + ncols + nclass * turns * 2 * slots
     weights, *sent = call(
-        "collect", functools.partial(collect_kernel, dims), [SM] + [HBM] * 6,
+        "collect", functools.partial(collect_kernel, dims), [HBM] * 7,
         [((wrows, blk), BF)] + [((trows, blk), BF)] * nclass,
-        [pltpu.VMEM((toks, width), BF), pltpu.VMEM((rank, width), BF), pltpu.SemaphoreType.DMA((ncopy,))],
-        (pairs, *(pltpu.with_memory_space_constraint(v, HBM) for v in (x, dy, left_t, up, down, right_factor))), 16, 10**8,
+        [pltpu.VMEM((toks, width), BF), pltpu.VMEM((rank, width), BF), pltpu.SMEM(pairs.shape, jnp.int32), pltpu.SemaphoreType.DMA((ncopy + 1,))],
+        tuple(pltpu.with_memory_space_constraint(v, HBM) for v in (pairs, x, dy, left_t, up, down, right_factor)), 16, 10**8,
     )
     held = [permute(f"weights{t}", weights, lambda z, d, c, t=t: (z ^ handled(d, c, t), d, c)) for t in range(turns)]
     got = [
@@ -314,10 +336,14 @@
     )
     owned = after(owned, dx)
     leave = pick(owned, 1 - core, 0).astype(BF)
-    total = pick(owned, core, 0) + permute("grads_core", leave, swap).astype(F32)
+    swapped = permute("grads_core", leave, swap)
     nblock = 2 * slots * rows
-    blocks = total[:nblock].reshape(2, 1, slots, rows, blk)
-    return dx[None], blocks[0], blocks[1], left.T, total[nblock:].reshape(rk, pwidth)
+    up_sum, down_sum, right_sum, left_sum = call(
+        "finish", functools.partial(finish_kernel, nblock), [VM] * 3,
+        [((slots, rows, blk), F32)] * 2 + [((rk, pwidth), F32), ((rk, chunk), F32)], [],
+        (pick(owned, core, 0), swapped, left), 4, 10**6,
+    )
+    return dx[None], up_sum[None], down_sum[None], left_sum.T, right_sum
 
 
 def solution(mesh):

time: 55.4 us -> 53.8 us (0.971)
  local copies, waits for them, and re-layouts: 2.24 us -> 0.26 us
  other arithmetic: 0.84 us -> 0.2 us
    slice x2 -> x0, local copies, waits for them, and re-layouts: 0.72 us -> none  [the longest x1 0.72 us: per_device(): blocks[1]]
    unnamed x8, local copies, waits for them, and re-layouts: 0.69 us -> 0.02 us
    reshape x1 -> x0, local copies, waits for them, and re-layouts: 0.62 us -> none  [per_device(): total[nblock:].reshape(rk, pwidth)]
    transpose x1 -> x0, other arithmetic: 0.61 us -> none  [per_device(): return (dx[None], blocks[0], blocks[1], left.T, total[nblock:].reshape(rk...]
    ppermute x15, waiting for transfers between devices: 23.6 us -> 24.1 us  [permute(): lax.ppermute(value, PLANE, [(flat(*spot), flat(*target(*spot))) for spot...]
    pallas_call x4 -> x5, Pallas kernels: 7.42 us -> 7.85 us  [call(): pl.pallas_call(kernel, out_shape=[jax.ShapeDtypeStruct(s, d) for s, d in...]
  transfers between devices with their start and end apart: 15 -> 15, of which waited for: 10 -> 10; matrix products, arithmetic and copies ran while one was open for 2% -> 1% of each run, Pallas kernels for 4% -> 5%
where the time goes in v3:
time: 53.8 us; the launch traced here: 53.6 us
  waiting for transfers between devices  24.1 us (45%)
  starting transfers between devices  20.3 us (38%)
  Pallas kernels  7.85 us (15%)
  between operations  0.84 us (2%)
    ppermute x15, waiting for transfers between devices, permute(): lax.ppermute(value, PLANE, [(flat(*spot), flat(*target(*spot))) for spot...  24.1 us
    ppermute x15, starting transfers between devices, permute(): lax.ppermute(value, PLANE, [(flat(*spot), flat(*target(*spot))) for spot...  20.3 us
    pallas_call x5, Pallas kernels, call(): pl.pallas_call(kernel, out_shape=[jax.ShapeDtypeStruct(s, d) for s, d in...  7.85 us
  transfers between devices with their start and end apart: 15, of which 10 were waited for; matrix products, arithmetic and copies ran while one was open for 1% of the time, Pallas kernels for 5%

profile of v3, /device:TPU:0, one launch (start us, length us, event | category | flops | bytes accessed | tf_op | source)
XLA Modules:
  0.0 53.6 jit_solution(7019577669916382331)
XLA Ops:
  0.6 2.2 %collect.1 = (bf16[1088,256]{1,0:T(8,128)(2,1)S(1)}, bf16[528,256]{1,0:T(8,128)(2,1)S(1)}, bf16[528,256]{1,0:T(8,128)(2,1)S(1)}, bf16[528,256]{1,0:T(8,128)(2,1)S(1)}, bf16[528,256]{1,0:T(8,128)(2,1)S(1)}) custom-call(s32[2,2,4]{2,1,0:T(2,128)} %bitcast.36, bf16[128,4096]{1,0:T(8,128)(2,1)} %bitcast.32, bf16[128,4096]{1,0:T(8,128)(2,1)} %bitcast.41, ...), custom_call_target="tpu_custom_call" | custom-call | flops 100000000 | bytes 1024 | tf_op jit(solution)/shard_map/collect/pallas_call | solution.py:208
  2.9 0.7 %collective-permute-start = (bf16[1088,256]{1,0:T(8,128)(2,1)S(1)}, bf16[1088,256]{1,0:T(8,128)(2,1)S(1)}, u32[]{:S(2)}, u32[]{:S(2)}) collective-permute-start(bf16[1088,256]{1,0:T(8,128)(2,1)S(1)} %get-tuple-element.27), channel_id=1, source_target_pairs={{0,0},{1,13},{2,6},{3,11},{4,4},{5,9},{6,2},{7,15},{8,8},{9,5},{10... | collective-permute-start | bytes 1671176 | tf_op jit(solution)/shard_map/weights0/ppermute | solution.py:227
  3.6 6.0 %collective-permute-start.1 = (bf16[528,256]{1,0:T(8,128)(2,1)S(1)}, bf16[528,256]{1,0:T(8,128)(2,1)S(1)}, u32[]{:S(2)}, u32[]{:S(2)}) collective-permute-start(bf16[528,256]{1,0:T(8,128)(2,1)S(1)} %get-tuple-element.28), channel_id=1, source_target_pairs={{0,3},{1,2},{2,1},{3,0},{4,7},{5,6},{6,5},{7,4},{8,11},{9,10},{10,... | collective-permute-start | bytes 811016 | tf_op jit(solution)/shard_map/tokens11/ppermute | solution.py:227
  9.6 1.5 %collective-permute-start.2 = (bf16[528,256]{1,0:T(8,128)(2,1)S(1)}, bf16[528,256]{1,0:T(8,128)(2,1)S(1)}, u32[]{:S(2)}, u32[]{:S(2)}) collective-permute-start(bf16[528,256]{1,0:T(8,128)(2,1)S(1)} %get-tuple-element.29), channel_id=1, source_target_pairs={{0,2},{1,3},{2,0},{3,1},{4,6},{5,7},{6,4},{7,5},{8,10},{9,11},{10,... | collective-permute-start | bytes 811016 | tf_op jit(solution)/shard_map/tokens10/ppermute | solution.py:227
  11.1 5.3 %collective-permute-done.1.refs_0_ = bf16[528,256]{1,0:T(8,128)(2,1)S(1)} collective-permute-done((bf16[528,256]{1,0:T(8,128)(2,1)S(1)}, bf16[528,256]{1,0:T(8,128)(2,1)S(1)}, u32[]{:S(2)}, u32[]{:S(2)}) %collective-permute-start.1) | collective-permute-done | bytes 270368 | tf_op jit(solution)/shard_map/tokens11/ppermute | solution.py:227
  16.4 6.0 %collective-permute-done.2.refs_1_ = bf16[528,256]{1,0:T(8,128)(2,1)S(1)} collective-permute-done((bf16[528,256]{1,0:T(8,128)(2,1)S(1)}, bf16[528,256]{1,0:T(8,128)(2,1)S(1)}, u32[]{:S(2)}, u32[]{:S(2)}) %collective-permute-start.2) | collective-permute-done | bytes 270368 | tf_op jit(solution)/shard_map/tokens10/ppermute | solution.py:227
  22.4 2.4 %panel0.1 = (bf16[2,2,2,2,64,256]{5,4,3,2,1,0:T(8,128)(2,1)S(1)}, f32[16,1024]{1,0:T(8,128)S(1)}, bf16[2,256,256]{2,1,0:T(8,128)(2,1)S(1)}, bf16[2,256,256]{2,1,...) custom-call(s32[2,2,4]{2,1,0:T(2,128)S(1)} %bitcast.37, s32[4]{0:T(128)S(1)} %copy-done.3, ...), custom_call_target="tpu_custom_call" | custom-call | flops 100000000 | bytes 1024 | tf_op jit(solution)/shard_map/panel0/pallas_call | solution.py:208
  25.4 0.7 %collective-permute-done.4 = f32[2,16,128]{2,1,0:T(8,128)S(1)} collective-permute-done((f32[2,16,128]{2,1,0:T(8,128)S(1)}, f32[2,16,128]{2,1,0:T(8,128)S(1)}, u32[]{:S(2)}, u32[]{:S(2)}) %collective-permute-start.4) | collective-permute-done | bytes 16416 | tf_op jit(solution)/shard_map/gfac_core/ppermute | solution.py:227
  26.1 1.6 %collective-permute-start.5 = (f32[16,128]{1,0:T(8,128)S(1)}, f32[16,128]{1,0:T(8,128)S(1)}, u32[]{:S(2)}, u32[]{:S(2)}) collective-permute-start(f32[16,128]{1,0:T(8,128)S(1)} %slice_bitcast_fusion.2), channel_id=1, source_target_pairs={{0,2},{1,3},{2,0},{3,1},{4,6},{5,7},{6,4},{7,5},{8,10},{9,11},{10,... | collective-permute-start | bytes 24584 | tf_op jit(solution)/shard_map/gfac_dp1/ppermute | solution.py:227
  27.7 2.0 %collective-permute-done.5 = f32[16,128]{1,0:T(8,128)S(1)} collective-permute-done((f32[16,128]{1,0:T(8,128)S(1)}, f32[16,128]{1,0:T(8,128)S(1)}, u32[]{:S(2)}, u32[]{:S(2)}) %collective-permute-start.5) | collective-permute-done | bytes 8224 | tf_op jit(solution)/shard_map/gfac_dp1/ppermute | solution.py:227
  30.2 1.2 %collective-permute-done.7 = f32[2,4,4,1024]{3,2,1,0:T(4,128)S(1)} collective-permute-done((f32[2,4,4,1024]{3,2,1,0:T(4,128)S(1)}, f32[2,4,4,1024]{3,2,1,0:T(4,128)S(1)}, u32[]{:S(2)}, u32[]{:S(2)}) %collective-permute-start.7) | collective-permute-done | bytes 131104 | tf_op jit(solution)/shard_map/left_core/ppermute | solution.py:227
  31.5 1.6 %collective-permute-start.12 = (bf16[4,4,1024]{2,1,0:T(4,128)(2,1)S(1)}, bf16[4,4,1024]{2,1,0:T(4,128)(2,1)S(1)}, u32[]{:S(2)}, u32[]{:S(2)}) collective-permute-start(bf16[4,4,1024]{2,1,0:T(4,128)(2,1)S(1)} %fusion.1), channel_id=1, source_target_pairs={{0,2},{1,3},{2,0},{3,1},{4,6},{5,7},{6,4},{7,5},{8,10},{9,11},{10,... | collective-permute-start | bytes 98312 | tf_op jit(solution)/shard_map/left_dp1/ppermute | solution.py:227
  33.2 0.5 collective-permute-start.10
  33.7 0.7 %collective-permute-start.9 = (bf16[2,272,256]{2,1,0:T(8,128)(2,1)S(1)}, bf16[2,272,256]{2,1,0:T(8,128)(2,1)S(1)}, u32[]{:S(2)}, u32[]{:S(2)}) collective-permute-start(bf16[2,272,256]{2,1,0:T(8,128)(2,1)S(1)} %get-tuple-element.42), channel_id=1, source_target_pairs={{0,0},{1,13},{2,6},{3,11},{4,4},{5,9},{6,2},{7,15},{8,8},{9,5},{10... | collective-permute-start | bytes 835592 | tf_op jit(solution)/shard_map/grads00/ppermute | solution.py:227
  34.3 1.1 %collective-permute-done.12 = bf16[4,4,1024]{2,1,0:T(4,128)(2,1)S(1)} collective-permute-done((bf16[4,4,1024]{2,1,0:T(4,128)(2,1)S(1)}, bf16[4,4,1024]{2,1,0:T(4,128)(2,1)S(1)}, u32[]{:S(2)}, u32[]{:S(2)}) %collective-permute-start.12) | collective-permute-done | bytes 32800 | tf_op jit(solution)/shard_map/left_dp1/ppermute | solution.py:227
  35.5 0.5 %collective-permute-start.13 = (bf16[2,4,1024]{2,1,0:T(4,128)(2,1)S(1)}, bf16[2,4,1024]{2,1,0:T(4,128)(2,1)S(1)}, u32[]{:S(2)}, u32[]{:S(2)}) collective-permute-start(bf16[2,4,1024]{2,1,0:T(4,128)(2,1)S(1)} %slice.62), channel_id=1, source_target_pairs={{0,8},{1,9},{2,10},{3,11},{4,12},{5,13},{6,14},{7,15},{8,0},{9,1},... | collective-permute-start | bytes 49160 | tf_op jit(solution)/shard_map/left_tensor2/ppermute | solution.py:227
  36.1 4.8 %collective-permute-start.8 = (bf16[2,256,256]{2,1,0:T(8,128)(2,1)S(1)}, bf16[2,256,256]{2,1,0:T(8,128)(2,1)S(1)}, u32[]{:S(2)}, u32[]{:S(2)}) collective-permute-start(bf16[2,256,256]{2,1,0:T(8,128)(2,1)S(1)} %pad_maximum_fusion.2), channel_id=1, source_target_pairs={{0,2},{1,3},{2,0},{3,1},{4,6},{5,7},{6,4},{7,5},{8,10},{9,11},{10,... | collective-permute-start | bytes 786440 | tf_op jit(solution)/shard_map/parts_dp01/ppermute | solution.py:227
  41.1 1.2 %collective-permute-start.14 = (bf16[1,4,1024]{2,1,0:T(4,128)(2,1)S(1)}, bf16[1,4,1024]{2,1,0:T(4,128)(2,1)S(1)}, u32[]{:S(2)}, u32[]{:S(2)}) collective-permute-start(bf16[1,4,1024]{2,1,0:T(4,128)(2,1)S(1)} %slice.63), channel_id=1, source_target_pairs={{0,4},{1,5},{2,6},{3,7},{4,0},{5,1},{6,2},{7,3},{8,12},{9,13},{10,... | collective-permute-start | bytes 24584 | tf_op jit(solution)/shard_map/left_tensor1/ppermute | solution.py:227
  42.2 1.0 %collective-permute-done.10 = bf16[2,272,256]{2,1,0:T(8,128)(2,1)S(1)} collective-permute-done((bf16[2,272,256]{2,1,0:T(8,128)(2,1)S(1)}, bf16[2,272,256]{2,1,0:T(8,128)(2,1)S(1)}, u32[]{:S(2)}, u32[]{:S(2)}) %collective-permute-start.10) | collective-permute-done | bytes 278560 | tf_op jit(solution)/shard_map/grads01/ppermute | solution.py:227
  43.3 5.7 %collective-permute-done.8.refs_2_ = bf16[2,256,256]{2,1,0:T(8,128)(2,1)S(1)} collective-permute-done((bf16[2,256,256]{2,1,0:T(8,128)(2,1)S(1)}, bf16[2,256,256]{2,1,0:T(8,128)(2,1)S(1)}, u32[]{:S(2)}, u32[]{:S(2)}) %collective-permute-start.8) | collective-permute-done | bytes 262176 | tf_op jit(solution)/shard_map/parts_dp01/ppermute | solution.py:227
  49.1 2.2 %dx.1 = bf16[128,4096]{1,0:T(8,128)(2,1)} custom-call(s32[2,2,4]{2,1,0:T(2,128)S(1)} %bitcast.38, s32[4]{0:T(128)S(1)} %copy-done.3, bf16[16,4096]{1,0:T(8,128)(2,1)S(1)} %bitcast.35, bf16[16,128]{1,0:T(8,128)(2,1)S(1)} %get-tuple-element.34.gfac, bf16[256,256]{1,0:T(8,128)(2,1)S(1)} %get-tuple-element.52.refs_0_, ...), custom_call_target="tpu_custom_call" | custom-call | flops 100000000 | bytes 1024 | tf_op jit(solution)/shard_map/dx/pallas_call | solution.py:208
  51.3 0.6 %collective-permute-start.11 = (bf16[272,256]{1,0:T(8,128)(2,1)S(1)}, bf16[272,256]{1,0:T(8,128)(2,1)S(1)}, u32[]{:S(2)}, u32[]{:S(2)}) collective-permute-start(bf16[272,256]{1,0:T(8,128)(2,1)S(1)} %fusion), channel_id=1, source_target_pairs={{0,1},{1,0},{2,3},{3,2},{4,5},{5,4},{6,7},{7,6},{8,9},{9,8},{10,11... | collective-permute-start | bytes 417800 | tf_op jit(solution)/shard_map/grads_core/ppermute | solution.py:227
  52.0 0.9 %collective-permute-done.11.other = bf16[272,256]{1,0:T(8,128)(2,1)S(1)} collective-permute-done((bf16[272,256]{1,0:T(8,128)(2,1)S(1)}, bf16[272,256]{1,0:T(8,128)(2,1)S(1)}, u32[]{:S(2)}, u32[]{:S(2)}) %collective-permute-start.11) | collective-permute-done | bytes 139296 | tf_op jit(solution)/shard_map/grads_core/ppermute | solution.py:227
  52.9 0.7 %finish.1 = (f32[2,64,256]{2,1,0:T(8,128)}, f32[2,64,256]{2,1,0:T(8,128)}, f32[4,1024]{1,0:T(4,128)}, f32[4,1024]{1,0:T(4,128)}) custom-call(f32[272,256]{1,0:T(8,128)S(1)} %dynamic-slice_bitcast_fusion.mine, bf16[272,256]{1,0:T(8,128)(2,1)S(1)} %collective-permute-done.11.other, f32[4,1024]{1,0:T(4,128)S(1)} %fusion.2.left), custom_call_target="tpu_custom_call" | custom-call | flops 1000000 | bytes 1024 | tf_op jit(solution)/shard_map/finish/pallas_call | solution.py:208
  (41 shorter events, 1.5 us)
Async XLA Ops:
  2.9 19.5 %collective-permute-start = (bf16[1088,256]{1,0:T(8,128)(2,1)S(1)}, bf16[1088,256]{1,0:T(8,128)(2,1)S(1)}, u32[]{:S(2)}, u32[]{:S(2)}) collective-permute-start(bf16[1088,256]{1,0:T(8,128)(2,1)S(1)} %get-tuple-element.27), channel_id=1, source_target_pairs={{0,0},{1,13},{2,6},{3,11},{4,4},{5,9},{6,2},{7,15},{8,8},{9,5},{10... | collective-permute-start | bytes 1671176 | tf_op jit(solution)/shard_map/weights0/ppermute | solution.py:227
  3.6 12.8 %collective-permute-start.1 = (bf16[528,256]{1,0:T(8,128)(2,1)S(1)}, bf16[528,256]{1,0:T(8,128)(2,1)S(1)}, u32[]{:S(2)}, u32[]{:S(2)}) collective-permute-start(bf16[528,256]{1,0:T(8,128)(2,1)S(1)} %get-tuple-element.28), channel_id=1, source_target_pairs={{0,3},{1,2},{2,1},{3,0},{4,7},{5,6},{6,5},{7,4},{8,11},{9,10},{10,... | collective-permute-start | bytes 811016 | tf_op jit(solution)/shard_map/tokens11/ppermute | solution.py:227
  9.6 12.8 %copy-start.2 = (s32[4,2,2]{0,2,1:T(2,128)S(1)}, s32[4,2,2]{0,2,1:T(2,128)}, u32[]{:S(2)}) copy-start(s32[4,2,2]{0,2,1:T(2,128)} %param.12) | copy-start | bytes 196
  9.6 12.8 %collective-permute-start.2 = (bf16[528,256]{1,0:T(8,128)(2,1)S(1)}, bf16[528,256]{1,0:T(8,128)(2,1)S(1)}, u32[]{:S(2)}, u32[]{:S(2)}) collective-permute-start(bf16[528,256]{1,0:T(8,128)(2,1)S(1)} %get-tuple-element.29), channel_id=1, source_target_pairs={{0,2},{1,3},{2,0},{3,1},{4,6},{5,7},{6,4},{7,5},{8,10},{9,11},{10,... | collective-permute-start | bytes 811016 | tf_op jit(solution)/shard_map/tokens10/ppermute | solution.py:227
  11.1 11.3 %copy-start.3 = (s32[4]{0:T(128)S(1)}, s32[4]{0:T(128)}, u32[]{:S(2)}) copy-start(s32[4]{0:T(128)} %live.3) | copy-start | bytes 52
  11.1 11.3 %collective-permute-start.3 = (bf16[528,256]{1,0:T(8,128)(2,1)S(1)}, bf16[528,256]{1,0:T(8,128)(2,1)S(1)}, u32[]{:S(2)}, u32[]{:S(2)}) collective-permute-start(bf16[528,256]{1,0:T(8,128)(2,1)S(1)} %get-tuple-element.30), channel_id=1, source_target_pairs={{0,1},{1,0},{2,3},{3,2},{4,5},{5,4},{6,7},{7,6},{8,9},{9,8},{10,11... | collective-permute-start | bytes 811016 | tf_op jit(solution)/shard_map/tokens01/ppermute | solution.py:227
  22.4 7.3 %copy-start = (bf16[1,128,4096]{2,1,0:T(8,128)(2,1)S(1)}, bf16[1,128,4096]{2,1,0:T(8,128)(2,1)}, u32[]{:S(2)}) copy-start(bf16[1,128,4096]{2,1,0:T(8,128)(2,1)} %param.8) | copy-start | bytes 3145732
  24.8 1.2 %collective-permute-start.4 = (f32[2,16,128]{2,1,0:T(8,128)S(1)}, f32[2,16,128]{2,1,0:T(8,128)S(1)}, u32[]{:S(2)}, u32[]{:S(2)}) collective-permute-start(f32[2,16,128]{2,1,0:T(8,128)S(1)} %get-tuple-element.33), channel_id=1, source_target_pairs={{0,1},{1,0},{2,3},{3,2},{4,5},{5,4},{6,7},{7,6},{8,9},{9,8},{10,11... | collective-permute-start | bytes 49160 | tf_op jit(solution)/shard_map/gfac_core/ppermute | solution.py:227
  24.9 11.1 %collective-permute-start.6 = (bf16[2,256,256]{2,1,0:T(8,128)(2,1)S(1)}, bf16[2,256,256]{2,1,0:T(8,128)(2,1)S(1)}, u32[]{:S(2)}, u32[]{:S(2)}) collective-permute-start(bf16[2,256,256]{2,1,0:T(8,128)(2,1)S(1)} %get-tuple-element.36), channel_id=1, source_target_pairs={{0,1},{1,0},{2,3},{3,2},{4,5},{5,4},{6,7},{7,6},{8,9},{9,8},{10,11... | collective-permute-start | bytes 786440 | tf_op jit(solution)/shard_map/parts_core0/ppermute | solution.py:227
  26.1 3.7 %collective-permute-start.5 = (f32[16,128]{1,0:T(8,128)S(1)}, f32[16,128]{1,0:T(8,128)S(1)}, u32[]{:S(2)}, u32[]{:S(2)}) collective-permute-start(f32[16,128]{1,0:T(8,128)S(1)} %slice_bitcast_fusion.2), channel_id=1, source_target_pairs={{0,2},{1,3},{2,0},{3,1},{4,6},{5,7},{6,4},{7,5},{8,10},{9,11},{10,... | collective-permute-start | bytes 24584 | tf_op jit(solution)/shard_map/gfac_dp1/ppermute | solution.py:227
  30.0 1.4 %collective-permute-start.7 = (f32[2,4,4,1024]{3,2,1,0:T(4,128)S(1)}, f32[2,4,4,1024]{3,2,1,0:T(4,128)S(1)}, u32[]{:S(2)}, u32[]{:S(2)}) collective-permute-start(f32[2,4,4,1024]{3,2,1,0:T(4,128)S(1)} %get-tuple-element.38), channel_id=1, source_target_pairs={{0,1},{1,0},{2,3},{3,2},{4,5},{5,4},{6,7},{7,6},{8,9},{9,8},{10,11... | collective-permute-start | bytes 393224 | tf_op jit(solution)/shard_map/left_core/ppermute | solution.py:227
  31.5 4.0 %collective-permute-start.12 = (bf16[4,4,1024]{2,1,0:T(4,128)(2,1)S(1)}, bf16[4,4,1024]{2,1,0:T(4,128)(2,1)S(1)}, u32[]{:S(2)}, u32[]{:S(2)}) collective-permute-start(bf16[4,4,1024]{2,1,0:T(4,128)(2,1)S(1)} %fusion.1), channel_id=1, source_target_pairs={{0,2},{1,3},{2,0},{3,1},{4,6},{5,7},{6,4},{7,5},{8,10},{9,11},{10,... | collective-permute-start | bytes 98312 | tf_op jit(solution)/shard_map/left_dp1/ppermute | solution.py:227
  33.2 10.1 %collective-permute-start.10 = (bf16[2,272,256]{2,1,0:T(8,128)(2,1)S(1)}, bf16[2,272,256]{2,1,0:T(8,128)(2,1)S(1)}, u32[]{:S(2)}, u32[]{:S(2)}) collective-permute-start(bf16[2,272,256]{2,1,0:T(8,128)(2,1)S(1)} %get-tuple-element.43), channel_id=1, source_target_pairs={{0,2},{1,15},{2,4},{3,9},{4,6},{5,11},{6,0},{7,13},{8,10},{9,7},{1... | collective-permute-start | bytes 835592 | tf_op jit(solution)/shard_map/grads01/ppermute | solution.py:227
  33.7 9.6 %collective-permute-start.9 = (bf16[2,272,256]{2,1,0:T(8,128)(2,1)S(1)}, bf16[2,272,256]{2,1,0:T(8,128)(2,1)S(1)}, u32[]{:S(2)}, u32[]{:S(2)}) collective-permute-start(bf16[2,272,256]{2,1,0:T(8,128)(2,1)S(1)} %get-tuple-element.42), channel_id=1, source_target_pairs={{0,0},{1,13},{2,6},{3,11},{4,4},{5,9},{6,2},{7,15},{8,8},{9,5},{10... | collective-permute-start | bytes 835592 | tf_op jit(solution)/shard_map/grads00/ppermute | solution.py:227
  35.5 5.5 %collective-permute-start.13 = (bf16[2,4,1024]{2,1,0:T(4,128)(2,1)S(1)}, bf16[2,4,1024]{2,1,0:T(4,128)(2,1)S(1)}, u32[]{:S(2)}, u32[]{:S(2)}) collective-permute-start(bf16[2,4,1024]{2,1,0:T(4,128)(2,1)S(1)} %slice.62), channel_id=1, source_target_pairs={{0,8},{1,9},{2,10},{3,11},{4,12},{5,13},{6,14},{7,15},{8,0},{9,1},... | collective-permute-start | bytes 49160 | tf_op jit(solution)/shard_map/left_tensor2/ppermute | solution.py:227
  36.1 13.0 %collective-permute-start.8 = (bf16[2,256,256]{2,1,0:T(8,128)(2,1)S(1)}, bf16[2,256,256]{2,1,0:T(8,128)(2,1)S(1)}, u32[]{:S(2)}, u32[]{:S(2)}) collective-permute-start(bf16[2,256,256]{2,1,0:T(8,128)(2,1)S(1)} %pad_maximum_fusion.2), channel_id=1, source_target_pairs={{0,2},{1,3},{2,0},{3,1},{4,6},{5,7},{6,4},{7,5},{8,10},{9,11},{10,... | collective-permute-start | bytes 786440 | tf_op jit(solution)/shard_map/parts_dp01/ppermute | solution.py:227
  41.1 8.0 %copy-start.1 = (bf16[4096,16]{0,1:T(8,128)(2,1)S(1)}, bf16[4096,16]{0,1:T(8,128)(2,1)}, u32[]{:S(2)}) copy-start(bf16[4096,16]{0,1:T(8,128)(2,1)} %param.14) | copy-start | bytes 393220
  41.1 10.8 %collective-permute-start.14 = (bf16[1,4,1024]{2,1,0:T(4,128)(2,1)S(1)}, bf16[1,4,1024]{2,1,0:T(4,128)(2,1)S(1)}, u32[]{:S(2)}, u32[]{:S(2)}) collective-permute-start(bf16[1,4,1024]{2,1,0:T(4,128)(2,1)S(1)} %slice.63), channel_id=1, source_target_pairs={{0,4},{1,5},{2,6},{3,7},{4,0},{5,1},{6,2},{7,3},{8,12},{9,13},{10,... | collective-permute-start | bytes 24584 | tf_op jit(solution)/shard_map/left_tensor1/ppermute | solution.py:227
  51.3 1.6 %collective-permute-start.11 = (bf16[272,256]{1,0:T(8,128)(2,1)S(1)}, bf16[272,256]{1,0:T(8,128)(2,1)S(1)}, u32[]{:S(2)}, u32[]{:S(2)}) collective-permute-start(bf16[272,256]{1,0:T(8,128)(2,1)S(1)} %fusion), channel_id=1, source_target_pairs={{0,1},{1,0},{2,3},{3,2},{4,5},{5,4},{6,7},{7,6},{8,9},{9,8},{10,11... | collective-permute-start | bytes 417800 | tf_op jit(solution)/shard_map/grads_core/ppermute | solution.py:227

commit v4 on v3

--- a/solution.py
+++ b/solution.py
@@ -86,10 +86,10 @@
     ndp, nseq, turns = dims
     nclass = ndp * nseq
     tokens, refs = refs[:nclass], refs[nclass:]
-    grads, rgrad = refs[:2]
-    parts, gfacs, (xcol, dycol, fact) = refs[2 : 2 + nseq], refs[2 + nseq : 2 + 2 * nseq], refs[2 + 2 * nseq :]
-    slots, rows, blk = grads.shape[3:]
-    rank = rgrad.shape[0]
+    xcol, dycol, fact, hidden, dhidden = refs[:5]
+    parts, gfacs = refs[5 : 5 + nseq], refs[5 + nseq :]
+    slots, _, blk = xcol.shape
+    rank = fact.shape[0]
     toks = fact.shape[1] // nclass
     me, d, c = (lax.axis_index(a) for a in PLANE)
     panel = me ^ (class_of(d, c, ndp) + turn * nclass)
@@ -107,7 +107,6 @@
     right = [weights[pl.ds(pl.multiple_of(2 * slots * blk + c_ * rank, rank), rank)] for c_ in cols]
     block_up = [dot(xcol[s], up[s], 1, 0) for s in range(slots)]
     block_down = [dot(dycol[s], down[s], 1, 1) for s in range(slots)]
-    rgrad[...] = jnp.zeros(rgrad.shape, F32)
     gsum = None
     for s in range(slots):
         pre = dot(fact[...], right[s], 0, 0)
@@ -121,24 +120,38 @@
                 single = jnp.logical_and(single, jnp.logical_not(same))
         act = pre.astype(BF).astype(F32)
         sig = jax.nn.sigmoid(act)
-        hid = (act * sig).astype(BF)
+        hidden[s] = (act * sig).astype(BF)
         dpre = (dh * (sig * (1.0 + act * (1.0 - sig)))).astype(BF)
-        once = jnp.where(single, dpre, jnp.zeros_like(dpre))
-        term = dot(right[s], once, 1, 1)
+        dhidden[s] = dpre
+        term = jnp.where(single, dot(right[s], dpre, 1, 1), 0.0)
         gsum = term if gsum is None else gsum + term
-        where = pl.ds(pl.multiple_of(cols[s] * blk, blk), blk)
-        rgrad[:, where] = rgrad[:, where] + dot(fact[...], once, 1, 0)
         part = jnp.where(alive[s], dot(dpre, up[s], 1, 1), 0.0).astype(BF)
         for n, (i, j) in enumerate(plane(ndp, nseq)):
             parts[j][i, s * toks : (s + 1) * toks] = part[n * toks : (n + 1) * toks]
-        gup = jnp.where(alive[s], dot(xcol[s], dpre, 0, 0), 0.0).astype(BF)
-        gdown = jnp.where(alive[s], dot(hid, dycol[s], 0, 0), 0.0).astype(BF)
+    for n, (i, j) in enumerate(plane(ndp, nseq)):
+        gfacs[j][i] = gsum[:, n * toks : (n + 1) * toks]
+
+
+def grads_kernel(dims, turn, pairs, live, xcol, dycol, fact, hidden, dhidden, grads, rgrad):
+    ndp, nseq, turns = dims
+    slots, rows, blk = grads.shape[3:]
+    me, d, c = (lax.axis_index(a) for a in PLANE)
+    panel = me ^ (class_of(d, c, ndp) + turn * ndp * nseq)
+    cols = [pairs[s, 1, panel] for s in range(slots)]
+    alive = [s < live[panel] for s in range(slots)]
+    rgrad[...] = jnp.zeros(rgrad.shape, F32)
+    for s in range(slots):
+        single = alive[s]
+        for t in range(s):
+            single = jnp.logical_and(single, jnp.logical_not(jnp.logical_and(cols[t] == cols[s], alive[t])))
+        where = pl.ds(pl.multiple_of(cols[s] * blk, blk), blk)
+        rgrad[:, where] = rgrad[:, where] + jnp.where(single, dot(fact[...], dhidden[s], 1, 0), 0.0)
+        gup = jnp.where(alive[s], dot(xcol[s], dhidden[s], 0, 0), 0.0).astype(BF)
+        gdown = jnp.where(alive[s], dot(hidden[s], dycol[s], 0, 0), 0.0).astype(BF)
         for a, grad in ((0, gup), (1, gdown)):
             for i, j in itertools.product(range(ndp), range(nseq)):
                 lo = (i * nseq + j) * rows
                 grads[i, j, a, s] = grad[lo : lo + rows]
-    for n, (i, j) in enumerate(plane(ndp, nseq)):
-        gfacs[j][i] = gsum[:, n * toks : (n + 1) * toks]
 
 
 def split_seq(value, ndp, nseq, here):
@@ -271,17 +284,20 @@
     ]
     grads, rights, parts, gfacs = [], [], [], []
     for t in range(turns):
-        grad, right, *rest = call(
+        states = [((slots, nclass * toks, blk), BF)] * 2 + [((rank, nclass * toks), BF)] + [((slots, nclass * toks, blk), BF)] * 2
+        *state, p0, p1, g0, g1 = call(
             f"panel{t}", functools.partial(panel_kernel, dims, t), [SM] * 2 + [VM] * (1 + nclass),
-            [((ndp, nseq, 2, slots, rows, blk), BF), ((rank, pwidth), F32)]
-            + [((ndp, slots * toks, blk), BF)] * nseq + [((ndp, rank, toks), F32)] * nseq,
-            [pltpu.VMEM((slots, nclass * toks, blk), BF)] * 2 + [pltpu.VMEM((rank, nclass * toks), BF)],
+            states + [((ndp, slots * toks, blk), BF)] * nseq + [((ndp, rank, toks), F32)] * nseq, [],
             (pairs, live, held[t], *got), 16, 10**8,
+        )
+        grad, right = call(
+            f"grads{t}", functools.partial(grads_kernel, dims, t), [SM] * 2 + [VM] * 5,
+            [((ndp, nseq, 2, slots, rows, blk), BF), ((rank, pwidth), F32)], [], (pairs, live, *state), 16, 10**8,
         )
         grads.append(grad)
         rights.append(right)
-        parts.append(rest[:nseq])
-        gfacs.append(rest[nseq:])
+        parts.append((p0, p1))
+        gfacs.append((g0, g1))
 
     swap = lambda z, d, c: (z, d, c ^ 1)
 

time: 53.8 us -> 53.4 us (level)
  waiting for transfers between devices: 24.1 us -> 23 us
  Pallas kernels: 7.85 us -> 8.51 us
    ppermute x15, waiting for transfers between devices: 24.1 us -> 23 us  [permute(): lax.ppermute(value, PLANE, [(flat(*spot), flat(*target(*spot))) for spot...]
    pallas_call x5 -> x6, Pallas kernels: 7.85 us -> 8.51 us  [call(): pl.pallas_call(kernel, out_shape=[jax.ShapeDtypeStruct(s, d) for s, d in...]
  transfers between devices with their start and end apart: 15 -> 15, of which waited for: 10 -> 10; matrix products, arithmetic and copies ran while one was open for 1% -> 1% of each run, Pallas kernels for 5% -> 7%
where the time goes in v4:
time: 53.4 us; the launch traced here: 53.2 us
  waiting for transfers between devices  23 us (43%)
  starting transfers between devices  20.4 us (38%)
  Pallas kernels  8.51 us (16%)
  between operations  0.83 us (2%)
    ppermute x15, waiting for transfers between devices, permute(): lax.ppermute(value, PLANE, [(flat(*spot), flat(*target(*spot))) for spot...  23 us
    ppermute x15, starting transfers between devices, permute(): lax.ppermute(value, PLANE, [(flat(*spot), flat(*target(*spot))) for spot...  20.4 us
    pallas_call x6, Pallas kernels, call(): pl.pallas_call(kernel, out_shape=[jax.ShapeDtypeStruct(s, d) for s, d in...  8.51 us
  transfers between devices with their start and end apart: 15, of which 10 were waited for; matrix products, arithmetic and copies ran while one was open for 1% of the time, Pallas kernels for 7%

profile of v4, /device:TPU:0, one launch (start us, length us, event | category | flops | bytes accessed | tf_op | source)
XLA Modules:
  0.0 53.2 jit_solution(305443626333425097)
XLA Ops:
  0.6 2.2 %collect.1 = (bf16[1088,256]{1,0:T(8,128)(2,1)S(1)}, bf16[528,256]{1,0:T(8,128)(2,1)S(1)}, bf16[528,256]{1,0:T(8,128)(2,1)S(1)}, bf16[528,256]{1,0:T(8,128)(2,1)S(1)}, bf16[528,256]{1,0:T(8,128)(2,1)S(1)}) custom-call(s32[2,2,4]{2,1,0:T(2,128)} %bitcast.36, bf16[128,4096]{1,0:T(8,128)(2,1)} %bitcast.32, bf16[128,4096]{1,0:T(8,128)(2,1)} %bitcast.42, ...), custom_call_target="tpu_custom_call" | custom-call | flops 100000000 | bytes 1024 | tf_op jit(solution)/shard_map/collect/pallas_call | solution.py:221
  2.9 0.7 %collective-permute-start = (bf16[1088,256]{1,0:T(8,128)(2,1)S(1)}, bf16[1088,256]{1,0:T(8,128)(2,1)S(1)}, u32[]{:S(2)}, u32[]{:S(2)}) collective-permute-start(bf16[1088,256]{1,0:T(8,128)(2,1)S(1)} %get-tuple-element.32), channel_id=1, source_target_pairs={{0,0},{1,13},{2,6},{3,11},{4,4},{5,9},{6,2},{7,15},{8,8},{9,5},{10... | collective-permute-start | bytes 1671176 | tf_op jit(solution)/shard_map/weights0/ppermute | solution.py:240
  3.6 6.0 %collective-permute-start.1 = (bf16[528,256]{1,0:T(8,128)(2,1)S(1)}, bf16[528,256]{1,0:T(8,128)(2,1)S(1)}, u32[]{:S(2)}, u32[]{:S(2)}) collective-permute-start(bf16[528,256]{1,0:T(8,128)(2,1)S(1)} %get-tuple-element.33), channel_id=1, source_target_pairs={{0,3},{1,2},{2,1},{3,0},{4,7},{5,6},{6,5},{7,4},{8,11},{9,10},{10,... | collective-permute-start | bytes 811016 | tf_op jit(solution)/shard_map/tokens11/ppermute | solution.py:240
  9.6 1.5 %collective-permute-start.2 = (bf16[528,256]{1,0:T(8,128)(2,1)S(1)}, bf16[528,256]{1,0:T(8,128)(2,1)S(1)}, u32[]{:S(2)}, u32[]{:S(2)}) collective-permute-start(bf16[528,256]{1,0:T(8,128)(2,1)S(1)} %get-tuple-element.34), channel_id=1, source_target_pairs={{0,2},{1,3},{2,0},{3,1},{4,6},{5,7},{6,4},{7,5},{8,10},{9,11},{10,... | collective-permute-start | bytes 811016 | tf_op jit(solution)/shard_map/tokens10/ppermute | solution.py:240
  11.1 5.3 %collective-permute-done.1.refs_0_ = bf16[528,256]{1,0:T(8,128)(2,1)S(1)} collective-permute-done((bf16[528,256]{1,0:T(8,128)(2,1)S(1)}, bf16[528,256]{1,0:T(8,128)(2,1)S(1)}, u32[]{:S(2)}, u32[]{:S(2)}) %collective-permute-start.1) | collective-permute-done | bytes 270368 | tf_op jit(solution)/shard_map/tokens11/ppermute | solution.py:240
  16.4 6.0 %collective-permute-done.2.refs_1_ = bf16[528,256]{1,0:T(8,128)(2,1)S(1)} collective-permute-done((bf16[528,256]{1,0:T(8,128)(2,1)S(1)}, bf16[528,256]{1,0:T(8,128)(2,1)S(1)}, u32[]{:S(2)}, u32[]{:S(2)}) %collective-permute-start.2) | collective-permute-done | bytes 270368 | tf_op jit(solution)/shard_map/tokens10/ppermute | solution.py:240
  22.4 2.0 %panel0.1 = (bf16[2,512,256]{2,1,0:T(8,128)(2,1)S(1)}, bf16[2,512,256]{2,1,0:T(8,128)(2,1)S(1)}, bf16[16,512]{1,0:T(8,128)(2,1)S(1)}, bf16[2,512,256]{2,1,0:T(8,...) custom-call(s32[2,2,4]{2,1,0:T(2,128)S(1)} %bitcast.37, ...), custom_call_target="tpu_custom_call" | custom-call | flops 100000000 | bytes 1024 | tf_op jit(solution)/shard_map/panel0/pallas_call | solution.py:221
  25.0 0.7 %collective-permute-done.4 = f32[2,16,128]{2,1,0:T(8,128)S(1)} collective-permute-done((f32[2,16,128]{2,1,0:T(8,128)S(1)}, f32[2,16,128]{2,1,0:T(8,128)S(1)}, u32[]{:S(2)}, u32[]{:S(2)}) %collective-permute-start.4) | collective-permute-done | bytes 16416 | tf_op jit(solution)/shard_map/gfac_core/ppermute | solution.py:240
  25.7 1.6 %collective-permute-start.5 = (f32[16,128]{1,0:T(8,128)S(1)}, f32[16,128]{1,0:T(8,128)S(1)}, u32[]{:S(2)}, u32[]{:S(2)}) collective-permute-start(f32[16,128]{1,0:T(8,128)S(1)} %slice_bitcast_fusion.2), channel_id=1, source_target_pairs={{0,2},{1,3},{2,0},{3,1},{4,6},{5,7},{6,4},{7,5},{8,10},{9,11},{10,... | collective-permute-start | bytes 24584 | tf_op jit(solution)/shard_map/gfac_dp1/ppermute | solution.py:240
  27.2 1.1 %grads0.1 = (bf16[2,2,2,2,64,256]{5,4,3,2,1,0:T(8,128)(2,1)S(1)}, f32[16,1024]{1,0:T(8,128)S(1)}) custom-call(s32[2,2,4]{2,1,0:T(2,128)S(1)} %bitcast.38, s32[4]{0:T(128)S(1)} %copy-done.3, bf16[2,512,256]{2,1,0:T(8,128)(2,1)S(1)} %get-tuple-element.45.xcol, bf16[2,512,256]{2,1,0:T(8,128)(2,1)S(1)} %get-tuple-element.46.dycol, ...), custom_call_target="tpu_custom_call" | custom-call | flops 100000000 | bytes 1024 | tf_op jit(solution)/shard_map/grads0/pallas_call | solution.py:221
  28.4 1.0 %collective-permute-done.5 = f32[16,128]{1,0:T(8,128)S(1)} collective-permute-done((f32[16,128]{1,0:T(8,128)S(1)}, f32[16,128]{1,0:T(8,128)S(1)}, u32[]{:S(2)}, u32[]{:S(2)}) %collective-permute-start.5) | collective-permute-done | bytes 8224 | tf_op jit(solution)/shard_map/gfac_dp1/ppermute | solution.py:240
  29.8 1.2 %collective-permute-done.7 = f32[2,4,4,1024]{3,2,1,0:T(4,128)S(1)} collective-permute-done((f32[2,4,4,1024]{3,2,1,0:T(4,128)S(1)}, f32[2,4,4,1024]{3,2,1,0:T(4,128)S(1)}, u32[]{:S(2)}, u32[]{:S(2)}) %collective-permute-start.7) | collective-permute-done | bytes 131104 | tf_op jit(solution)/shard_map/left_core/ppermute | solution.py:240
  31.1 1.6 %collective-permute-start.12 = (bf16[4,4,1024]{2,1,0:T(4,128)(2,1)S(1)}, bf16[4,4,1024]{2,1,0:T(4,128)(2,1)S(1)}, u32[]{:S(2)}, u32[]{:S(2)}) collective-permute-start(bf16[4,4,1024]{2,1,0:T(4,128)(2,1)S(1)} %fusion.1), channel_id=1, source_target_pairs={{0,2},{1,3},{2,0},{3,1},{4,6},{5,7},{6,4},{7,5},{8,10},{9,11},{10,... | collective-permute-start | bytes 98312 | tf_op jit(solution)/shard_map/left_dp1/ppermute | solution.py:240
  33.2 0.7 %collective-permute-start.9 = (bf16[2,272,256]{2,1,0:T(8,128)(2,1)S(1)}, bf16[2,272,256]{2,1,0:T(8,128)(2,1)S(1)}, u32[]{:S(2)}, u32[]{:S(2)}) collective-permute-start(bf16[2,272,256]{2,1,0:T(8,128)(2,1)S(1)} %get-tuple-element.52), channel_id=1, source_target_pairs={{0,0},{1,13},{2,6},{3,11},{4,4},{5,9},{6,2},{7,15},{8,8},{9,5},{10... | collective-permute-start | bytes 835592 | tf_op jit(solution)/shard_map/grads00/ppermute | solution.py:240
  33.9 1.1 %collective-permute-done.12 = bf16[4,4,1024]{2,1,0:T(4,128)(2,1)S(1)} collective-permute-done((bf16[4,4,1024]{2,1,0:T(4,128)(2,1)S(1)}, bf16[4,4,1024]{2,1,0:T(4,128)(2,1)S(1)}, u32[]{:S(2)}, u32[]{:S(2)}) %collective-permute-start.12) | collective-permute-done | bytes 32800 | tf_op jit(solution)/shard_map/left_dp1/ppermute | solution.py:240
  35.1 0.6 %collective-permute-start.13 = (bf16[2,4,1024]{2,1,0:T(4,128)(2,1)S(1)}, bf16[2,4,1024]{2,1,0:T(4,128)(2,1)S(1)}, u32[]{:S(2)}, u32[]{:S(2)}) collective-permute-start(bf16[2,4,1024]{2,1,0:T(4,128)(2,1)S(1)} %slice.62), channel_id=1, source_target_pairs={{0,8},{1,9},{2,10},{3,11},{4,12},{5,13},{6,14},{7,15},{8,0},{9,1},... | collective-permute-start | bytes 49160 | tf_op jit(solution)/shard_map/left_tensor2/ppermute | solution.py:240
  35.7 4.8 %collective-permute-start.8 = (bf16[2,256,256]{2,1,0:T(8,128)(2,1)S(1)}, bf16[2,256,256]{2,1,0:T(8,128)(2,1)S(1)}, u32[]{:S(2)}, u32[]{:S(2)}) collective-permute-start(bf16[2,256,256]{2,1,0:T(8,128)(2,1)S(1)} %pad_maximum_fusion.2), channel_id=1, source_target_pairs={{0,2},{1,3},{2,0},{3,1},{4,6},{5,7},{6,4},{7,5},{8,10},{9,11},{10,... | collective-permute-start | bytes 786440 | tf_op jit(solution)/shard_map/parts_dp01/ppermute | solution.py:240
  40.6 1.2 %collective-permute-start.14 = (bf16[1,4,1024]{2,1,0:T(4,128)(2,1)S(1)}, bf16[1,4,1024]{2,1,0:T(4,128)(2,1)S(1)}, u32[]{:S(2)}, u32[]{:S(2)}) collective-permute-start(bf16[1,4,1024]{2,1,0:T(4,128)(2,1)S(1)} %slice.63), channel_id=1, source_target_pairs={{0,4},{1,5},{2,6},{3,7},{4,0},{5,1},{6,2},{7,3},{8,12},{9,13},{10,... | collective-permute-start | bytes 24584 | tf_op jit(solution)/shard_map/left_tensor1/ppermute | solution.py:240
  41.8 1.0 %collective-permute-done.10 = bf16[2,272,256]{2,1,0:T(8,128)(2,1)S(1)} collective-permute-done((bf16[2,272,256]{2,1,0:T(8,128)(2,1)S(1)}, bf16[2,272,256]{2,1,0:T(8,128)(2,1)S(1)}, u32[]{:S(2)}, u32[]{:S(2)}) %collective-permute-start.10) | collective-permute-done | bytes 278560 | tf_op jit(solution)/shard_map/grads01/ppermute | solution.py:240
  42.9 5.7 %collective-permute-done.8.refs_2_ = bf16[2,256,256]{2,1,0:T(8,128)(2,1)S(1)} collective-permute-done((bf16[2,256,256]{2,1,0:T(8,128)(2,1)S(1)}, bf16[2,256,256]{2,1,0:T(8,128)(2,1)S(1)}, u32[]{:S(2)}, u32[]{:S(2)}) %collective-permute-start.8) | collective-permute-done | bytes 262176 | tf_op jit(solution)/shard_map/parts_dp01/ppermute | solution.py:240
  48.6 2.2 %dx.1 = bf16[128,4096]{1,0:T(8,128)(2,1)} custom-call(s32[2,2,4]{2,1,0:T(2,128)S(1)} %bitcast.39, s32[4]{0:T(128)S(1)} %copy-done.3, bf16[16,4096]{1,0:T(8,128)(2,1)S(1)} %bitcast.35, bf16[16,128]{1,0:T(8,128)(2,1)S(1)} %get-tuple-element.39.gfac, bf16[256,256]{1,0:T(8,128)(2,1)S(1)} %get-tuple-element.62.refs_0_, ...), custom_call_target="tpu_custom_call" | custom-call | flops 100000000 | bytes 1024 | tf_op jit(solution)/shard_map/dx/pallas_call | solution.py:221
  50.9 0.6 %collective-permute-start.11 = (bf16[272,256]{1,0:T(8,128)(2,1)S(1)}, bf16[272,256]{1,0:T(8,128)(2,1)S(1)}, u32[]{:S(2)}, u32[]{:S(2)}) collective-permute-start(bf16[272,256]{1,0:T(8,128)(2,1)S(1)} %fusion), channel_id=1, source_target_pairs={{0,1},{1,0},{2,3},{3,2},{4,5},{5,4},{6,7},{7,6},{8,9},{9,8},{10,11... | collective-permute-start | bytes 417800 | tf_op jit(solution)/shard_map/grads_core/ppermute | solution.py:240
  51.5 0.9 %collective-permute-done.11.other = bf16[272,256]{1,0:T(8,128)(2,1)S(1)} collective-permute-done((bf16[272,256]{1,0:T(8,128)(2,1)S(1)}, bf16[272,256]{1,0:T(8,128)(2,1)S(1)}, u32[]{:S(2)}, u32[]{:S(2)}) %collective-permute-start.11) | collective-permute-done | bytes 139296 | tf_op jit(solution)/shard_map/grads_core/ppermute | solution.py:240
  52.5 0.7 %finish.1 = (f32[2,64,256]{2,1,0:T(8,128)}, f32[2,64,256]{2,1,0:T(8,128)}, f32[4,1024]{1,0:T(4,128)}, f32[4,1024]{1,0:T(4,128)}) custom-call(f32[272,256]{1,0:T(8,128)S(1)} %dynamic-slice_bitcast_fusion.mine, bf16[272,256]{1,0:T(8,128)(2,1)S(1)} %collective-permute-done.11.other, f32[4,1024]{1,0:T(4,128)S(1)} %fusion.2.left), custom_call_target="tpu_custom_call" | custom-call | flops 1000000 | bytes 1024 | tf_op jit(solution)/shard_map/finish/pallas_call | solution.py:221
  (42 shorter events, 2.0 us)
Async XLA Ops:
  2.9 19.5 %collective-permute-start = (bf16[1088,256]{1,0:T(8,128)(2,1)S(1)}, bf16[1088,256]{1,0:T(8,128)(2,1)S(1)}, u32[]{:S(2)}, u32[]{:S(2)}) collective-permute-start(bf16[1088,256]{1,0:T(8,128)(2,1)S(1)} %get-tuple-element.32), channel_id=1, source_target_pairs={{0,0},{1,13},{2,6},{3,11},{4,4},{5,9},{6,2},{7,15},{8,8},{9,5},{10... | collective-permute-start | bytes 1671176 | tf_op jit(solution)/shard_map/weights0/ppermute | solution.py:240
  3.6 12.8 %collective-permute-start.1 = (bf16[528,256]{1,0:T(8,128)(2,1)S(1)}, bf16[528,256]{1,0:T(8,128)(2,1)S(1)}, u32[]{:S(2)}, u32[]{:S(2)}) collective-permute-start(bf16[528,256]{1,0:T(8,128)(2,1)S(1)} %get-tuple-element.33), channel_id=1, source_target_pairs={{0,3},{1,2},{2,1},{3,0},{4,7},{5,6},{6,5},{7,4},{8,11},{9,10},{10,... | collective-permute-start | bytes 811016 | tf_op jit(solution)/shard_map/tokens11/ppermute | solution.py:240
  9.6 12.8 %collective-permute-start.2 = (bf16[528,256]{1,0:T(8,128)(2,1)S(1)}, bf16[528,256]{1,0:T(8,128)(2,1)S(1)}, u32[]{:S(2)}, u32[]{:S(2)}) collective-permute-start(bf16[528,256]{1,0:T(8,128)(2,1)S(1)} %get-tuple-element.34), channel_id=1, source_target_pairs={{0,2},{1,3},{2,0},{3,1},{4,6},{5,7},{6,4},{7,5},{8,10},{9,11},{10,... | collective-permute-start | bytes 811016 | tf_op jit(solution)/shard_map/tokens10/ppermute | solution.py:240
  11.1 11.3 %collective-permute-start.3 = (bf16[528,256]{1,0:T(8,128)(2,1)S(1)}, bf16[528,256]{1,0:T(8,128)(2,1)S(1)}, u32[]{:S(2)}, u32[]{:S(2)}) collective-permute-start(bf16[528,256]{1,0:T(8,128)(2,1)S(1)} %get-tuple-element.35), channel_id=1, source_target_pairs={{0,1},{1,0},{2,3},{3,2},{4,5},{5,4},{6,7},{7,6},{8,9},{9,8},{10,11... | collective-permute-start | bytes 811016 | tf_op jit(solution)/shard_map/tokens01/ppermute | solution.py:240
  11.1 11.3 %copy-start.2 = (s32[4,2,2]{0,2,1:T(2,128)S(1)}, s32[4,2,2]{0,2,1:T(2,128)}, u32[]{:S(2)}) copy-start(s32[4,2,2]{0,2,1:T(2,128)} %param.12) | copy-start | bytes 196
  11.1 11.3 %copy-start.3 = (s32[4]{0:T(128)S(1)}, s32[4]{0:T(128)}, u32[]{:S(2)}) copy-start(s32[4]{0:T(128)} %live.5) | copy-start | bytes 52
  24.4 1.2 %collective-permute-start.4 = (f32[2,16,128]{2,1,0:T(8,128)S(1)}, f32[2,16,128]{2,1,0:T(8,128)S(1)}, u32[]{:S(2)}, u32[]{:S(2)}) collective-permute-start(f32[2,16,128]{2,1,0:T(8,128)S(1)} %get-tuple-element.38), channel_id=1, source_target_pairs={{0,1},{1,0},{2,3},{3,2},{4,5},{5,4},{6,7},{7,6},{8,9},{9,8},{10,11... | collective-permute-start | bytes 49160 | tf_op jit(solution)/shard_map/gfac_core/ppermute | solution.py:240
  24.5 11.2 %collective-permute-start.6 = (bf16[2,256,256]{2,1,0:T(8,128)(2,1)S(1)}, bf16[2,256,256]{2,1,0:T(8,128)(2,1)S(1)}, u32[]{:S(2)}, u32[]{:S(2)}) collective-permute-start(bf16[2,256,256]{2,1,0:T(8,128)(2,1)S(1)} %get-tuple-element.41), channel_id=1, source_target_pairs={{0,1},{1,0},{2,3},{3,2},{4,5},{5,4},{6,7},{7,6},{8,9},{9,8},{10,11... | collective-permute-start | bytes 786440 | tf_op jit(solution)/shard_map/parts_core0/ppermute | solution.py:240
  25.7 3.7 %collective-permute-start.5 = (f32[16,128]{1,0:T(8,128)S(1)}, f32[16,128]{1,0:T(8,128)S(1)}, u32[]{:S(2)}, u32[]{:S(2)}) collective-permute-start(f32[16,128]{1,0:T(8,128)S(1)} %slice_bitcast_fusion.2), channel_id=1, source_target_pairs={{0,2},{1,3},{2,0},{3,1},{4,6},{5,7},{6,4},{7,5},{8,10},{9,11},{10,... | collective-permute-start | bytes 24584 | tf_op jit(solution)/shard_map/gfac_dp1/ppermute | solution.py:240
  27.2 2.1 %copy-start = (bf16[1,128,4096]{2,1,0:T(8,128)(2,1)S(1)}, bf16[1,128,4096]{2,1,0:T(8,128)(2,1)}, u32[]{:S(2)}) copy-start(bf16[1,128,4096]{2,1,0:T(8,128)(2,1)} %param.8) | copy-start | bytes 3145732
  29.6 1.4 %collective-permute-start.7 = (f32[2,4,4,1024]{3,2,1,0:T(4,128)S(1)}, f32[2,4,4,1024]{3,2,1,0:T(4,128)S(1)}, u32[]{:S(2)}, u32[]{:S(2)}) collective-permute-start(f32[2,4,4,1024]{3,2,1,0:T(4,128)S(1)} %get-tuple-element.43), channel_id=1, source_target_pairs={{0,1},{1,0},{2,3},{3,2},{4,5},{5,4},{6,7},{7,6},{8,9},{9,8},{10,11... | collective-permute-start | bytes 393224 | tf_op jit(solution)/shard_map/left_core/ppermute | solution.py:240
  31.1 4.0 %collective-permute-start.12 = (bf16[4,4,1024]{2,1,0:T(4,128)(2,1)S(1)}, bf16[4,4,1024]{2,1,0:T(4,128)(2,1)S(1)}, u32[]{:S(2)}, u32[]{:S(2)}) collective-permute-start(bf16[4,4,1024]{2,1,0:T(4,128)(2,1)S(1)} %fusion.1), channel_id=1, source_target_pairs={{0,2},{1,3},{2,0},{3,1},{4,6},{5,7},{6,4},{7,5},{8,10},{9,11},{10,... | collective-permute-start | bytes 98312 | tf_op jit(solution)/shard_map/left_dp1/ppermute | solution.py:240
  32.7 10.1 %collective-permute-start.10 = (bf16[2,272,256]{2,1,0:T(8,128)(2,1)S(1)}, bf16[2,272,256]{2,1,0:T(8,128)(2,1)S(1)}, u32[]{:S(2)}, u32[]{:S(2)}) collective-permute-start(bf16[2,272,256]{2,1,0:T(8,128)(2,1)S(1)} %get-tuple-element.53), channel_id=1, source_target_pairs={{0,2},{1,15},{2,4},{3,9},{4,6},{5,11},{6,0},{7,13},{8,10},{9,7},{1... | collective-permute-start | bytes 835592 | tf_op jit(solution)/shard_map/grads01/ppermute | solution.py:240
  33.2 9.6 %collective-permute-start.9 = (bf16[2,272,256]{2,1,0:T(8,128)(2,1)S(1)}, bf16[2,272,256]{2,1,0:T(8,128)(2,1)S(1)}, u32[]{:S(2)}, u32[]{:S(2)}) collective-permute-start(bf16[2,272,256]{2,1,0:T(8,128)(2,1)S(1)} %get-tuple-element.52), channel_id=1, source_target_pairs={{0,0},{1,13},{2,6},{3,11},{4,4},{5,9},{6,2},{7,15},{8,8},{9,5},{10... | collective-permute-start | bytes 835592 | tf_op jit(solution)/shard_map/grads00/ppermute | solution.py:240
  35.1 5.5 %collective-permute-start.13 = (bf16[2,4,1024]{2,1,0:T(4,128)(2,1)S(1)}, bf16[2,4,1024]{2,1,0:T(4,128)(2,1)S(1)}, u32[]{:S(2)}, u32[]{:S(2)}) collective-permute-start(bf16[2,4,1024]{2,1,0:T(4,128)(2,1)S(1)} %slice.62), channel_id=1, source_target_pairs={{0,8},{1,9},{2,10},{3,11},{4,12},{5,13},{6,14},{7,15},{8,0},{9,1},... | collective-permute-start | bytes 49160 | tf_op jit(solution)/shard_map/left_tensor2/ppermute | solution.py:240
  35.7 12.9 %collective-permute-start.8 = (bf16[2,256,256]{2,1,0:T(8,128)(2,1)S(1)}, bf16[2,256,256]{2,1,0:T(8,128)(2,1)S(1)}, u32[]{:S(2)}, u32[]{:S(2)}) collective-permute-start(bf16[2,256,256]{2,1,0:T(8,128)(2,1)S(1)} %pad_maximum_fusion.2), channel_id=1, source_target_pairs={{0,2},{1,3},{2,0},{3,1},{4,6},{5,7},{6,4},{7,5},{8,10},{9,11},{10,... | collective-permute-start | bytes 786440 | tf_op jit(solution)/shard_map/parts_dp01/ppermute | solution.py:240
  40.6 8.0 %copy-start.1 = (bf16[4096,16]{0,1:T(8,128)(2,1)S(1)}, bf16[4096,16]{0,1:T(8,128)(2,1)}, u32[]{:S(2)}) copy-start(bf16[4096,16]{0,1:T(8,128)(2,1)} %param.14) | copy-start | bytes 393220
  40.6 10.8 %collective-permute-start.14 = (bf16[1,4,1024]{2,1,0:T(4,128)(2,1)S(1)}, bf16[1,4,1024]{2,1,0:T(4,128)(2,1)S(1)}, u32[]{:S(2)}, u32[]{:S(2)}) collective-permute-start(bf16[1,4,1024]{2,1,0:T(4,128)(2,1)S(1)} %slice.63), channel_id=1, source_target_pairs={{0,4},{1,5},{2,6},{3,7},{4,0},{5,1},{6,2},{7,3},{8,12},{9,13},{10,... | collective-permute-start | bytes 24584 | tf_op jit(solution)/shard_map/left_tensor1/ppermute | solution.py:240
  50.9 1.6 %collective-permute-start.11 = (bf16[272,256]{1,0:T(8,128)(2,1)S(1)}, bf16[272,256]{1,0:T(8,128)(2,1)S(1)}, u32[]{:S(2)}, u32[]{:S(2)}) collective-permute-start(bf16[272,256]{1,0:T(8,128)(2,1)S(1)} %fusion), channel_id=1, source_target_pairs={{0,1},{1,0},{2,3},{3,2},{4,5},{5,4},{6,7},{7,6},{8,9},{9,8},{10,11... | collective-permute-start | bytes 417800 | tf_op jit(solution)/shard_map/grads_core/ppermute | solution.py:240

commit v5 on v4

--- a/solution.py
+++ b/solution.py
@@ -66,13 +66,18 @@
             panel = me ^ (cls + t * nclass)
             for s in range(slots):
                 row = table[s, 0, panel]
-                for a, src in enumerate((x, dy)):
-                    lo = ((t * 2 + a) * slots + s) * toks
-                    copy = pltpu.make_async_copy(block(src, row, blk), out.at[pl.ds(lo, toks)], sems.at[len(copies)])
-                    copy.start()
-                    copies.append(copy)
+                lo = ((t * 2 + 1) * slots + s) * toks
+                copy = pltpu.make_async_copy(block(dy, row, blk), out.at[pl.ds(lo, toks)], sems.at[len(copies)])
+                copy.start()
+                copies.append(copy)
     for copy in copies[:first]:
         copy.wait()
+    for (i, j), out in zip(plane(ndp, nseq), outs):
+        for t in range(turns):
+            panel = me ^ (class_of(d ^ i, c ^ j, ndp) + t * nclass)
+            for s in range(slots):
+                lo = t * 2 * slots * toks + s * toks
+                out[lo : lo + toks] = block(xbuf, table[s, 0, panel], blk)[...]
     factor = dot(lbuf[...], xbuf[...], 1, 1).astype(BF)
     for out in outs:
         tail = pl.ds(out.shape[0] - rank, rank)
@@ -110,12 +115,15 @@
     gsum = None
     for s in range(slots):
         pre = dot(fact[...], right[s], 0, 0)
-        dh = jnp.zeros(pre.shape, F32)
+        dh = 0.0
         single = alive[s]
         for t in range(slots):
             same = jnp.logical_and(cols[t] == cols[s], alive[t])
-            pre = pre + jnp.where(same, block_up[t], 0.0)
-            dh = dh + jnp.where(same, block_down[t], 0.0)
+            if t == s:
+                pre, dh = pre + block_up[t], dh + block_down[t]
+            else:
+                pre = pre + jnp.where(same, block_up[t], 0.0)
+                dh = dh + jnp.where(same, block_down[t], 0.0)
             if t < s:
                 single = jnp.logical_and(single, jnp.logical_not(same))
         act = pre.astype(BF).astype(F32)

time: 53.4 us -> 53.2 us (level)
  no operation moved by 1% of the time
where the time goes in v5:
time: 53.2 us; the launch traced here: 53 us
  waiting for transfers between devices  23 us (43%)
  starting transfers between devices  20.4 us (38%)
  Pallas kernels  8.33 us (16%)
  between operations  0.83 us (2%)
    ppermute x15, waiting for transfers between devices, permute(): lax.ppermute(value, PLANE, [(flat(*spot), flat(*target(*spot))) for spot...  23 us
    ppermute x15, starting transfers between devices, permute(): lax.ppermute(value, PLANE, [(flat(*spot), flat(*target(*spot))) for spot...  20.4 us
    pallas_call x6, Pallas kernels, call(): pl.pallas_call(kernel, out_shape=[jax.ShapeDtypeStruct(s, d) for s, d in...  8.33 us
  transfers between devices with their start and end apart: 15, of which 10 were waited for; matrix products, arithmetic and copies ran while one was open for 1% of the time, Pallas kernels for 7%

profile of v5, /device:TPU:0, one launch (start us, length us, event | category | flops | bytes accessed | tf_op | source)
XLA Modules:
  0.0 53.0 jit_solution(14310979978029271939)
XLA Ops:
  0.6 2.1 %collect.1 = (bf16[1088,256]{1,0:T(8,128)(2,1)S(1)}, bf16[528,256]{1,0:T(8,128)(2,1)S(1)}, bf16[528,256]{1,0:T(8,128)(2,1)S(1)}, bf16[528,256]{1,0:T(8,128)(2,1)S(1)}, bf16[528,256]{1,0:T(8,128)(2,1)S(1)}) custom-call(s32[2,2,4]{2,1,0:T(2,128)} %bitcast.36, bf16[128,4096]{1,0:T(8,128)(2,1)} %bitcast.32, bf16[128,4096]{1,0:T(8,128)(2,1)} %bitcast.42, ...), custom_call_target="tpu_custom_call" | custom-call | flops 100000000 | bytes 1024 | tf_op jit(solution)/shard_map/collect/pallas_call | solution.py:229
  2.7 0.7 %collective-permute-start = (bf16[1088,256]{1,0:T(8,128)(2,1)S(1)}, bf16[1088,256]{1,0:T(8,128)(2,1)S(1)}, u32[]{:S(2)}, u32[]{:S(2)}) collective-permute-start(bf16[1088,256]{1,0:T(8,128)(2,1)S(1)} %get-tuple-element.32), channel_id=1, source_target_pairs={{0,0},{1,13},{2,6},{3,11},{4,4},{5,9},{6,2},{7,15},{8,8},{9,5},{10... | collective-permute-start | bytes 1671176 | tf_op jit(solution)/shard_map/weights0/ppermute | solution.py:248
  3.4 6.0 %collective-permute-start.1 = (bf16[528,256]{1,0:T(8,128)(2,1)S(1)}, bf16[528,256]{1,0:T(8,128)(2,1)S(1)}, u32[]{:S(2)}, u32[]{:S(2)}) collective-permute-start(bf16[528,256]{1,0:T(8,128)(2,1)S(1)} %get-tuple-element.33), channel_id=1, source_target_pairs={{0,3},{1,2},{2,1},{3,0},{4,7},{5,6},{6,5},{7,4},{8,11},{9,10},{10,... | collective-permute-start | bytes 811016 | tf_op jit(solution)/shard_map/tokens11/ppermute | solution.py:248
  9.4 1.5 %collective-permute-start.2 = (bf16[528,256]{1,0:T(8,128)(2,1)S(1)}, bf16[528,256]{1,0:T(8,128)(2,1)S(1)}, u32[]{:S(2)}, u32[]{:S(2)}) collective-permute-start(bf16[528,256]{1,0:T(8,128)(2,1)S(1)} %get-tuple-element.34), channel_id=1, source_target_pairs={{0,2},{1,3},{2,0},{3,1},{4,6},{5,7},{6,4},{7,5},{8,10},{9,11},{10,... | collective-permute-start | bytes 811016 | tf_op jit(solution)/shard_map/tokens10/ppermute | solution.py:248
  10.9 5.3 %collective-permute-done.1.refs_0_ = bf16[528,256]{1,0:T(8,128)(2,1)S(1)} collective-permute-done((bf16[528,256]{1,0:T(8,128)(2,1)S(1)}, bf16[528,256]{1,0:T(8,128)(2,1)S(1)}, u32[]{:S(2)}, u32[]{:S(2)}) %collective-permute-start.1) | collective-permute-done | bytes 270368 | tf_op jit(solution)/shard_map/tokens11/ppermute | solution.py:248
  16.2 6.0 %collective-permute-done.2.refs_1_ = bf16[528,256]{1,0:T(8,128)(2,1)S(1)} collective-permute-done((bf16[528,256]{1,0:T(8,128)(2,1)S(1)}, bf16[528,256]{1,0:T(8,128)(2,1)S(1)}, u32[]{:S(2)}, u32[]{:S(2)}) %collective-permute-start.2) | collective-permute-done | bytes 270368 | tf_op jit(solution)/shard_map/tokens10/ppermute | solution.py:248
  22.3 2.0 %panel0.1 = (bf16[2,512,256]{2,1,0:T(8,128)(2,1)S(1)}, bf16[2,512,256]{2,1,0:T(8,128)(2,1)S(1)}, bf16[16,512]{1,0:T(8,128)(2,1)S(1)}, bf16[2,512,256]{2,1,0:T(8,...) custom-call(s32[2,2,4]{2,1,0:T(2,128)S(1)} %bitcast.37, ...), custom_call_target="tpu_custom_call" | custom-call | flops 100000000 | bytes 1024 | tf_op jit(solution)/shard_map/panel0/pallas_call | solution.py:229
  24.8 0.7 %collective-permute-done.4 = f32[2,16,128]{2,1,0:T(8,128)S(1)} collective-permute-done((f32[2,16,128]{2,1,0:T(8,128)S(1)}, f32[2,16,128]{2,1,0:T(8,128)S(1)}, u32[]{:S(2)}, u32[]{:S(2)}) %collective-permute-start.4) | collective-permute-done | bytes 16416 | tf_op jit(solution)/shard_map/gfac_core/ppermute | solution.py:248
  25.5 1.6 %collective-permute-start.5 = (f32[16,128]{1,0:T(8,128)S(1)}, f32[16,128]{1,0:T(8,128)S(1)}, u32[]{:S(2)}, u32[]{:S(2)}) collective-permute-start(f32[16,128]{1,0:T(8,128)S(1)} %slice_bitcast_fusion.2), channel_id=1, source_target_pairs={{0,2},{1,3},{2,0},{3,1},{4,6},{5,7},{6,4},{7,5},{8,10},{9,11},{10,... | collective-permute-start | bytes 24584 | tf_op jit(solution)/shard_map/gfac_dp1/ppermute | solution.py:248
  27.0 1.1 %grads0.1 = (bf16[2,2,2,2,64,256]{5,4,3,2,1,0:T(8,128)(2,1)S(1)}, f32[16,1024]{1,0:T(8,128)S(1)}) custom-call(s32[2,2,4]{2,1,0:T(2,128)S(1)} %bitcast.38, s32[4]{0:T(128)S(1)} %copy-done.3, bf16[2,512,256]{2,1,0:T(8,128)(2,1)S(1)} %get-tuple-element.45.xcol, bf16[2,512,256]{2,1,0:T(8,128)(2,1)S(1)} %get-tuple-element.46.dycol, ...), custom_call_target="tpu_custom_call" | custom-call | flops 100000000 | bytes 1024 | tf_op jit(solution)/shard_map/grads0/pallas_call | solution.py:229
  28.2 1.0 %collective-permute-done.5 = f32[16,128]{1,0:T(8,128)S(1)} collective-permute-done((f32[16,128]{1,0:T(8,128)S(1)}, f32[16,128]{1,0:T(8,128)S(1)}, u32[]{:S(2)}, u32[]{:S(2)}) %collective-permute-start.5) | collective-permute-done | bytes 8224 | tf_op jit(solution)/shard_map/gfac_dp1/ppermute | solution.py:248
  29.6 1.2 %collective-permute-done.7 = f32[2,4,4,1024]{3,2,1,0:T(4,128)S(1)} collective-permute-done((f32[2,4,4,1024]{3,2,1,0:T(4,128)S(1)}, f32[2,4,4,1024]{3,2,1,0:T(4,128)S(1)}, u32[]{:S(2)}, u32[]{:S(2)}) %collective-permute-start.7) | collective-permute-done | bytes 131104 | tf_op jit(solution)/shard_map/left_core/ppermute | solution.py:248
  30.9 1.6 %collective-permute-start.12 = (bf16[4,4,1024]{2,1,0:T(4,128)(2,1)S(1)}, bf16[4,4,1024]{2,1,0:T(4,128)(2,1)S(1)}, u32[]{:S(2)}, u32[]{:S(2)}) collective-permute-start(bf16[4,4,1024]{2,1,0:T(4,128)(2,1)S(1)} %fusion.1), channel_id=1, source_target_pairs={{0,2},{1,3},{2,0},{3,1},{4,6},{5,7},{6,4},{7,5},{8,10},{9,11},{10,... | collective-permute-start | bytes 98312 | tf_op jit(solution)/shard_map/left_dp1/ppermute | solution.py:248
  33.0 0.7 %collective-permute-start.9 = (bf16[2,272,256]{2,1,0:T(8,128)(2,1)S(1)}, bf16[2,272,256]{2,1,0:T(8,128)(2,1)S(1)}, u32[]{:S(2)}, u32[]{:S(2)}) collective-permute-start(bf16[2,272,256]{2,1,0:T(8,128)(2,1)S(1)} %get-tuple-element.52), channel_id=1, source_target_pairs={{0,0},{1,13},{2,6},{3,11},{4,4},{5,9},{6,2},{7,15},{8,8},{9,5},{10... | collective-permute-start | bytes 835592 | tf_op jit(solution)/shard_map/grads00/ppermute | solution.py:248
  33.7 1.1 %collective-permute-done.12 = bf16[4,4,1024]{2,1,0:T(4,128)(2,1)S(1)} collective-permute-done((bf16[4,4,1024]{2,1,0:T(4,128)(2,1)S(1)}, bf16[4,4,1024]{2,1,0:T(4,128)(2,1)S(1)}, u32[]{:S(2)}, u32[]{:S(2)}) %collective-permute-start.12) | collective-permute-done | bytes 32800 | tf_op jit(solution)/shard_map/left_dp1/ppermute | solution.py:248
  34.9 0.6 %collective-permute-start.13 = (bf16[2,4,1024]{2,1,0:T(4,128)(2,1)S(1)}, bf16[2,4,1024]{2,1,0:T(4,128)(2,1)S(1)}, u32[]{:S(2)}, u32[]{:S(2)}) collective-permute-start(bf16[2,4,1024]{2,1,0:T(4,128)(2,1)S(1)} %slice.62), channel_id=1, source_target_pairs={{0,8},{1,9},{2,10},{3,11},{4,12},{5,13},{6,14},{7,15},{8,0},{9,1},... | collective-permute-start | bytes 49160 | tf_op jit(solution)/shard_map/left_tensor2/ppermute | solution.py:248
  35.5 4.8 %collective-permute-start.8 = (bf16[2,256,256]{2,1,0:T(8,128)(2,1)S(1)}, bf16[2,256,256]{2,1,0:T(8,128)(2,1)S(1)}, u32[]{:S(2)}, u32[]{:S(2)}) collective-permute-start(bf16[2,256,256]{2,1,0:T(8,128)(2,1)S(1)} %pad_maximum_fusion.2), channel_id=1, source_target_pairs={{0,2},{1,3},{2,0},{3,1},{4,6},{5,7},{6,4},{7,5},{8,10},{9,11},{10,... | collective-permute-start | bytes 786440 | tf_op jit(solution)/shard_map/parts_dp01/ppermute | solution.py:248
  40.5 1.2 %collective-permute-start.14 = (bf16[1,4,1024]{2,1,0:T(4,128)(2,1)S(1)}, bf16[1,4,1024]{2,1,0:T(4,128)(2,1)S(1)}, u32[]{:S(2)}, u32[]{:S(2)}) collective-permute-start(bf16[1,4,1024]{2,1,0:T(4,128)(2,1)S(1)} %slice.63), channel_id=1, source_target_pairs={{0,4},{1,5},{2,6},{3,7},{4,0},{5,1},{6,2},{7,3},{8,12},{9,13},{10,... | collective-permute-start | bytes 24584 | tf_op jit(solution)/shard_map/left_tensor1/ppermute | solution.py:248
  41.6 1.0 %collective-permute-done.10 = bf16[2,272,256]{2,1,0:T(8,128)(2,1)S(1)} collective-permute-done((bf16[2,272,256]{2,1,0:T(8,128)(2,1)S(1)}, bf16[2,272,256]{2,1,0:T(8,128)(2,1)S(1)}, u32[]{:S(2)}, u32[]{:S(2)}) %collective-permute-start.10) | collective-permute-done | bytes 278560 | tf_op jit(solution)/shard_map/grads01/ppermute | solution.py:248
  42.7 5.7 %collective-permute-done.8.refs_2_ = bf16[2,256,256]{2,1,0:T(8,128)(2,1)S(1)} collective-permute-done((bf16[2,256,256]{2,1,0:T(8,128)(2,1)S(1)}, bf16[2,256,256]{2,1,0:T(8,128)(2,1)S(1)}, u32[]{:S(2)}, u32[]{:S(2)}) %collective-permute-start.8) | collective-permute-done | bytes 262176 | tf_op jit(solution)/shard_map/parts_dp01/ppermute | solution.py:248
  48.5 2.2 %dx.1 = bf16[128,4096]{1,0:T(8,128)(2,1)} custom-call(s32[2,2,4]{2,1,0:T(2,128)S(1)} %bitcast.39, s32[4]{0:T(128)S(1)} %copy-done.3, bf16[16,4096]{1,0:T(8,128)(2,1)S(1)} %bitcast.35, bf16[16,128]{1,0:T(8,128)(2,1)S(1)} %get-tuple-element.39.gfac, bf16[256,256]{1,0:T(8,128)(2,1)S(1)} %get-tuple-element.62.refs_0_, ...), custom_call_target="tpu_custom_call" | custom-call | flops 100000000 | bytes 1024 | tf_op jit(solution)/shard_map/dx/pallas_call | solution.py:229
  50.7 0.6 %collective-permute-start.11 = (bf16[272,256]{1,0:T(8,128)(2,1)S(1)}, bf16[272,256]{1,0:T(8,128)(2,1)S(1)}, u32[]{:S(2)}, u32[]{:S(2)}) collective-permute-start(bf16[272,256]{1,0:T(8,128)(2,1)S(1)} %fusion), channel_id=1, source_target_pairs={{0,1},{1,0},{2,3},{3,2},{4,5},{5,4},{6,7},{7,6},{8,9},{9,8},{10,11... | collective-permute-start | bytes 417800 | tf_op jit(solution)/shard_map/grads_core/ppermute | solution.py:248
  51.3 0.9 %collective-permute-done.11.other = bf16[272,256]{1,0:T(8,128)(2,1)S(1)} collective-permute-done((bf16[272,256]{1,0:T(8,128)(2,1)S(1)}, bf16[272,256]{1,0:T(8,128)(2,1)S(1)}, u32[]{:S(2)}, u32[]{:S(2)}) %collective-permute-start.11) | collective-permute-done | bytes 139296 | tf_op jit(solution)/shard_map/grads_core/ppermute | solution.py:248
  52.3 0.7 %finish.1 = (f32[2,64,256]{2,1,0:T(8,128)}, f32[2,64,256]{2,1,0:T(8,128)}, f32[4,1024]{1,0:T(4,128)}, f32[4,1024]{1,0:T(4,128)}) custom-call(f32[272,256]{1,0:T(8,128)S(1)} %dynamic-slice_bitcast_fusion.mine, bf16[272,256]{1,0:T(8,128)(2,1)S(1)} %collective-permute-done.11.other, f32[4,1024]{1,0:T(4,128)S(1)} %fusion.2.left), custom_call_target="tpu_custom_call" | custom-call | flops 1000000 | bytes 1024 | tf_op jit(solution)/shard_map/finish/pallas_call | solution.py:229
  (42 shorter events, 2.0 us)
Async XLA Ops:
  2.7 19.5 %collective-permute-start = (bf16[1088,256]{1,0:T(8,128)(2,1)S(1)}, bf16[1088,256]{1,0:T(8,128)(2,1)S(1)}, u32[]{:S(2)}, u32[]{:S(2)}) collective-permute-start(bf16[1088,256]{1,0:T(8,128)(2,1)S(1)} %get-tuple-element.32), channel_id=1, source_target_pairs={{0,0},{1,13},{2,6},{3,11},{4,4},{5,9},{6,2},{7,15},{8,8},{9,5},{10... | collective-permute-start | bytes 1671176 | tf_op jit(solution)/shard_map/weights0/ppermute | solution.py:248
  3.4 12.8 %collective-permute-start.1 = (bf16[528,256]{1,0:T(8,128)(2,1)S(1)}, bf16[528,256]{1,0:T(8,128)(2,1)S(1)}, u32[]{:S(2)}, u32[]{:S(2)}) collective-permute-start(bf16[528,256]{1,0:T(8,128)(2,1)S(1)} %get-tuple-element.33), channel_id=1, source_target_pairs={{0,3},{1,2},{2,1},{3,0},{4,7},{5,6},{6,5},{7,4},{8,11},{9,10},{10,... | collective-permute-start | bytes 811016 | tf_op jit(solution)/shard_map/tokens11/ppermute | solution.py:248
  9.4 12.8 %collective-permute-start.2 = (bf16[528,256]{1,0:T(8,128)(2,1)S(1)}, bf16[528,256]{1,0:T(8,128)(2,1)S(1)}, u32[]{:S(2)}, u32[]{:S(2)}) collective-permute-start(bf16[528,256]{1,0:T(8,128)(2,1)S(1)} %get-tuple-element.34), channel_id=1, source_target_pairs={{0,2},{1,3},{2,0},{3,1},{4,6},{5,7},{6,4},{7,5},{8,10},{9,11},{10,... | collective-permute-start | bytes 811016 | tf_op jit(solution)/shard_map/tokens10/ppermute | solution.py:248
  10.9 11.3 %collective-permute-start.3 = (bf16[528,256]{1,0:T(8,128)(2,1)S(1)}, bf16[528,256]{1,0:T(8,128)(2,1)S(1)}, u32[]{:S(2)}, u32[]{:S(2)}) collective-permute-start(bf16[528,256]{1,0:T(8,128)(2,1)S(1)} %get-tuple-element.35), channel_id=1, source_target_pairs={{0,1},{1,0},{2,3},{3,2},{4,5},{5,4},{6,7},{7,6},{8,9},{9,8},{10,11... | collective-permute-start | bytes 811016 | tf_op jit(solution)/shard_map/tokens01/ppermute | solution.py:248
  10.9 11.3 %copy-start.2 = (s32[4,2,2]{0,2,1:T(2,128)S(1)}, s32[4,2,2]{0,2,1:T(2,128)}, u32[]{:S(2)}) copy-start(s32[4,2,2]{0,2,1:T(2,128)} %param.12) | copy-start | bytes 196
  10.9 11.3 %copy-start.3 = (s32[4]{0:T(128)S(1)}, s32[4]{0:T(128)}, u32[]{:S(2)}) copy-start(s32[4]{0:T(128)} %live.5) | copy-start | bytes 52
  24.2 1.2 %collective-permute-start.4 = (f32[2,16,128]{2,1,0:T(8,128)S(1)}, f32[2,16,128]{2,1,0:T(8,128)S(1)}, u32[]{:S(2)}, u32[]{:S(2)}) collective-permute-start(f32[2,16,128]{2,1,0:T(8,128)S(1)} %get-tuple-element.38), channel_id=1, source_target_pairs={{0,1},{1,0},{2,3},{3,2},{4,5},{5,4},{6,7},{7,6},{8,9},{9,8},{10,11... | collective-permute-start | bytes 49160 | tf_op jit(solution)/shard_map/gfac_core/ppermute | solution.py:248
  24.3 11.2 %collective-permute-start.6 = (bf16[2,256,256]{2,1,0:T(8,128)(2,1)S(1)}, bf16[2,256,256]{2,1,0:T(8,128)(2,1)S(1)}, u32[]{:S(2)}, u32[]{:S(2)}) collective-permute-start(bf16[2,256,256]{2,1,0:T(8,128)(2,1)S(1)} %get-tuple-element.41), channel_id=1, source_target_pairs={{0,1},{1,0},{2,3},{3,2},{4,5},{5,4},{6,7},{7,6},{8,9},{9,8},{10,11... | collective-permute-start | bytes 786440 | tf_op jit(solution)/shard_map/parts_core0/ppermute | solution.py:248
  25.5 3.7 %collective-permute-start.5 = (f32[16,128]{1,0:T(8,128)S(1)}, f32[16,128]{1,0:T(8,128)S(1)}, u32[]{:S(2)}, u32[]{:S(2)}) collective-permute-start(f32[16,128]{1,0:T(8,128)S(1)} %slice_bitcast_fusion.2), channel_id=1, source_target_pairs={{0,2},{1,3},{2,0},{3,1},{4,6},{5,7},{6,4},{7,5},{8,10},{9,11},{10,... | collective-permute-start | bytes 24584 | tf_op jit(solution)/shard_map/gfac_dp1/ppermute | solution.py:248
  27.0 2.1 %copy-start = (bf16[1,128,4096]{2,1,0:T(8,128)(2,1)S(1)}, bf16[1,128,4096]{2,1,0:T(8,128)(2,1)}, u32[]{:S(2)}) copy-start(bf16[1,128,4096]{2,1,0:T(8,128)(2,1)} %param.8) | copy-start | bytes 3145732
  29.4 1.4 %collective-permute-start.7 = (f32[2,4,4,1024]{3,2,1,0:T(4,128)S(1)}, f32[2,4,4,1024]{3,2,1,0:T(4,128)S(1)}, u32[]{:S(2)}, u32[]{:S(2)}) collective-permute-start(f32[2,4,4,1024]{3,2,1,0:T(4,128)S(1)} %get-tuple-element.43), channel_id=1, source_target_pairs={{0,1},{1,0},{2,3},{3,2},{4,5},{5,4},{6,7},{7,6},{8,9},{9,8},{10,11... | collective-permute-start | bytes 393224 | tf_op jit(solution)/shard_map/left_core/ppermute | solution.py:248
  30.9 4.0 %collective-permute-start.12 = (bf16[4,4,1024]{2,1,0:T(4,128)(2,1)S(1)}, bf16[4,4,1024]{2,1,0:T(4,128)(2,1)S(1)}, u32[]{:S(2)}, u32[]{:S(2)}) collective-permute-start(bf16[4,4,1024]{2,1,0:T(4,128)(2,1)S(1)} %fusion.1), channel_id=1, source_target_pairs={{0,2},{1,3},{2,0},{3,1},{4,6},{5,7},{6,4},{7,5},{8,10},{9,11},{10,... | collective-permute-start | bytes 98312 | tf_op jit(solution)/shard_map/left_dp1/ppermute | solution.py:248
  32.5 10.1 %collective-permute-start.10 = (bf16[2,272,256]{2,1,0:T(8,128)(2,1)S(1)}, bf16[2,272,256]{2,1,0:T(8,128)(2,1)S(1)}, u32[]{:S(2)}, u32[]{:S(2)}) collective-permute-start(bf16[2,272,256]{2,1,0:T(8,128)(2,1)S(1)} %get-tuple-element.53), channel_id=1, source_target_pairs={{0,2},{1,15},{2,4},{3,9},{4,6},{5,11},{6,0},{7,13},{8,10},{9,7},{1... | collective-permute-start | bytes 835592 | tf_op jit(solution)/shard_map/grads01/ppermute | solution.py:248
  33.0 9.6 %collective-permute-start.9 = (bf16[2,272,256]{2,1,0:T(8,128)(2,1)S(1)}, bf16[2,272,256]{2,1,0:T(8,128)(2,1)S(1)}, u32[]{:S(2)}, u32[]{:S(2)}) collective-permute-start(bf16[2,272,256]{2,1,0:T(8,128)(2,1)S(1)} %get-tuple-element.52), channel_id=1, source_target_pairs={{0,0},{1,13},{2,6},{3,11},{4,4},{5,9},{6,2},{7,15},{8,8},{9,5},{10... | collective-permute-start | bytes 835592 | tf_op jit(solution)/shard_map/grads00/ppermute | solution.py:248
  34.9 5.5 %collective-permute-start.13 = (bf16[2,4,1024]{2,1,0:T(4,128)(2,1)S(1)}, bf16[2,4,1024]{2,1,0:T(4,128)(2,1)S(1)}, u32[]{:S(2)}, u32[]{:S(2)}) collective-permute-start(bf16[2,4,1024]{2,1,0:T(4,128)(2,1)S(1)} %slice.62), channel_id=1, source_target_pairs={{0,8},{1,9},{2,10},{3,11},{4,12},{5,13},{6,14},{7,15},{8,0},{9,1},... | collective-permute-start | bytes 49160 | tf_op jit(solution)/shard_map/left_tensor2/ppermute | solution.py:248
  35.5 12.9 %collective-permute-start.8 = (bf16[2,256,256]{2,1,0:T(8,128)(2,1)S(1)}, bf16[2,256,256]{2,1,0:T(8,128)(2,1)S(1)}, u32[]{:S(2)}, u32[]{:S(2)}) collective-permute-start(bf16[2,256,256]{2,1,0:T(8,128)(2,1)S(1)} %pad_maximum_fusion.2), channel_id=1, source_target_pairs={{0,2},{1,3},{2,0},{3,1},{4,6},{5,7},{6,4},{7,5},{8,10},{9,11},{10,... | collective-permute-start | bytes 786440 | tf_op jit(solution)/shard_map/parts_dp01/ppermute | solution.py:248
  40.4 8.0 %copy-start.1 = (bf16[4096,16]{0,1:T(8,128)(2,1)S(1)}, bf16[4096,16]{0,1:T(8,128)(2,1)}, u32[]{:S(2)}) copy-start(bf16[4096,16]{0,1:T(8,128)(2,1)} %param.14) | copy-start | bytes 393220
  40.5 10.8 %collective-permute-start.14 = (bf16[1,4,1024]{2,1,0:T(4,128)(2,1)S(1)}, bf16[1,4,1024]{2,1,0:T(4,128)(2,1)S(1)}, u32[]{:S(2)}, u32[]{:S(2)}) collective-permute-start(bf16[1,4,1024]{2,1,0:T(4,128)(2,1)S(1)} %slice.63), channel_id=1, source_target_pairs={{0,4},{1,5},{2,6},{3,7},{4,0},{5,1},{6,2},{7,3},{8,12},{9,13},{10,... | collective-permute-start | bytes 24584 | tf_op jit(solution)/shard_map/left_tensor1/ppermute | solution.py:248
  50.7 1.6 %collective-permute-start.11 = (bf16[272,256]{1,0:T(8,128)(2,1)S(1)}, bf16[272,256]{1,0:T(8,128)(2,1)S(1)}, u32[]{:S(2)}, u32[]{:S(2)}) collective-permute-start(bf16[272,256]{1,0:T(8,128)(2,1)S(1)} %fusion), channel_id=1, source_target_pairs={{0,1},{1,0},{2,3},{3,2},{4,5},{5,4},{6,7},{7,6},{8,9},{9,8},{10,11... | collective-permute-start | bytes 417800 | tf_op jit(solution)/shard_map/grads_core/ppermute | solution.py:248
